TPU v7x, 32 devices: a whole 2x2x4 slice. The times are simulated.
32 devices in a mesh: seq: 4 (over x, core), dp: 8 (over z, y).
Axes of the slice: x: 2, y: 2, z: 4, core: 2. Of those that a mesh axis runs over, the one named last changes fastest.
Arguments:
- characters: bfloat16 [16, 2048, 768], P('dp', 'seq'), may hold values from -6 to 6
- cotangent: bfloat16 [16, 2048, 768], P('dp', 'seq'), may hold values from -6 to 6
- lengths: int32 [16], P('dp'), may hold values from 200 to 2048, as said below
- vectors: float32 [12, 768], replicated, may hold values from -0.6 to 1.4
- vector_acc: float32 [12, 768], replicated, may hold values from 1 to 4
- attend_weight: float32 [768, 4, 768], P(None, None, ('seq', 'dp')), may hold values from -1.7320508 to 1.7320508
- attend_moment: float32 [768, 4, 768], P(None, None, ('seq', 'dp')), may hold values from -4 to 4
- attend_left: float32 [768, 4, 768], P(('seq', 'dp')), may hold values from 0 to 4, as said below
- attend_right: float32 [768, 4, 768], P(None, None, ('seq', 'dp')), may hold values from 0 to 4, as said below
- attend_rootleft: float32 [768, 4, 768], P(('seq', 'dp')), may hold values from -0.1 to 1.7
- attend_rootright: float32 [768, 4, 768], P(None, None, ('seq', 'dp')), may hold values from -0.1 to 1.7
- expand_weight: float32 [768, 3072], P(None, ('seq', 'dp')), may hold values from -0.21875 to 0.21875
- expand_moment: float32 [768, 3072], P(None, ('seq', 'dp')), may hold values from -4 to 4
- expand_left: float32 [768, 768], P(('seq', 'dp')), may hold values from 0 to 4, as said below
- expand_right: float32 [3072, 3072], P(None, ('seq', 'dp')), may hold values from 0 to 4, as said below
- expand_rootleft: float32 [768, 768], P(('seq', 'dp')), may hold values from -0.1 to 1.7
- expand_rootright: float32 [3072, 3072], P(None, ('seq', 'dp')), may hold values from -0.1 to 1.7
- shrink_weight: float32 [3072, 768], P(None, ('seq', 'dp')), may hold values from -0.109375 to 0.109375
- shrink_moment: float32 [3072, 768], P(None, ('seq', 'dp')), may hold values from -4 to 4
- shrink_left: float32 [3072, 3072], P(('seq', 'dp')), may hold values from 0 to 4, as said below
- shrink_right: float32 [768, 768], P(None, ('seq', 'dp')), may hold values from 0 to 4, as said below
- shrink_rootleft: float32 [3072, 3072], P(('seq', 'dp')), may hold values from -0.1 to 1.7
- shrink_rootright: float32 [768, 768], P(None, ('seq', 'dp')), may hold values from -0.1 to 1.7
Outputs:
- layer_output: bfloat16 [16, 2048, 768], P('dp', 'seq')
- characters_grad: bfloat16 [16, 2048, 768], P('dp', 'seq')
- attend_grad: float32 [768, 4, 768], P(('seq', 'dp'))
- attend_newmoment: float32 [768, 4, 768], P(None, None, ('seq', 'dp'))
- attend_newweight: float32 [768, 4, 768], P(None, None, ('seq', 'dp'))
- attend_newleft: float32 [768, 4, 768], P(('seq', 'dp'))
- attend_newright: float32 [768, 4, 768], P(None, None, ('seq', 'dp'))
- expand_grad: float32 [768, 3072], P(('seq', 'dp'))
- expand_newmoment: float32 [768, 3072], P(None, ('seq', 'dp'))
- expand_newweight: float32 [768, 3072], P(None, ('seq', 'dp'))
- expand_newleft: float32 [768, 768], P(('seq', 'dp'))
- expand_newright: float32 [3072, 3072], P(None, ('seq', 'dp'))
- shrink_grad: float32 [3072, 768], P(('seq', 'dp'))
- shrink_newmoment: float32 [3072, 768], P(None, ('seq', 'dp'))
- shrink_newweight: float32 [3072, 768], P(None, ('seq', 'dp'))
- shrink_newleft: float32 [3072, 3072], P(('seq', 'dp'))
- shrink_newright: float32 [768, 768], P(None, ('seq', 'dp'))
- vector_grad: float32 [12, 768], replicated
- vector_newacc: float32 [12, 768], replicated
- vector_new: float32 [12, 768], replicated
Inputs may be any that keep to these rules, and one draw needn't show every extreme that they name: `lengths`: among the texts of each index of dp (runs of 2), one text chosen by the seed has length 2048. `attend_left`: Symmetric. `attend_right`: Symmetric. `expand_left`: Symmetric. `expand_right`: Symmetric. `shrink_left`: Symmetric. `shrink_right`: Symmetric.
All inputs are finite; a program needn't handle non-finite values.
Results may differ from a plain program's by a relative error of at most 0.0099.
Values may be sent and summed in bfloat16 or wider, within the bound.
No kernel may reach another device: no remote copies, remote signals or barrier semaphores. Data moves between devices by JAX's collectives and lax.ppermute only.
A program may use at most 256 MiB of HBM per device.

v0:
```python
import math

import jax
import jax.numpy as jnp
from jax import lax
from jax.sharding import PartitionSpec as P

HEAD = 64
WIN = 128


EPSILON = 1e-05
STAT_EPSILON = 1e-06
MATRIX_RATE = 0.5
VECTOR_RATE = 0.3
MOMENTUM = 0.9
MASKED = -1e30
HIGHEST = lax.Precision.HIGHEST


def extended(cells, sides, width):
    for axis, dim in sides:
        count = lax.axis_size(axis)
        ends = count - 1
        head = lax.slice_in_dim(cells, 0, width, axis=dim)
        tail = lax.slice_in_dim(cells, cells.shape[dim] - width, cells.shape[dim], axis=dim)
        cells = jnp.concatenate(
            [
                lax.ppermute(tail, axis, [(i, (i + 1) % count) for i in range(ends)]),
                cells,
                lax.ppermute(head, axis, [((i + 1) % count, i) for i in range(ends)]),
            ],
            axis=dim,
        )
    return cells


def from_behind(x, axis, by):
    length = lax.axis_size(axis)
    pairs = [(i, i + by) for i in range(length) if 0 <= i + by < length]
    return lax.ppermute(x, axis, pairs)


def normalize(values, gain_row, bias_row):
    centre = values - jnp.mean(values, axis=-1, keepdims=True)
    spread = jnp.mean(centre * centre, axis=-1, keepdims=True)
    return centre * lax.rsqrt(spread + EPSILON) * gain_row + bias_row


def smooth_gate(values):
    return jax.nn.gelu(values, approximate=False)


def across(left_rows, right_rows):
    return lax.dot_general(
        left_rows, right_rows, (((0,), (0,)), ((), ())), preferred_element_type=jnp.float32
    )


def against(grad_rows, weight):
    return lax.dot_general(
        grad_rows, weight, (((1,), (1,)), ((), ())), preferred_element_type=jnp.float32
    )


def split_heads(tensor, group_index, group_width):
    sliced = tensor[..., group_index * group_width : (group_index + 1) * group_width]
    return sliced.reshape(sliced.shape[:-1] + (group_width // HEAD, HEAD))


def masked_scores(queries, keys_group, allowed):
    scores = (
        jnp.einsum("tqhe,tkhe->thqk", queries, keys_group, preferred_element_type=jnp.float32)
        * 0.125
    )
    return jnp.where(allowed, scores, MASKED)


def statistics(own_rows, whole, left_rows, right_cols, col_block):
    total_rows = whole.shape[0]
    total_cols = whole.shape[2]
    col_count = right_cols.shape[2]
    mean_square = jnp.mean(whole * whole, axis=(0, 2), keepdims=True) + STAT_EPSILON
    gram_rows = jnp.einsum("rwk,iwk->rwi", own_rows, whole, precision=HIGHEST)
    new_left = 0.5 * left_rows + 0.5 * gram_rows / (total_cols * mean_square)
    own_cols = lax.dynamic_slice_in_dim(whole, col_block * col_count, col_count, 2)
    gram_cols = jnp.einsum("iwk,iwj->kwj", whole, own_cols, precision=HIGHEST)
    new_right = 0.5 * right_cols + 0.5 * gram_cols / (total_rows * mean_square)
    return (mean_square, new_left, new_right)


def left_apply(rootleft_rows, whole):
    return jnp.einsum("rwi,iwj->rwj", rootleft_rows, whole, precision=HIGHEST)


def right_apply(whole, rootright_cols):
    return jnp.einsum("iwk,kwj->iwj", whole, rootright_cols, precision=HIGHEST)


def finish(direction, mean_square, moment, weight):
    new_moment = MOMENTUM * moment + direction * lax.rsqrt(mean_square)
    new_weight = weight - MATRIX_RATE / math.sqrt(weight.shape[0]) * new_moment
    return (new_moment, new_weight)


def shards(
    characters,
    cotangent,
    lengths,
    vectors,
    vector_acc,
    attend_weight,
    attend_moment,
    attend_left,
    attend_right,
    attend_rootleft,
    attend_rootright,
    expand_weight,
    expand_moment,
    expand_left,
    expand_right,
    expand_rootleft,
    expand_rootright,
    shrink_weight,
    shrink_moment,
    shrink_left,
    shrink_right,
    shrink_rootleft,
    shrink_rootright,
):
    text_count, block_size, model_width = characters.shape
    window = WIN
    token_rows = text_count * block_size
    tokens_all = token_rows * lax.axis_size("seq") * lax.axis_size("dp")
    grad_scale = 1.0 / math.sqrt(tokens_all)
    wide_index = lax.axis_index(("seq", "dp"))
    attend_full, expand_full, shrink_full = (
        lax.all_gather(attend_weight.astype(jnp.bfloat16), ("seq", "dp"), axis=2, tiled=True),
        lax.all_gather(expand_weight.astype(jnp.bfloat16), ("seq", "dp"), axis=1, tiled=True),
        lax.all_gather(shrink_weight.astype(jnp.bfloat16), ("seq", "dp"), axis=1, tiled=True),
    )
    qkv_weight = attend_full[:, :3, :].reshape(model_width, 3 * model_width)
    out_weight = attend_full[:, 3, :]
    layer_input = characters.astype(jnp.float32).reshape(token_rows, model_width)
    gain_one = vectors[0]
    bias_one = vectors[1]
    query_bias = vectors[2]
    value_bias = vectors[3]
    out_bias = vectors[4]
    gain_two = vectors[5]
    bias_two = vectors[6]
    shrink_bias = vectors[7]
    expand_bias = vectors[8:].reshape(-1)
    normed_low = normalize(layer_input, gain_one, bias_one).astype(jnp.bfloat16)
    projected = jnp.dot(normed_low, qkv_weight, preferred_element_type=jnp.float32)
    query_low = (
        (projected[:, :model_width] + query_bias)
        .astype(jnp.bfloat16)
        .reshape(text_count, block_size, model_width)
    )
    key_low = (
        projected[:, model_width : 2 * model_width]
        .astype(jnp.bfloat16)
        .reshape(text_count, block_size, model_width)
    )
    value_low = (
        (projected[:, 2 * model_width :] + value_bias)
        .astype(jnp.bfloat16)
        .reshape(text_count, block_size, model_width)
    )
    pair_ext = extended(jnp.stack([key_low, value_low]), (("seq", 2),), window)
    key_ext = pair_ext[0]
    value_ext = pair_ext[1]
    seq_index = lax.axis_index("seq")
    query_pos = seq_index * block_size + jnp.arange(block_size, dtype=jnp.int32)
    key_pos = seq_index * block_size - window + jnp.arange(block_size + 2 * window, dtype=jnp.int32)
    near = jnp.abs(query_pos[:, None] - key_pos[None, :]) <= window
    itself = query_pos[:, None] == key_pos[None, :]
    inside = (key_pos[None, None, :] < lengths[:, None, None]) & (key_pos[None, None, :] >= 0)
    allowed = (near[None] & (inside | itself[None]))[:, None]
    group_width = 2 * HEAD
    group_count = model_width // group_width
    mixed_list = []
    total_list = []
    for group_index in range(group_count):
        queries = split_heads(query_low, group_index, group_width)
        keys_group = split_heads(key_ext, group_index, group_width)
        values_group = split_heads(value_ext, group_index, group_width)
        scores = masked_scores(queries, keys_group, allowed)
        row_peak = jnp.max(scores, axis=-1, keepdims=True)
        log_total = row_peak + jnp.log(jnp.sum(jnp.exp(scores - row_peak), axis=-1, keepdims=True))
        weights_low = jnp.exp(scores - log_total).astype(jnp.bfloat16)
        mixed_heads = jnp.einsum(
            "thqk,tkhe->tqhe", weights_low, values_group, preferred_element_type=jnp.float32
        )
        mixed_list.append(mixed_heads.reshape(text_count, block_size, group_width))
        total_list.append(log_total)
    attended_low = (
        jnp.concatenate(mixed_list, axis=-1).astype(jnp.bfloat16).reshape(token_rows, model_width)
    )
    middle = (
        layer_input
        + jnp.dot(attended_low, out_weight, preferred_element_type=jnp.float32)
        + out_bias
    )
    normed_two_low = normalize(middle, gain_two, bias_two).astype(jnp.bfloat16)
    expanded = (
        jnp.dot(normed_two_low, expand_full, preferred_element_type=jnp.float32) + expand_bias
    )
    gated_low = smooth_gate(expanded).astype(jnp.bfloat16)
    layer_output = (
        middle + jnp.dot(gated_low, shrink_full, preferred_element_type=jnp.float32) + shrink_bias
    )
    layer_output = layer_output.astype(jnp.bfloat16).reshape(text_count, block_size, model_width)
    upstream = cotangent.reshape(token_rows, model_width)
    upstream_float = upstream.astype(jnp.float32)
    grad_shrink = across(gated_low, upstream)
    grad_shrink_bias = jnp.sum(upstream_float, axis=0)
    gate_grad = against(upstream, shrink_full)
    unused_gate, gate_back = jax.vjp(smooth_gate, expanded)
    expanded_grad = gate_back(gate_grad)[0].astype(jnp.bfloat16)
    grad_expand = across(normed_two_low, expanded_grad)
    grad_expand_bias = jnp.sum(expanded_grad.astype(jnp.float32), axis=0)
    normed_two_grad = against(expanded_grad, expand_full)
    unused_norm, norm_two_back = jax.vjp(normalize, middle, gain_two, bias_two)
    middle_part, grad_gain_two, grad_bias_two = norm_two_back(normed_two_grad)
    middle_grad = upstream_float + middle_part
    branch_grad = middle_grad.astype(jnp.bfloat16)
    grad_out_bias = jnp.sum(branch_grad.astype(jnp.float32), axis=0)
    grad_out = across(attended_low, branch_grad)
    attended_grad = (
        against(branch_grad, out_weight)
        .astype(jnp.bfloat16)
        .reshape(text_count, block_size, model_width)
    )
    query_grads = []
    key_grads = []
    value_grads = []
    for group_index in range(group_count):
        queries = split_heads(query_low, group_index, group_width)
        keys_group = split_heads(key_ext, group_index, group_width)
        values_group = split_heads(value_ext, group_index, group_width)
        scores = masked_scores(queries, keys_group, allowed)
        soft_weights = jnp.exp(scores - total_list[group_index])
        weights_low = soft_weights.astype(jnp.bfloat16)
        upstream_group = split_heads(attended_grad, group_index, group_width)
        weight_grad = jnp.einsum(
            "tqhe,tkhe->thqk", upstream_group, values_group, preferred_element_type=jnp.float32
        )
        value_grad = jnp.einsum(
            "thqk,tqhe->tkhe", weights_low, upstream_group, preferred_element_type=jnp.float32
        )
        score_grad = soft_weights * (
            weight_grad - jnp.sum(weight_grad * soft_weights, axis=-1, keepdims=True)
        )
        score_low = score_grad.astype(jnp.bfloat16)
        query_grad = (
            jnp.einsum("thqk,tkhe->tqhe", score_low, keys_group, preferred_element_type=jnp.float32)
            * 0.125
        )
        key_grad = (
            jnp.einsum("thqk,tqhe->tkhe", score_low, queries, preferred_element_type=jnp.float32)
            * 0.125
        )
        query_grads.append(query_grad.reshape(text_count, block_size, group_width))
        key_grads.append(key_grad.reshape(text_count, block_size + 2 * window, group_width))
        value_grads.append(value_grad.reshape(text_count, block_size + 2 * window, group_width))
    query_grad_low = jnp.concatenate(query_grads, axis=-1).astype(jnp.bfloat16)
    pair_grad = jnp.stack(
        [jnp.concatenate(key_grads, axis=-1), jnp.concatenate(value_grads, axis=-1)]
    )
    from_above = from_behind(pair_grad[:, :, :window].astype(jnp.bfloat16), "seq", -1).astype(
        jnp.float32
    )
    from_below = from_behind(
        pair_grad[:, :, block_size + window :].astype(jnp.bfloat16), "seq", 1
    ).astype(jnp.float32)
    pair_own = pair_grad[:, :, window : window + block_size]
    pair_own = pair_own.at[:, :, block_size - window :].add(from_above)
    pair_own = pair_own.at[:, :, :window].add(from_below)
    pair_low = pair_own.astype(jnp.bfloat16)
    combined = jnp.concatenate([query_grad_low, pair_low[0], pair_low[1]], axis=-1).reshape(
        token_rows, 3 * model_width
    )
    grad_qkv = across(normed_low, combined).reshape(model_width, 3, model_width)
    grad_attend = jnp.concatenate([grad_qkv, grad_out[:, None, :]], axis=1)
    combined_float = jnp.sum(combined.astype(jnp.float32), axis=0)
    grad_query_bias = combined_float[:model_width]
    grad_value_bias = combined_float[2 * model_width :]
    normed_grad = against(combined, qkv_weight)
    unused_first, norm_one_back = jax.vjp(normalize, layer_input, gain_one, bias_one)
    input_part, grad_gain_one, grad_bias_one = norm_one_back(normed_grad)
    characters_grad = (
        (middle_grad + input_part).astype(jnp.bfloat16).reshape(text_count, block_size, model_width)
    )
    vector_terms = jnp.concatenate(
        [
            jnp.stack(
                [
                    grad_gain_one,
                    grad_bias_one,
                    grad_query_bias,
                    grad_value_bias,
                    grad_out_bias,
                    grad_gain_two,
                    grad_bias_two,
                    grad_shrink_bias,
                ]
            ),
            grad_expand_bias.reshape(-1, model_width),
        ],
        axis=0,
    )
    attend_rows, expand_rows, shrink_rows = (
        lax.psum_scatter(grad_attend, ("seq", "dp"), scatter_dimension=0, tiled=True),
        lax.psum_scatter(grad_expand[:, None, :], ("seq", "dp"), scatter_dimension=0, tiled=True),
        lax.psum_scatter(grad_shrink[:, None, :], ("seq", "dp"), scatter_dimension=0, tiled=True),
    )
    vector_sum = lax.psum(vector_terms, ("seq", "dp"))
    attend_rows = attend_rows * grad_scale
    expand_rows = expand_rows * grad_scale
    shrink_rows = shrink_rows * grad_scale
    vector_grad = vector_sum * grad_scale
    vector_newacc = vector_acc + vector_grad * vector_grad
    vector_new = vectors - VECTOR_RATE * vector_grad / (jnp.sqrt(vector_newacc) + 1e-08)
    whole_attend, whole_expand, whole_shrink = (
        lax.all_gather(attend_rows.astype(jnp.bfloat16), ("seq", "dp"), axis=0, tiled=True).astype(
            attend_rows.dtype
        ),
        lax.all_gather(expand_rows.astype(jnp.bfloat16), ("seq", "dp"), axis=0, tiled=True).astype(
            expand_rows.dtype
        ),
        lax.all_gather(shrink_rows.astype(jnp.bfloat16), ("seq", "dp"), axis=0, tiled=True).astype(
            shrink_rows.dtype
        ),
    )
    attend_square, attend_newleft, attend_newright = statistics(
        attend_rows, whole_attend, attend_left, attend_right, wide_index
    )
    expand_square, expand_newleft, expand_newright = statistics(
        expand_rows, whole_expand, expand_left[:, None, :], expand_right[:, None, :], wide_index
    )
    shrink_square, shrink_newleft, shrink_newright = statistics(
        shrink_rows, whole_shrink, shrink_left[:, None, :], shrink_right[:, None, :], wide_index
    )
    attend_applied, expand_applied, shrink_applied = (
        lax.all_gather(
            left_apply(attend_rootleft, whole_attend).astype(jnp.bfloat16),
            ("seq", "dp"),
            axis=0,
            tiled=True,
        ).astype(jnp.float32),
        lax.all_gather(
            left_apply(expand_rootleft[:, None, :], whole_expand).astype(jnp.bfloat16),
            ("seq", "dp"),
            axis=0,
            tiled=True,
        ).astype(jnp.float32),
        lax.all_gather(
            left_apply(shrink_rootleft[:, None, :], whole_shrink).astype(jnp.bfloat16),
            ("seq", "dp"),
            axis=0,
            tiled=True,
        ).astype(jnp.float32),
    )
    attend_direction = right_apply(attend_applied, attend_rootright)
    expand_direction = right_apply(expand_applied, expand_rootright[:, None, :])
    shrink_direction = right_apply(shrink_applied, shrink_rootright[:, None, :])
    attend_newmoment, attend_newweight = finish(
        attend_direction, attend_square, attend_moment, attend_weight
    )
    expand_newmoment, expand_newweight = finish(
        expand_direction, expand_square, expand_moment[:, None, :], expand_weight[:, None, :]
    )
    shrink_newmoment, shrink_newweight = finish(
        shrink_direction, shrink_square, shrink_moment[:, None, :], shrink_weight[:, None, :]
    )
    return (
        layer_output,
        characters_grad,
        attend_rows,
        attend_newmoment,
        attend_newweight,
        attend_newleft,
        attend_newright,
        expand_rows[:, 0, :],
        expand_newmoment[:, 0, :],
        expand_newweight[:, 0, :],
        expand_newleft[:, 0, :],
        expand_newright[:, 0, :],
        shrink_rows[:, 0, :],
        shrink_newmoment[:, 0, :],
        shrink_newweight[:, 0, :],
        shrink_newleft[:, 0, :],
        shrink_newright[:, 0, :],
        vector_grad,
        vector_newacc,
        vector_new,
    )


def solution(mesh):
    return jax.shard_map(
        shards,
        mesh=mesh,
        in_specs=(
            P("dp", "seq", None),
            P("dp", "seq", None),
            P("dp"),
            P(),
            P(),
            P(None, None, ("seq", "dp")),
            P(None, None, ("seq", "dp")),
            P(("seq", "dp"), None, None),
            P(None, None, ("seq", "dp")),
            P(("seq", "dp"), None, None),
            P(None, None, ("seq", "dp")),
            P(None, ("seq", "dp")),
            P(None, ("seq", "dp")),
            P(("seq", "dp"), None),
            P(None, ("seq", "dp")),
            P(("seq", "dp"), None),
            P(None, ("seq", "dp")),
            P(None, ("seq", "dp")),
            P(None, ("seq", "dp")),
            P(("seq", "dp"), None),
            P(None, ("seq", "dp")),
            P(("seq", "dp"), None),
            P(None, ("seq", "dp")),
        ),
        out_specs=(
            P("dp", "seq", None),
            P("dp", "seq", None),
            P(("seq", "dp"), None, None),
            P(None, None, ("seq", "dp")),
            P(None, None, ("seq", "dp")),
            P(("seq", "dp"), None, None),
            P(None, None, ("seq", "dp")),
            P(("seq", "dp"), None),
            P(None, ("seq", "dp")),
            P(None, ("seq", "dp")),
            P(("seq", "dp"), None),
            P(None, ("seq", "dp")),
            P(("seq", "dp"), None),
            P(None, ("seq", "dp")),
            P(None, ("seq", "dp")),
            P(("seq", "dp"), None),
            P(None, ("seq", "dp")),
            P(),
            P(),
            P(),
        ),
        check_vma=False,
    )
```

profile of v0, /device:TPU:0, one launch (start us, length us, event | category | flops | bytes accessed | tf_op | source)
XLA Modules:
  0.0 1098.0 jit_solution(11447907366498030084)
XLA Ops:
  23.2 54.8 %all-gather.10.cloned.1.call-done = bf16[768,4,768]{0,2,1:T(8,128)(2,1)} async-done(((bf16[768,4,24]{0,2,1:T(8,128)(2,1)}), bf16[768,4,768]{0,2,1:T(8,128)(2,1)}) %all-gather.10.cloned.1.call-update) | async-done | bytes 4718608 | tf_op jit(solution)/shard_map/all_gather | solution.py:138
  80.5 3.9 fusion.222
  133.3 4.8 fusion.226
  141.9 3.7 fusion.224
  146.7 4.6 fusion.13
  151.3 13.5 %exponential_reduce_fusion = (f32[2,2,512]{2,1,0:T(2,128)S(1)}, f32[2,2,512]{2,1,0:T(2,128)S(1)}, f32[2,2,512]{2,1,0:T(2,128)S(1)}, f32[2,2,512]{2,1,0:T(2,128)S...) fusion(f32[2,2,512,768]{3,2,1,0:T(8,128)} %get-tuple-element.184, ...), kind=kOutput, calls=%fused_computation.43 | convolution fusion | flops 232771584 | bytes 39256064 | tf_op jit(solution)/shard_map/tqhe,tkhe->thqk/dot_general | solution.py:73
  164.9 11.7 %exponential_reduce_fusion.1 = (f32[2,2,512]{2,1,0:T(2,128)S(1)}, f32[2,2,512]{2,1,0:T(2,128)S(1)}, f32[2,2,512]{2,1,0:T(2,128)S(1)}, f32[2,2,512]{2,1,0:T(2,128)S(1)}) fusion(f32[2,2,512,768]{3,2,1,0:T(8,128)} %fusion.226, f32[2,2,512]{2,1,0:T(2,128)S(1)} %get-tuple-element.101, pred[2,512,768]{2,1,0:T(8,128)(4,1)S(1)} %or_and_fusion, ...), kind=kLoop, calls=%fused_computation.46 | loop fusion | flops 25157632 | bytes 26017792 | tf_op jit(solution)/shard_map/reduce_sum | solution.py:191
  180.0 4.9 fusion.125
  201.9 37.0 %multiply_convert_fusion = (bf16[1024,3072]{1,0:T(8,128)(2,1)}, f32[1024,3072]{1,0:T(8,128)}, f32[1024,3072]{1,0:T(8,128)}) fusion(f32[3072]{0:T(1024)} %add.301, bf16[768,3072]{0,1:T(8,128)(2,1)} %all-gather.12.cloned.1.call-done, f32[1024,768]{1,0:T(8,128)} %copy-done.9, f32[768]{0:T(1024)S(1)} %get-tuple-element.110, f32[768]{0:T(1024)S(1)} %get-tuple-element.111, ...), kind=kOutput, calls=%fused_computation.9 | convolution fusion | flops 5043388416 | bytes 39348224 | tf_op jit(solution)/shard_map/dot_general | solution.py:208
  239.0 17.5 %convert_reduce_fusion = (f32[3072]{0:T(1024)}, bf16[1024,3072]{1,0:T(8,128)(2,1)}) fusion(f32[1024,3072]{1,0:T(8,128)} %get-tuple-element.125, bf16[1024,768]{1,0:T(8,128)(2,1)S(1)} %bitcast.496, bf16[3072,768]{0,1:T(8,128)(2,1)} %all-gather.14.cloned.1.call-done, f32[1024,3072]{1,0:T(8,128)} %get-tuple-element.188, f32[3072]{0:T(1024)S(1)} %copy-done.117), kind=kOutput, calls=%fused_computation.7 | convolution fusion | flops 4885312512 | bytes 37773312 | tf_op jit(solution)/shard_map/dot_general | solution.py:61
  256.5 10.7 convolution_bitcast_fusion.1
  267.3 10.8 multiply_reduce_fusion.9
  295.5 4.8 fusion.231
  303.9 4.0 fusion.229
  307.9 3.7 fusion.228
  330.1 7.6 convolution_bitcast_fusion
  337.9 28.5 %multiply_reduce_fusion.3 = (f32[2,2,512]{2,1,0:T(2,128)}, f32[2,2,512]{2,1,0:T(2,128)}, f32[2,2,512]{2,1,0:T(2,128)}, f32[2,2,512]{2,1,0:T(2,128)}, f32[2,2,512...) fusion(f32[2,2,512,768]{3,2,1,0:T(8,128)} %get-tuple-element.184, ...), kind=kOutput, calls=%fused_computation.31 | convolution fusion | flops 248500224 | bytes 77037568 | tf_op jit(solution)/shard_map/tqhe,tkhe->thqk/dot_general | solution.py:247
  366.4 12.9 %multiply_convert_fusion.2 = (bf16[2,2,512,768]{3,2,1,0:T(8,128)(2,1)}, bf16[2,2,512,768]{3,2,1,0:T(8,128)(2,1)}) fusion(f32[2,2,512,768]{3,2,1,0:T(8,128)} %fusion.231, f32[2,2,512,768]{3,2,1,0:T(8,128)} %fusion.226, f32[2,2,512]{2,1,0:T(2,128)S(1)} %get-tuple-element.96, f32[2,2,512]{2,1,0:T(2,128)S(1)} %copy-done.99, ...), kind=kLoop, calls=%fused_computation.32 | loop fusion | flops 18874368 | bytes 32276480 | tf_op jit(solution)/shard_map/convert_element_type | solution.py:256
  379.2 4.9 fusion.193
  403.8 22.5 %multiply_convert_fusion.1 = (bf16[2,2,512,768]{3,2,1,0:T(8,128)(2,1)S(1)}, bf16[2,2,512,768]{3,2,1,0:T(8,128)(2,1)}, bf16[2,2,512,768]{3,2,1,0:T(8,128)(2,1)}, bf16[2,2,512,768]{3,2,1,0:T(8,128)(2,1)}) fusion(f32[2,2,512,768]{3,2,1,0:T(8,128)} %get-tuple-element.190, f32[2,2,512,768]{3,2,1,0:T(8,128)} %get-tuple-element.184, ...), kind=kLoop, calls=%fused_computation.30 | loop fusion | flops 37748736 | bytes 63766528 | tf_op jit(solution)/shard_map/convert_element_type | solution.py:256
  431.9 3.8 fusion.132
  446.2 3.9 fusion.130
  503.2 4.0 fusion.7
  517.1 6.8 copy.126
  523.8 6.9 fusion.232
  530.7 4.2 pad_maximum_fusion.1
  536.8 7.4 reduce-scatter.8.cloned.1.call-done
  546.1 138.7 %reduce-scatter.4.cloned.1.call-done = f32[24,4,768]{2,0,1:T(8,128)} async-done(((f32[768,4,768]{2,0,1:T(8,128)}), f32[24,4,768]{2,0,1:T(8,128)}) %reduce-scatter.4.cloned.1.call-update) | async-done | bytes 294928 | tf_op jit(solution)/shard_map/reduce_scatter | solution.py:315
  686.6 64.8 %all-gather.20.cloned.1.call-done = bf16[768,1,3072]{2,0,1:T(8,128)(2,1)} async-done(((bf16[24,1,3072]{2,0,1:T(8,128)(2,1)}), bf16[768,1,3072]{2,0,1:T(8,128)(2,1)}) %all-gather.20.cloned.1.call-update) | async-done | bytes 4718608 | tf_op jit(solution)/shard_map/all_gather | solution.py:330
  751.4 4.9 fusion.60
  756.6 61.2 %all-gather.24.cloned.1.call-done = bf16[3072,1,768]{2,0,1:T(8,128)(2,1)} async-done(((bf16[96,1,768]{2,0,1:T(8,128)(2,1)}), bf16[3072,1,768]{2,0,1:T(8,128)(2,1)}) %all-gather.24.cloned.1.call-update) | async-done | bytes 4718608 | tf_op jit(solution)/shard_map/all_gather | solution.py:333
  817.8 5.3 fusion.140
  823.5 60.7 %all-gather.16.cloned.1.call-done = bf16[768,4,768]{2,0,1:T(8,128)(2,1)} async-done(((bf16[24,4,768]{2,0,1:T(8,128)(2,1)}), bf16[768,4,768]{2,0,1:T(8,128)(2,1)}) %all-gather.16.cloned.1.call-update) | async-done | bytes 4718608 | tf_op jit(solution)/shard_map/all_gather | solution.py:327
  884.3 5.0 fusion.139
  889.4 10.1 add_convert_fusion.2
  899.5 7.0 fusion.210
  911.4 40.6 %psum.7 = f32[12,768]{1,0:T(8,128)S(1)} all-reduce(f32[12,768]{1,0:T(8,128)S(1)} %concatenate.80), channel_id=1, replica_groups=mesh['seq'=4,'dp'=8] {'seq','dp'}, use_global_device_ids=true, to_apply=%region_40.41 | all-reduce | flops 9216 | bytes 73728 | tf_op jit(solution)/shard_map/psum | solution.py:319
  952.8 5.2 add_convert_fusion.1
  962.6 5.5 multiply_reduce_fusion
  968.8 4.7 fusion.170
  973.5 6.8 fusion.158
  982.5 5.5 fusion.72
  989.3 4.0 fusion.115
  996.0 7.2 fusion.133
  1004.0 13.4 %all-gather.26.cloned.1.call-done = bf16[3072,1,768]{2,0,1:T(8,128)(2,1)} async-done(((bf16[96,1,768]{2,0,1:T(8,128)(2,1)}), bf16[3072,1,768]{2,0,1:T(8,128)(2,1)}) %all-gather.26.cloned.1.call-update) | async-done | bytes 4718608 | tf_op jit(solution)/shard_map/all_gather | solution.py:359
  1017.4 6.1 fusion.54
  1024.4 59.4 %all-gather.18.cloned.1.call-done = bf16[768,4,768]{2,0,1:T(8,128)(2,1)} async-done(((bf16[24,4,768]{2,0,1:T(8,128)(2,1)}), bf16[768,4,768]{2,0,1:T(8,128)(2,1)}) %all-gather.18.cloned.1.call-update) | async-done | bytes 4718608 | tf_op jit(solution)/shard_map/all_gather | solution.py:347
  1083.8 6.9 multiply_subtract_fusion
  (544 shorter events, 252.7 us)
Async XLA Ops:
  7.2 810.6 %copy-start = (f32[96,3072]{1,0:T(8,128)S(1)}, f32[96,3072]{1,0:T(8,128)}, u32[]{:S(2)}) copy-start(f32[96,3072]{1,0:T(8,128)} %param.48) | copy-start | bytes 3538948
  7.2 14.2 %copy-start.5 = (bf16[2,512,768]{2,1,0:T(8,128)(2,1)S(1)}, bf16[2,512,768]{2,1,0:T(8,128)(2,1)}, u32[]{:S(2)}) copy-start(bf16[2,512,768]{2,1,0:T(8,128)(2,1)} %param.27) | copy-start | bytes 4718596
  7.2 70.8 %all-gather.10.cloned.1.call-start = ((), (), s32[]{:S(2)}) async-start(), calls=%async_computation.3 | async-start | bytes 4866048 | tf_op jit(solution)/shard_map/all_gather | solution.py:138
  9.1 192.8 %all-gather.12.cloned.1.call-start = ((), (), s32[]{:S(2)}) async-start(), calls=%async_computation.4 | async-start | bytes 4866048 | tf_op jit(solution)/shard_map/all_gather | solution.py:139
  10.8 228.1 %all-gather.14.cloned.1.call-start = ((), (), s32[]{:S(2)}) async-start(), calls=%async_computation.5 | async-start | bytes 4866048 | tf_op jit(solution)/shard_map/all_gather | solution.py:140
  12.5 522.5 %reduce-scatter.6.cloned.1.call-start = ((), (), s32[]{:S(2)}) async-start(), calls=%async_computation.9 | async-start | bytes 9732096 | tf_op jit(solution)/shard_map/reduce_scatter | solution.py:316
  14.3 66.0 %copy-start.106 = (f32[768]{0:T(1024)}, f32[768]{0:T(1024)S(1)}, u32[]{:S(2)}) copy-start(f32[768]{0:T(1024)S(1)} %get-tuple-element.116) | copy-start | bytes 9220
  86.9 17.1 %collective-permute-start = (bf16[2,2,128,768]{3,2,1,0:T(8,128)(2,1)}, bf16[2,2,128,768]{3,2,1,0:T(8,128)(2,1)}, u32[]{:S(2)}, u32[]{:S(2)}) collective-permute-start(bf16[2,2,128,768]{3,2,1,0:T(8,128)(2,1)} %get-tuple-element.134), channel_id=1, source_target_pairs={{0,8},{8,16},{16,24},{1,9},{9,17},{17,25},{2,10},{10,18},{18,26},{... | collective-permute-start | bytes 2359304 | tf_op jit(solution)/shard_map/ppermute | solution.py:29
  89.9 14.1 %collective-permute-start.1 = (bf16[2,2,128,768]{3,2,1,0:T(8,128)(2,1)}, bf16[2,2,128,768]{3,2,1,0:T(8,128)(2,1)}, u32[]{:S(2)}, u32[]{:S(2)}) collective-permute-start(bf16[2,2,128,768]{3,2,1,0:T(8,128)(2,1)} %get-tuple-element.135), channel_id=1, source_target_pairs={{8,0},{16,8},{24,16},{9,1},{17,9},{25,17},{10,2},{18,10},{26,18},{... | collective-permute-start | bytes 2359304 | tf_op jit(solution)/shard_map/ppermute | solution.py:31
  91.9 101.5 %copy-start.7 = (pred[2,512,768]{2,1,0:T(8,128)(4,1)}, pred[2,512,768]{2,1,0:T(8,128)(4,1)S(1)}, u32[]{:S(2)}) copy-start(pred[2,512,768]{2,1,0:T(8,128)(4,1)S(1)} %or_and_fusion) | copy-start | bytes 2359300
  146.6 44.0 %copy-start.1 = (f32[2,2,512,768]{3,2,1,0:T(8,128)}, f32[2,2,512,768]{3,2,1,0:T(8,128)S(1)}, u32[]{:S(2)}) copy-start(f32[2,2,512,768]{3,2,1,0:T(8,128)S(1)} %fusion.223) | copy-start | bytes 18874372
  164.9 28.5 %copy-start.90 = (f32[2,2,512]{2,1,0:T(2,128)}, f32[2,2,512]{2,1,0:T(2,128)S(1)}, u32[]{:S(2)}) copy-start(f32[2,2,512]{2,1,0:T(2,128)S(1)} %log_add_fusion) | copy-start | bytes 24580
  164.9 25.8 %copy-start.92 = (f32[2,2,512]{2,1,0:T(2,128)}, f32[2,2,512]{2,1,0:T(2,128)S(1)}, u32[]{:S(2)}) copy-start(f32[2,2,512]{2,1,0:T(2,128)S(1)} %log_add_fusion.5) | copy-start | bytes 24580
  201.9 37.1 %copy-start.15 = (bf16[2,512,768]{2,1,0:T(8,128)(2,1)S(1)}, bf16[2,512,768]{2,1,0:T(8,128)(2,1)}, u32[]{:S(2)}) copy-start(bf16[2,512,768]{2,1,0:T(8,128)(2,1)} %param.28) | copy-start | bytes 4718596
  201.9 37.0 %copy-start.117 = (f32[3072]{0:T(1024)S(1)}, f32[3072]{0:T(1024)}, u32[]{:S(2)}) copy-start(f32[3072]{0:T(1024)} %add.301) | copy-start | bytes 36868
  239.0 17.5 %copy-start.10 = (f32[1024,768]{1,0:T(8,128)S(1)}, f32[1024,768]{1,0:T(8,128)}, u32[]{:S(2)}) copy-start(f32[1024,768]{1,0:T(8,128)} %copy-done.9) | copy-start | bytes 9437188
  267.3 277.0 %reduce-scatter.8.cloned.1.call-start = ((), (), s32[]{:S(2)}) async-start(), calls=%async_computation.12 | async-start | bytes 9732096 | tf_op jit(solution)/shard_map/reduce_scatter | solution.py:317
  337.8 347.0 %reduce-scatter.4.cloned.1.call-start = ((), (), s32[]{:S(2)}) async-start(), calls=%async_computation.6 | async-start | bytes 9732096 | tf_op jit(solution)/shard_map/reduce_scatter | solution.py:315
  337.8 28.5 %copy-start.99 = (f32[2,2,512]{2,1,0:T(2,128)S(1)}, f32[2,2,512]{2,1,0:T(2,128)}, u32[]{:S(2)}) copy-start(f32[2,2,512]{2,1,0:T(2,128)} %copy-done.98) | copy-start | bytes 24580
  337.9 28.5 %copy-start.102 = (f32[2,2,512]{2,1,0:T(2,128)S(1)}, f32[2,2,512]{2,1,0:T(2,128)}, u32[]{:S(2)}) copy-start(f32[2,2,512]{2,1,0:T(2,128)} %copy-done.100) | copy-start | bytes 24580
  403.8 24.2 %copy-start.39 = (bf16[2,512,128]{1,2,0:T(8,128)(2,1)S(1)}, bf16[2,512,128]{1,2,0:T(8,128)(2,1)}, u32[]{:S(2)}) copy-start(bf16[2,512,128]{1,2,0:T(8,128)(2,1)} %copy.93) | copy-start | bytes 786436
  431.9 14.3 %copy-start.25 = (bf16[2,768,128]{1,2,0:T(8,128)(2,1)S(1)}, bf16[2,768,128]{1,2,0:T(8,128)(2,1)}, u32[]{:S(2)}) copy-start(bf16[2,768,128]{1,2,0:T(8,128)(2,1)} %copy.82) | copy-start | bytes 1179652
  446.2 14.2 %copy-start.23 = (bf16[2,768,128]{1,2,0:T(8,128)(2,1)S(1)}, bf16[2,768,128]{1,2,0:T(8,128)(2,1)}, u32[]{:S(2)}) copy-start(bf16[2,768,128]{1,2,0:T(8,128)(2,1)} %copy.86) | copy-start | bytes 1179652
  490.5 21.8 %collective-permute-start.3 = (bf16[2,2,128,768]{3,2,1,0:T(8,128)(2,1)}, bf16[2,2,128,768]{3,2,1,0:T(8,128)(2,1)}, u32[]{:S(2)}, u32[]{:S(2)}) collective-permute-start(bf16[2,2,128,768]{3,2,1,0:T(8,128)(2,1)} %get-tuple-element.128), channel_id=1, source_target_pairs={{0,8},{8,16},{16,24},{1,9},{9,17},{17,25},{2,10},{10,18},{18,26},{... | collective-permute-start | bytes 2359304 | tf_op jit(solution)/shard_map/ppermute | solution.py:41
  494.0 16.7 %collective-permute-start.2 = (bf16[2,2,128,768]{3,2,1,0:T(8,128)(2,1)}, bf16[2,2,128,768]{3,2,1,0:T(8,128)(2,1)}, u32[]{:S(2)}, u32[]{:S(2)}) collective-permute-start(bf16[2,2,128,768]{3,2,1,0:T(8,128)(2,1)} %get-tuple-element.129), channel_id=1, source_target_pairs={{8,0},{16,8},{24,16},{9,1},{17,9},{25,17},{10,2},{18,10},{26,18},{... | collective-permute-start | bytes 2359304 | tf_op jit(solution)/shard_map/ppermute | solution.py:41
  534.9 216.5 %copy-start.105 = (f32[24,768]{1,0:T(8,128)S(1)}, f32[24,768]{1,0:T(8,128)}, u32[]{:S(2)}) copy-start(f32[24,768]{1,0:T(8,128)} %param.42) | copy-start | bytes 221188
  534.9 216.5 %all-gather.20.cloned.1.call-start = ((), (), s32[]{:S(2)}) async-start(), calls=%async_computation.10 | async-start | bytes 4866048 | tf_op jit(solution)/shard_map/all_gather | solution.py:330
  536.8 281.0 %all-gather.24.cloned.1.call-start = ((), (), s32[]{:S(2)}) async-start(), calls=%async_computation.13 | async-start | bytes 4866048 | tf_op jit(solution)/shard_map/all_gather | solution.py:333
  546.0 338.2 %all-gather.16.cloned.1.call-start = ((), (), s32[]{:S(2)}) async-start(), calls=%async_computation.7 | async-start | bytes 4866048 | tf_op jit(solution)/shard_map/all_gather | solution.py:327
  686.6 309.4 %all-gather.22.cloned.1.call-start = ((), (), s32[]{:S(2)}) async-start(), calls=%async_computation.11 | async-start | bytes 4866048 | tf_op jit(solution)/shard_map/all_gather | solution.py:353
  756.4 67.1 %copy-start.114 = (f32[1,4,2,128]{3,2,1,0:T(2,128)S(1)}, f32[1,4,2,128]{3,2,1,0:T(2,128)}, u32[]{:S(2)}) copy-start(f32[1,4,2,128]{3,2,1,0:T(2,128)} %get-tuple-element.180) | copy-start | bytes 12292
  756.4 67.1 %copy-start.115 = (f32[1,4,2,128]{3,2,1,0:T(2,128)S(1)}, f32[1,4,2,128]{3,2,1,0:T(2,128)}, u32[]{:S(2)}) copy-start(f32[1,4,2,128]{3,2,1,0:T(2,128)} %get-tuple-element.178) | copy-start | bytes 12292
  756.4 127.9 %copy-start.83 = (f32[24,4,768]{2,1,0:T(4,128)S(1)}, f32[24,4,768]{2,1,0:T(4,128)}, u32[]{:S(2)}) copy-start(f32[24,4,768]{2,1,0:T(4,128)} %param.36) | copy-start | bytes 884740
  756.4 261.0 %all-gather.26.cloned.1.call-start = ((), (), s32[]{:S(2)}) async-start(), calls=%async_computation.14 | async-start | bytes 4866048 | tf_op jit(solution)/shard_map/all_gather | solution.py:359
  823.1 66.2 %copy-start.118 = (f32[768]{0:T(1024)S(1)}, f32[768]{0:T(1024)}, u32[]{:S(2)}) copy-start(f32[768]{0:T(1024)} %get-tuple-element.109) | copy-start | bytes 9220
  823.2 260.6 %all-gather.18.cloned.1.call-start = ((), (), s32[]{:S(2)}) async-start(), calls=%async_computation.8 | async-start | bytes 4866048 | tf_op jit(solution)/shard_map/all_gather | solution.py:347
  906.6 45.5 %copy-start.89 = (f32[12,768]{1,0:T(8,128)S(1)}, f32[12,768]{1,0:T(8,128)}, u32[]{:S(2)}) copy-start(f32[12,768]{1,0:T(8,128)} %param.30) | copy-start | bytes 110596
  906.6 45.5 %copy-start.108 = (f32[12,768]{1,0:T(8,128)S(1)}, f32[12,768]{1,0:T(8,128)}, u32[]{:S(2)}) copy-start(f32[12,768]{1,0:T(8,128)} %param.31) | copy-start | bytes 110596
  906.6 46.2 %copy-start.112 = (f32[1024]{0:T(1024)S(1)}, f32[1024]{0:T(1024)}, u32[]{:S(2)}) copy-start(f32[1024]{0:T(1024)} %copy-done.111) | copy-start | bytes 12292
  908.2 50.6 %slice-start.12 = ((s8[4718592]{0:T(1024)(128)(4,1)}), s8[524288]{0:T(1024)(128)(4,1)S(1)}, s32[]{:S(2)}) async-start(s8[4718592]{0:T(1024)(128)(4,1)} %bitcast.476), calls=%async_computation.27 | async-start | bytes 1048576
  962.6 17.7 %slice-start.14 = ((s8[4718592]{0:T(1024)(128)(4,1)}), s8[524288]{0:T(1024)(128)(4,1)S(1)}, s32[]{:S(2)}) async-start(s8[4718592]{0:T(1024)(128)(4,1)} %bitcast.478), calls=%async_computation.29 | async-start | bytes 1048576
  996.0 21.5 %copy-start.85 = (f32[3072,24]{0,1:T(8,128)S(1)}, f32[3072,24]{0,1:T(8,128)}, u32[]{:S(2)}) copy-start(f32[3072,24]{0,1:T(8,128)} %param.45) | copy-start | bytes 884740
  1003.2 87.5 %copy-start.43 = (f32[768,1,96]{0,2,1:T(8,128)}, f32[768,1,96]{0,2,1:T(8,128)S(1)}, u32[]{:S(2)}) copy-start(f32[768,1,96]{0,2,1:T(8,128)S(1)} %fusion.133) | copy-start | bytes 884740
  1003.2 20.3 %copy-start.66 = (f32[3072,24]{0,1:T(8,128)S(1)}, f32[3072,24]{0,1:T(8,128)}, u32[]{:S(2)}) copy-start(f32[3072,24]{0,1:T(8,128)} %param.44) | copy-start | bytes 884740
  1003.2 80.5 %copy-start.63 = (f32[768,4,24]{0,2,1:T(8,128)S(1)}, f32[768,4,24]{0,2,1:T(8,128)}, u32[]{:S(2)}) copy-start(f32[768,4,24]{0,2,1:T(8,128)} %param.32) | copy-start | bytes 884740
  1003.3 80.5 %copy-start.86 = (f32[768,4,24]{0,2,1:T(8,128)S(1)}, f32[768,4,24]{0,2,1:T(8,128)}, u32[]{:S(2)}) copy-start(f32[768,4,24]{0,2,1:T(8,128)} %param.37) | copy-start | bytes 884740
  1003.3 80.5 %copy-start.87 = (f32[768,4,24]{0,2,1:T(8,128)S(1)}, f32[768,4,24]{0,2,1:T(8,128)}, u32[]{:S(2)}) copy-start(f32[768,4,24]{0,2,1:T(8,128)} %param.33) | copy-start | bytes 884740
  1023.6 67.1 %copy-start.62 = (f32[3072,1,24]{0,2,1:T(8,128)}, f32[3072,1,24]{0,2,1:T(8,128)S(1)}, u32[]{:S(2)}) copy-start(f32[3072,1,24]{0,2,1:T(8,128)S(1)} %fusion.54) | copy-start | bytes 884740
  (121 other events, 686.9 us)
Sparse Core Ops, SparseCore 0:
  11.5 66.4 all-gather.9
  81.5 62.3 all-gather.11
  147.4 62.5 all-gather.13
  267.4 135.4 reduce-scatter.5
  409.6 134.5 reduce-scatter.7
  550.0 134.7 reduce-scatter.3
  688.7 62.6 all-gather.19
  755.3 62.4 all-gather.23
  821.7 62.5 all-gather.15
  888.0 62.9 all-gather.21
  954.9 62.5 all-gather.25
  1021.1 62.5 all-gather.17
where the time goes:
time: 1110 us; the launch traced here: 1100 us
  waiting for transfers between devices  461 us (42%)
  matrix products  331 us (30%)
  local copies, waits for them, and re-layouts  128 us (12%)
  other arithmetic  110 us (10%)
  blocking collectives  40.6 us (4%)
  between operations  18.4 us (2%)
    reduce_scatter x1, waiting for transfers between devices, shards(): lax.psum_scatter(grad_attend, ('seq', 'dp'), scatter_dimension=0, tiled=T...  139 us
    all_gather x1, waiting for transfers between devices, shards(): lax.all_gather(expand_rows.astype(jnp.bfloat16), ('seq', 'dp'), axis=0, t...  64.8 us
    all_gather x1, waiting for transfers between devices, shards(): lax.all_gather(shrink_rows.astype(jnp.bfloat16), ('seq', 'dp'), axis=0, t...  61.2 us
    all_gather x1, waiting for transfers between devices, shards(): lax.all_gather(attend_rows.astype(jnp.bfloat16), ('seq', 'dp'), axis=0, t...  60.7 us
    all_gather x1, waiting for transfers between devices, shards(): lax.all_gather(left_apply(attend_rootleft, whole_attend).astype(jnp.bfloa...  59.4 us
    all_gather x1, waiting for transfers between devices, shards(): lax.all_gather(attend_weight.astype(jnp.bfloat16), ('seq', 'dp'), axis=2,...  54.8 us
    slice x27, local copies, waits for them, and re-layouts, split_heads(): tensor[..., group_index * group_width:(group_index + 1) * group_width]  48.9 us
    dot_general x6, matrix products, shards(): jnp.einsum('tqhe,tkhe->thqk', upstream_group, values_group, preferred_ele...  48.3 us
  transfers between devices with their start and end apart: 16, of which 8 were waited for; matrix products, arithmetic and copies ran while one was open for 48% of the time, Pallas kernels for 0%

commit v1 on v0

v1 whole, which is shorter than its diff:
```python
import functools
import math

import jax
import jax.numpy as jnp
from jax import lax
from jax.experimental import pallas as pl
from jax.experimental.pallas import tpu as pltpu
from jax.sharding import PartitionSpec as P

HEAD = 64
WIN = 128
PAIR = 2 * HEAD
KEYS = 3 * WIN
VMEM_BYTES = 56 * 1024 * 1024

EPSILON = 1e-05
STAT_EPSILON = 1e-06
MATRIX_RATE = 0.5
VECTOR_RATE = 0.3
MOMENTUM = 0.9
MASKED = -1e30

TAIL_SLOPE = 0.372
TAIL_POLY = (
    0.14840650094319077,
    0.14841262582366468,
    0.1276493296855659,
    0.0898105241362328,
    0.013338554384341726,
    0.06117535709592349,
    -0.19401880881817585,
    0.1376568075417028,
    -0.0324309766125075,
)


def nt(left_rows, right_rows):
    return lax.dot_general(
        left_rows, right_rows, (((1,), (1,)), ((), ())), preferred_element_type=jnp.float32
    )


def nn(left_rows, right_cols):
    return jnp.dot(left_rows, right_cols, preferred_element_type=jnp.float32)


def across(left_rows, right_rows):
    return lax.dot_general(
        left_rows, right_rows, (((0,), (0,)), ((), ())), preferred_element_type=jnp.float32
    )


def low(values):
    return values.astype(jnp.bfloat16)


def normalize(values, gain_row, bias_row):
    centre = values - jnp.mean(values, axis=-1, keepdims=True)
    spread = jnp.mean(centre * centre, axis=-1, keepdims=True)
    return centre * lax.rsqrt(spread + EPSILON) * gain_row + bias_row


def params():
    return pltpu.CompilerParams(vmem_limit_bytes=VMEM_BYTES)


def write_mask(bias_ref, length, base, blocks):
    for i in range(blocks):
        key = lax.broadcasted_iota(jnp.int32, (KEYS, WIN), 0)
        query = lax.broadcasted_iota(jnp.int32, (KEYS, WIN), 1)
        place = key + (base + (i - 1) * WIN)
        near = (key >= query) & (key <= query + 2 * WIN)
        seen = ((place >= 0) & (place < length)) | (key == query + WIN)
        bias_ref[i] = jnp.where(near & seen, 0.0, MASKED)


def stacked(rows, scale):
    lane = lax.broadcasted_iota(jnp.int32, rows.shape, 1)
    rows = rows.astype(jnp.float32) * scale
    first = jnp.where(lane < HEAD, rows, 0.0)
    second = jnp.where(lane < HEAD, 0.0, rows)
    return low(jnp.concatenate([first, second], axis=0))


def unstacked(turned):
    pair = jnp.concatenate([turned[:HEAD, :WIN], turned[HEAD:, WIN:]], axis=0)
    return pair.T


def attend_forward(blocks, lengths, base, q_ref, k_ref, v_ref, o_ref, total_ref, bias_ref):
    text = pl.program_id(0)

    @pl.when(pl.program_id(1) == 0)
    def _():
        write_mask(bias_ref, lengths[text], base[0], blocks)

    for i in range(blocks):
        keys = k_ref[0, i * WIN : i * WIN + KEYS, :]
        values = v_ref[0, i * WIN : i * WIN + KEYS, :]
        queries = stacked(q_ref[0, i * WIN : (i + 1) * WIN, :], 0.125)
        bias = bias_ref[i]
        scores = nt(keys, queries) + jnp.concatenate([bias, bias], axis=1)
        peak = jnp.max(scores, axis=0, keepdims=True)
        weights = jnp.exp(scores - peak)
        total = jnp.sum(weights, axis=0, keepdims=True)
        mixed = across(values, low(weights)) * (1.0 / total)
        o_ref[0, i * WIN : (i + 1) * WIN, :] = low(unstacked(mixed))
        log_total = peak + jnp.log(total)
        total_ref[0, 0, 2 * i : 2 * i + 1, :] = log_total[:, :WIN]
        total_ref[0, 0, 2 * i + 1 : 2 * i + 2, :] = log_total[:, WIN:]


def attend_backward(
    blocks,
    lengths,
    base,
    q_ref,
    k_ref,
    v_ref,
    up_ref,
    total_ref,
    dq_ref,
    dk_ref,
    dv_ref,
    bias_ref,
    dk_sum,
    dv_sum,
):
    text = pl.program_id(0)

    @pl.when(pl.program_id(1) == 0)
    def _():
        write_mask(bias_ref, lengths[text], base[0], blocks)

    dk_sum[...] = jnp.zeros_like(dk_sum)
    dv_sum[...] = jnp.zeros_like(dv_sum)
    for i in range(blocks):
        window = slice(i * WIN, i * WIN + KEYS)
        own = slice(i * WIN, (i + 1) * WIN)
        keys = k_ref[0, window, :]
        values = v_ref[0, window, :]
        queries = stacked(q_ref[0, own, :], 0.125)
        upstream = stacked(up_ref[0, own, :], 1.0)
        bias = bias_ref[i]
        log_total = jnp.concatenate(
            [total_ref[0, 0, 2 * i : 2 * i + 1, :], total_ref[0, 0, 2 * i + 1 : 2 * i + 2, :]],
            axis=1,
        )
        scores = nt(keys, queries) + jnp.concatenate([bias, bias], axis=1)
        weights = jnp.exp(scores - log_total)
        weight_grad = nt(values, upstream)
        product = weights * weight_grad
        score_grad = low(product - weights * jnp.sum(product, axis=0, keepdims=True))
        dv_sum[window, :] += nn(low(weights), upstream)
        dk_sum[window, :] += nn(score_grad, queries)
        dq_ref[0, own, :] = low(unstacked(across(keys, score_grad)) * 0.125)
    dk_ref[0] = low(dk_sum[...])
    dv_ref[0] = low(dv_sum[...])


def attention_specs(block_size):
    wide = block_size + 2 * WIN
    blocks = block_size // WIN
    own = pl.BlockSpec((1, block_size, PAIR), lambda t, g: (t, 0, g))
    ext = pl.BlockSpec((1, wide, PAIR), lambda t, g: (t, 0, g))
    sums = pl.BlockSpec((1, 1, 2 * blocks, WIN), lambda t, g: (t, g, 0, 0))
    smem = pl.BlockSpec(memory_space=pltpu.SMEM)
    return wide, blocks, own, ext, sums, smem


def run_forward(lengths, base, query, key_ext, value_ext):
    texts, block_size, width = query.shape
    wide, blocks, own, ext, sums, smem = attention_specs(block_size)
    work = texts * blocks * (width // PAIR)
    return pl.pallas_call(
        functools.partial(attend_forward, blocks),
        grid=(texts, width // PAIR),
        in_specs=[smem, smem, own, ext, ext],
        out_specs=[own, sums],
        out_shape=[
            jax.ShapeDtypeStruct(query.shape, jnp.bfloat16),
            jax.ShapeDtypeStruct((texts, width // PAIR, 2 * blocks, WIN), jnp.float32),
        ],
        scratch_shapes=[pltpu.VMEM((blocks, KEYS, WIN), jnp.float32)],
        compiler_params=params(),
        cost_estimate=pl.CostEstimate(
            flops=work * 4 * KEYS * PAIR * 2 * WIN,
            bytes_accessed=query.size * 2 * 5,
            transcendentals=work * KEYS * 2 * WIN,
        ),
        name="attend_forward",
    )(lengths, base, query, key_ext, value_ext)


def run_backward(lengths, base, query, key_ext, value_ext, upstream, totals):
    texts, block_size, width = query.shape
    wide, blocks, own, ext, sums, smem = attention_specs(block_size)
    work = texts * blocks * (width // PAIR)
    return pl.pallas_call(
        functools.partial(attend_backward, blocks),
        grid=(texts, width // PAIR),
        in_specs=[smem, smem, own, ext, ext, own, sums],
        out_specs=[own, ext, ext],
        out_shape=[
            jax.ShapeDtypeStruct(query.shape, jnp.bfloat16),
            jax.ShapeDtypeStruct(key_ext.shape, jnp.bfloat16),
            jax.ShapeDtypeStruct(key_ext.shape, jnp.bfloat16),
        ],
        scratch_shapes=[
            pltpu.VMEM((blocks, KEYS, WIN), jnp.float32),
            pltpu.VMEM((wide, PAIR), jnp.float32),
            pltpu.VMEM((wide, PAIR), jnp.float32),
        ],
        compiler_params=params(),
        cost_estimate=pl.CostEstimate(
            flops=work * 10 * KEYS * PAIR * 2 * WIN,
            bytes_accessed=query.size * 2 * 10,
            transcendentals=work * KEYS * 2 * WIN,
        ),
        name="attend_backward",
    )(lengths, base, query, key_ext, value_ext, upstream, totals)


GATE_ROWS = 256
GATE_SLAB = 16


def gate_kernel(rows_ref, weight_ref, bias_ref, gate_ref, slope_ref, hidden):
    hidden[...] = nt(rows_ref[...], weight_ref[...])

    def slab(i, carry):
        own = pl.ds(pl.multiple_of(i * GATE_SLAB, GATE_SLAB), GATE_SLAB)
        u = hidden[own, :] + bias_ref[...]
        bell = jnp.exp(-0.5 * (u * u))
        t = 1.0 / (1.0 + TAIL_SLOPE * jnp.abs(u))
        poly = TAIL_POLY[-1] * t + TAIL_POLY[-2]
        for term in TAIL_POLY[-3::-1]:
            poly = poly * t + term
        tail = poly * t * bell
        phi = jnp.where(u < 0.0, tail, 1.0 - tail)
        gate_ref[own, :] = low(u * phi)
        slope_ref[own, :] = low(phi + u * bell * (1.0 / math.sqrt(2.0 * math.pi)))
        return carry

    lax.fori_loop(0, GATE_ROWS // GATE_SLAB, slab, 0, unroll=2)


def run_gate(rows, weight_t, bias):
    tokens, width = rows.shape
    hidden = weight_t.shape[0]
    part = width
    out = jax.ShapeDtypeStruct((tokens, hidden), jnp.bfloat16)
    return pl.pallas_call(
        gate_kernel,
        grid=(hidden // part, tokens // GATE_ROWS),
        in_specs=[
            pl.BlockSpec((GATE_ROWS, width), lambda j, i: (i, 0)),
            pl.BlockSpec((part, width), lambda j, i: (j, 0)),
            pl.BlockSpec((1, part), lambda j, i: (0, j)),
        ],
        out_specs=[pl.BlockSpec((GATE_ROWS, part), lambda j, i: (i, j))] * 2,
        out_shape=[out, out],
        scratch_shapes=[pltpu.VMEM((GATE_ROWS, part), jnp.float32)],
        compiler_params=params(),
        cost_estimate=pl.CostEstimate(
            flops=2 * tokens * width * hidden,
            bytes_accessed=2 * (tokens * width + width * hidden + 2 * tokens * hidden),
            transcendentals=2 * tokens * hidden,
        ),
        name="gate",
    )(rows, weight_t, bias)


def core_swap(blocks):
    count = lax.axis_size("seq")
    return lax.ppermute(blocks, "seq", [(i, i ^ 1) for i in range(count)])


def chip_swap(blocks):
    count = lax.axis_size("seq")
    return lax.ppermute(blocks, "seq", [(i, i ^ 2) for i in range(count)])


def swap(blocks):
    return lax.all_to_all(blocks, "seq", split_axis=0, concat_axis=0, tiled=True)


def spread(block):
    count = lax.axis_size("dp")
    copies = jnp.broadcast_to(block[None], (count,) + block.shape)
    return lax.all_to_all(copies, "dp", split_axis=0, concat_axis=0, tiled=True)


def ordered(index, own, other):
    return jnp.where(index == 0, jnp.stack([own, other]), jnp.stack([other, own]))


def add_low(left, right):
    return low(left.astype(jnp.float32) + right.astype(jnp.float32))


def summed(matrices, core, chip, blocks_of):
    first, second, third, fourth = matrices
    lower = jnp.stack([first, third])
    upper = jnp.stack([second, fourth])
    sent = jnp.where(core == 0, upper, lower)
    kept = jnp.where(core == 0, lower, upper)
    both = add_low(kept, core_swap(sent))
    sent = jnp.where(chip == 0, both[1], both[0])
    kept = jnp.where(chip == 0, both[0], both[1])
    one = add_low(kept, chip_swap(sent))
    got = lax.all_to_all(blocks_of(one), "dp", split_axis=0, concat_axis=0, tiled=True)
    return jnp.sum(got.astype(jnp.float32), axis=0)


def thirds(value):
    high = low(value)
    rest = value - high.astype(jnp.float32)
    middle = low(rest)
    tail = low(rest - middle.astype(jnp.float32))
    return jnp.stack([high, middle, tail])


def finish(direction, moment, weight, row_count):
    new_moment = MOMENTUM * moment + direction
    new_weight = weight - MATRIX_RATE / math.sqrt(row_count) * new_moment
    return (new_moment, new_weight)


def shards(
    characters,
    cotangent,
    lengths,
    vectors,
    vector_acc,
    attend_weight,
    attend_moment,
    attend_left,
    attend_right,
    attend_rootleft,
    attend_rootright,
    expand_weight,
    expand_moment,
    expand_left,
    expand_right,
    expand_rootleft,
    expand_rootright,
    shrink_weight,
    shrink_moment,
    shrink_left,
    shrink_right,
    shrink_rootleft,
    shrink_rootright,
):
    text_count, block_size, model_width = characters.shape
    token_rows = text_count * block_size
    both = ("seq", "dp")
    seq_count = lax.axis_size("seq")
    dp_count = lax.axis_size("dp")
    seq_index = lax.axis_index("seq")
    dp_index = lax.axis_index("dp")
    core = seq_index % 2
    chip = seq_index // 2
    tokens_all = token_rows * seq_count * dp_count
    grad_scale = 1.0 / math.sqrt(tokens_all)
    hidden = expand_weight.shape[1] * seq_count * dp_count
    part = hidden // seq_count
    block = model_width // (seq_count * dp_count)
    hidden_block = hidden // (seq_count * dp_count)
    rows_own = seq_count * block

    attend_t = attend_weight.transpose(1, 2, 0)
    expand_t = expand_weight.T
    shrink_t = shrink_weight.T
    shrink_cut = low(shrink_t).reshape(block, seq_count, part).transpose(1, 0, 2)
    packed = jnp.concatenate(
        [low(attend_t[3]), low(expand_t), shrink_cut.reshape(seq_count * block, part)]
    )
    packed_all = lax.all_gather(packed, both, axis=0)
    over_dp = spread(low(attend_t[:3]))
    over_chip = ordered(chip, over_dp, chip_swap(over_dp))
    over_core = ordered(core, over_chip, core_swap(over_chip))
    qkv_t = over_core.transpose(3, 1, 0, 2, 4, 5).reshape(3 * model_width, model_width)

    ends = seq_count - 1
    before = lax.ppermute(
        characters[:, block_size - WIN :], "seq", [(i, i + 1) for i in range(ends)]
    )
    after = lax.ppermute(characters[:, :WIN], "seq", [(i + 1, i) for i in range(ends)])
    input_ext = jnp.concatenate([before, characters, after], axis=1)
    wide = block_size + 2 * WIN

    gain_one = vectors[0]
    bias_one = vectors[1]
    query_bias = vectors[2]
    value_bias = vectors[3]
    out_bias = vectors[4]
    gain_two = vectors[5]
    bias_two = vectors[6]
    shrink_bias = vectors[7]
    expand_bias = vectors[8:].reshape(1, -1)
    normed_ext = low(normalize(input_ext.astype(jnp.float32), gain_one, bias_one))
    normed_low = normed_ext[:, WIN : WIN + block_size].reshape(token_rows, model_width)
    ext_rows = normed_ext.reshape(text_count * wide, model_width)
    query_low = low(nt(normed_low, qkv_t[:model_width]) + query_bias).reshape(characters.shape)
    key_ext = low(nt(ext_rows, qkv_t[model_width : 2 * model_width])).reshape(
        text_count, wide, model_width
    )
    value_ext = low(nt(ext_rows, qkv_t[2 * model_width :]) + value_bias).reshape(
        text_count, wide, model_width
    )
    base = (seq_index * block_size).astype(jnp.int32).reshape(1)
    attended, totals = run_forward(lengths, base, query_low, key_ext, value_ext)
    attended_low = attended.reshape(token_rows, model_width)

    out_t = packed_all[:, :block].reshape(model_width, model_width)
    expand_all = packed_all[:, block : block + hidden_block].reshape(hidden, model_width)
    shrink_all = (
        packed_all[:, block + hidden_block :]
        .reshape(seq_count * dp_count, seq_count, block, part)
        .transpose(0, 2, 1, 3)
        .reshape(model_width, hidden)
    )
    layer_input = characters.astype(jnp.float32).reshape(token_rows, model_width)
    middle = layer_input + nt(attended_low, out_t) + out_bias
    normed_two_low = low(normalize(middle, gain_two, bias_two))
    gated_low, slope_low = run_gate(normed_two_low, expand_all, expand_bias)
    layer_output = middle + nt(gated_low, shrink_all) + shrink_bias
    layer_output = low(layer_output).reshape(text_count, block_size, model_width)

    upstream = cotangent.reshape(token_rows, model_width)
    upstream_float = upstream.astype(jnp.float32)
    grad_shrink_bias = jnp.sum(upstream_float, axis=0)
    expanded_grad = low(nn(upstream, shrink_all) * slope_low.astype(jnp.float32))
    grad_expand_bias = jnp.sum(expanded_grad.astype(jnp.float32), axis=0)
    normed_two_grad = nn(expanded_grad, expand_all)

    def panel(rows, index):
        return rows[:, index * part : (index + 1) * part]

    def by_owner(one):
        return one.reshape(seq_count, dp_count, block, model_width).transpose(1, 0, 2, 3)

    def in_order(one):
        return one.reshape(dp_count, hidden_block, model_width)

    shrink_own = summed(
        [low(across(panel(gated_low, i), upstream)) for i in range(seq_count)],
        core,
        chip,
        in_order,
    )
    expand_own = summed(
        [low(across(normed_two_low, panel(expanded_grad, i))) for i in range(seq_count)],
        core,
        chip,
        by_owner,
    )
    unused_norm, norm_two_back = jax.vjp(normalize, middle, gain_two, bias_two)
    middle_part, grad_gain_two, grad_bias_two = norm_two_back(normed_two_grad)
    middle_grad = upstream_float + middle_part
    branch_grad = low(middle_grad)
    grad_out_bias = jnp.sum(branch_grad.astype(jnp.float32), axis=0)
    grad_out = low(across(attended_low, branch_grad))
    attended_grad = low(nn(branch_grad, out_t)).reshape(characters.shape)

    query_grad, key_grad, value_grad = run_backward(
        lengths, base, query_low, key_ext, value_ext, attended_grad, totals
    )
    pair_grad = jnp.stack([key_grad, value_grad])
    from_above = lax.ppermute(
        pair_grad[:, :, :WIN], "seq", [(i + 1, i) for i in range(ends)]
    )
    from_below = lax.ppermute(
        pair_grad[:, :, block_size + WIN :], "seq", [(i, i + 1) for i in range(ends)]
    )
    pair_own = pair_grad[:, :, WIN : WIN + block_size]
    pair_low = jnp.concatenate(
        [
            add_low(pair_own[:, :, :WIN], from_below),
            pair_own[:, :, WIN : block_size - WIN],
            add_low(pair_own[:, :, block_size - WIN :], from_above),
        ],
        axis=2,
    ).reshape(2, token_rows, model_width)
    query_rows = query_grad.reshape(token_rows, model_width)
    attend_own = summed(
        [
            low(across(normed_low, query_rows)),
            low(across(normed_low, pair_low[0])),
            low(across(normed_low, pair_low[1])),
            grad_out,
        ],
        core,
        chip,
        by_owner,
    )
    grad_query_bias = jnp.sum(query_rows.astype(jnp.float32), axis=0)
    grad_value_bias = jnp.sum(pair_low[1].astype(jnp.float32), axis=0)
    combined = jnp.concatenate([query_rows, pair_low[0], pair_low[1]], axis=1)
    normed_grad = nn(combined, qkv_t)
    unused_first, norm_one_back = jax.vjp(normalize, layer_input, gain_one, bias_one)
    input_part, grad_gain_one, grad_bias_one = norm_one_back(normed_grad)
    characters_grad = low(middle_grad + input_part).reshape(characters.shape)
    vector_terms = jnp.concatenate(
        [
            jnp.stack(
                [
                    grad_gain_one,
                    grad_bias_one,
                    grad_query_bias,
                    grad_value_bias,
                    grad_out_bias,
                    grad_gain_two,
                    grad_bias_two,
                    grad_shrink_bias,
                ]
            ),
            grad_expand_bias.reshape(-1, model_width),
        ],
        axis=0,
    )
    vector_sum = jnp.sum(lax.all_gather(vector_terms, both, axis=0), axis=0)
    vector_grad = vector_sum * grad_scale
    vector_newacc = vector_acc + vector_grad * vector_grad
    vector_new = vectors - VECTOR_RATE * vector_grad / (jnp.sqrt(vector_newacc) + 1e-08)

    expand_rt = low(expand_rootright.T).reshape(hidden_block, seq_count, part).transpose(1, 0, 2)
    shrink_lt = low(shrink_rootleft).reshape(hidden_block, seq_count, part).transpose(1, 0, 2)
    attend_lt = low(attend_rootleft).transpose(1, 0, 2)
    attend_rt = low(attend_rootright.transpose(1, 2, 0))
    roots = swap(jnp.concatenate([expand_rt, shrink_lt, attend_lt, attend_rt], axis=1))
    cut = 2 * hidden_block
    expand_rc = roots[:, :hidden_block].reshape(seq_count * hidden_block, part)
    shrink_lr = roots[:, hidden_block:cut].reshape(seq_count * hidden_block, part)
    attend_rc = roots[:, cut + block :].reshape(rows_own, model_width)
    attend_lw = lax.all_gather(
        roots[:, cut : cut + block], "dp", axis=1, tiled=True
    ).reshape(model_width, model_width)
    small = lax.all_gather(
        jnp.stack([low(expand_rootleft), low(shrink_rootright.T)]), both, axis=1, tiled=True
    )
    expand_lw = small[0]
    shrink_rt = small[1]

    shrink_own_low = low(shrink_own)
    expand_own_low = low(expand_own)
    panels = lax.all_gather(jnp.stack([shrink_own_low, expand_own_low.reshape(rows_own, part)]), "dp", axis=0)
    shrink_panel = panels[:, 0].reshape(part, model_width)
    shrink_sum = jnp.sum(jnp.square(shrink_panel.astype(jnp.float32)))
    expand_panel = (
        panels[:, 1]
        .reshape(dp_count, seq_count, block, part)
        .transpose(1, 0, 2, 3)
        .reshape(model_width, part)
    )
    expand_sum = jnp.sum(jnp.square(expand_panel.astype(jnp.float32)))
    expand_cols = lax.dynamic_slice_in_dim(expand_panel, dp_index * hidden_block, hidden_block, 1).T
    sums = jnp.broadcast_to(
        jnp.concatenate([thirds(shrink_sum), thirds(expand_sum), jnp.zeros((10,), jnp.bfloat16)])[
            :, None
        ],
        (16, model_width),
    )
    mixed = lax.all_gather(jnp.concatenate([shrink_own_low, expand_cols, sums]), "seq", axis=0)
    shrink_rows = mixed[:, :hidden_block].reshape(seq_count * hidden_block, model_width)
    expand_colset = mixed[:, hidden_block:cut].reshape(seq_count * hidden_block, model_width)
    totals = jnp.sum(mixed[:, cut : cut + 6, 0].astype(jnp.float32), axis=0)
    count_all = model_width * hidden
    square_scale = grad_scale * grad_scale
    shrink_square = jnp.sum(totals[:3]) * square_scale / count_all + STAT_EPSILON
    expand_square = jnp.sum(totals[3:]) * square_scale / count_all + STAT_EPSILON

    def col_set(panel):
        picked = lax.dynamic_slice_in_dim(
            panel.reshape(panel.shape[0], seq_count, dp_count, block), dp_index, 1, 2
        )
        return picked.reshape(panel.shape[0], rows_own)

    shrink_left_new = nt(shrink_rows, shrink_panel).reshape(seq_count, hidden_block, part)
    shrink_right_new = across(col_set(shrink_panel), shrink_panel).reshape(
        seq_count, block, model_width
    )
    shrink_applied = nn(shrink_lr, shrink_panel).reshape(seq_count, hidden_block, model_width)
    expand_right_new = nn(expand_colset, expand_panel).reshape(seq_count, hidden_block, part)
    expand_left_new = nt(expand_own_low.reshape(rows_own, part), expand_panel).reshape(
        seq_count, block, model_width
    )
    expand_applied = nt(expand_rc, expand_panel).reshape(seq_count, hidden_block, model_width)
    back = swap(
        jnp.concatenate(
            [
                low(shrink_left_new),
                low(shrink_applied),
                low(expand_right_new),
                low(expand_applied),
                low(shrink_right_new),
                low(expand_left_new),
                expand_own_low,
            ],
            axis=1,
        )
    )
    parts = []
    start = 0
    for width in [hidden_block] * 4 + [block] * 3:
        parts.append(back[:, start : start + width])
        start += width

    def unfold(blocks):
        return blocks.transpose(1, 0, 2).reshape(blocks.shape[1], -1)

    def total(blocks):
        return jnp.sum(blocks.astype(jnp.float32), axis=0)

    shrink_scale = square_scale / shrink_square
    expand_scale = square_scale / expand_square
    shrink_newleft = 0.5 * shrink_left + unfold(parts[0]).astype(jnp.float32) * (
        0.5 * shrink_scale / model_width
    )
    shrink_newright_t = 0.5 * shrink_right.T + total(parts[4]) * (0.5 * shrink_scale / hidden)
    expand_newright_t = 0.5 * expand_right.T + unfold(parts[2]).astype(jnp.float32) * (
        0.5 * expand_scale / model_width
    )
    expand_newleft = 0.5 * expand_left + total(parts[5]) * (0.5 * expand_scale / hidden)
    expand_rows = unfold(parts[6]).astype(jnp.float32) * grad_scale
    expand_direction_t = nt(low(total(parts[3])), expand_lw) * (
        grad_scale * lax.rsqrt(expand_square)
    )
    shrink_turned = nt(shrink_rt, low(total(parts[1])))
    shrink_direction_t = (
        lax.all_to_all(
            low(shrink_turned).reshape(seq_count * dp_count, block, hidden_block),
            both,
            split_axis=0,
            concat_axis=0,
            tiled=True,
        )
        .transpose(1, 0, 2)
        .reshape(block, hidden)
        .astype(jnp.float32)
    ) * (grad_scale * lax.rsqrt(shrink_square))
    expand_newmoment_t, expand_newweight_t = finish(
        expand_direction_t, expand_moment.T, expand_t, model_width
    )
    shrink_newmoment_t, shrink_newweight_t = finish(
        shrink_direction_t, shrink_moment.T, shrink_t, hidden
    )

    attend_own_low = low(attend_own)
    whole = (
        spread(attend_own_low).transpose(1, 0, 2, 3).reshape(model_width, model_width)
    )
    attend_square = (
        jnp.mean(jnp.square(whole.astype(jnp.float32))) * square_scale + STAT_EPSILON
    )
    gram_scale = 0.5 * square_scale / attend_square / model_width
    attend_left_new = nt(attend_own_low.reshape(rows_own, model_width), whole) * gram_scale
    attend_right_new = across(col_set(whole), whole) * gram_scale
    attend_turned = nt(low(nt(attend_rc, whole)), attend_lw) * (
        grad_scale * lax.rsqrt(attend_square)
    )
    returned = swap(
        jnp.concatenate(
            [
                low(attend_left_new).reshape(seq_count, block, model_width),
                low(attend_right_new).reshape(seq_count, block, model_width),
                low(attend_turned).reshape(seq_count, block, model_width),
                attend_own_low,
            ],
            axis=1,
        )
    ).astype(jnp.float32)
    attend_newleft = 0.5 * attend_left + returned[:, :block].transpose(1, 0, 2)
    attend_newright_t = 0.5 * attend_right.transpose(1, 2, 0) + returned[:, block : 2 * block]
    attend_direction_t = returned[:, 2 * block : 3 * block]
    attend_rows = returned[:, 3 * block :].transpose(1, 0, 2) * grad_scale
    attend_newmoment_t, attend_newweight_t = finish(
        attend_direction_t, attend_moment.transpose(1, 2, 0), attend_t, model_width
    )
    shrink_grad = shrink_own * grad_scale
    return (
        layer_output,
        characters_grad,
        attend_rows,
        attend_newmoment_t.transpose(2, 0, 1),
        attend_newweight_t.transpose(2, 0, 1),
        attend_newleft,
        attend_newright_t.transpose(2, 0, 1),
        expand_rows,
        expand_newmoment_t.T,
        expand_newweight_t.T,
        expand_newleft,
        expand_newright_t.T,
        shrink_grad,
        shrink_newmoment_t.T,
        shrink_newweight_t.T,
        shrink_newleft,
        shrink_newright_t.T,
        vector_grad,
        vector_newacc,
        vector_new,
    )


def solution(mesh):
    return jax.shard_map(
        shards,
        mesh=mesh,
        in_specs=(
            P("dp", "seq", None),
            P("dp", "seq", None),
            P("dp"),
            P(),
            P(),
            P(None, None, ("seq", "dp")),
            P(None, None, ("seq", "dp")),
            P(("seq", "dp"), None, None),
            P(None, None, ("seq", "dp")),
            P(("seq", "dp"), None, None),
            P(None, None, ("seq", "dp")),
            P(None, ("seq", "dp")),
            P(None, ("seq", "dp")),
            P(("seq", "dp"), None),
            P(None, ("seq", "dp")),
            P(("seq", "dp"), None),
            P(None, ("seq", "dp")),
            P(None, ("seq", "dp")),
            P(None, ("seq", "dp")),
            P(("seq", "dp"), None),
            P(None, ("seq", "dp")),
            P(("seq", "dp"), None),
            P(None, ("seq", "dp")),
        ),
        out_specs=(
            P("dp", "seq", None),
            P("dp", "seq", None),
            P(("seq", "dp"), None, None),
            P(None, None, ("seq", "dp")),
            P(None, None, ("seq", "dp")),
            P(("seq", "dp"), None, None),
            P(None, None, ("seq", "dp")),
            P(("seq", "dp"), None),
            P(None, ("seq", "dp")),
            P(None, ("seq", "dp")),
            P(("seq", "dp"), None),
            P(None, ("seq", "dp")),
            P(("seq", "dp"), None),
            P(None, ("seq", "dp")),
            P(None, ("seq", "dp")),
            P(("seq", "dp"), None),
            P(None, ("seq", "dp")),
            P(),
            P(),
            P(),
        ),
        check_vma=False,
    )
```

time: 1110 us -> 608 us (0.55)
  waiting for transfers between devices: 461 us -> 158 us
  matrix products: 331 us -> 94.5 us
  Pallas kernels: 0 us -> 74.2 us
  local copies, waits for them, and re-layouts: 128 us -> 81.4 us
  starting transfers between devices: 9.81 us -> 48.8 us
  other arithmetic: 110 us -> 87.3 us
    all_gather x9 -> x6, waiting for transfers between devices: 314 us -> 5.74 us  [the longest x1 3.65 us: shards(): lax.all_gather(jnp.stack([shrink_own_low, expand_own_low.reshape(rows_own...]
    dot_general x56 -> x18, matrix products: 303 us -> 67.5 us  [the longest x12 34.7 us: nt(): lax.dot_general(left_rows, right_rows, (((1,), (1,)), ((), ())), preferre...]
    reduce_scatter x3 -> x0, waiting for transfers between devices: 146 us -> none  [the longest x1 139 us: shards(): lax.psum_scatter(grad_attend, ('seq', 'dp'), scatter_dimension=0, tiled=T...]
    all_to_all x0 -> x8, waiting for transfers between devices: none -> 91.3 us  [the longest x3 35.2 us: swap(): lax.all_to_all(blocks, 'seq', split_axis=0, concat_axis=0, tiled=True)]
    pallas_call x0 -> x3, Pallas kernels: none -> 74.2 us  [the longest x1 27.1 us: run_gate(): pl.pallas_call(gate_kernel, grid=(hidden // part, tokens // GATE_ROWS), i...]
    ppermute x4 -> x12, waiting for transfers between devices: 0.01 us -> 60.4 us  [the longest x4 60.4 us: chip_swap(): return lax.ppermute(blocks, 'seq', [(i, i ^ 2) for i in range(count)])]
    psum x1 -> x0, blocking collectives: 40.6 us -> none  [shards(): vector_sum = lax.psum(vector_terms, ('seq', 'dp'))]
    all_to_all x0 -> x1, blocking collectives: none -> 37.1 us  [spread(): return lax.all_to_all(copies, 'dp', split_axis=0, concat_axis=0, tiled=True)]
  transfers between devices with their start and end apart: 16 -> 26, of which waited for: 8 -> 11; matrix products, arithmetic and copies ran while one was open for 48% -> 36% of each run, Pallas kernels for 0% -> 8%
where the time goes in v1:
time: 608 us; the launch traced here: 602 us
  waiting for transfers between devices  158 us (26%)
  matrix products  94.5 us (16%)
  other arithmetic  87.3 us (14%)
  local copies, waits for them, and re-layouts  81.4 us (13%)
  Pallas kernels  74.2 us (12%)
  starting transfers between devices  48.8 us (8%)
  blocking collectives  37.1 us (6%)
  between operations  20.9 us (3%)
    ppermute x4, waiting for transfers between devices, chip_swap(): return lax.ppermute(blocks, 'seq', [(i, i ^ 2) for i in range(count)])  60.4 us
    all_to_all x1, blocking collectives, spread(): return lax.all_to_all(copies, 'dp', split_axis=0, concat_axis=0, tiled=True)  37.1 us
    all_to_all x3, waiting for transfers between devices, swap(): lax.all_to_all(blocks, 'seq', split_axis=0, concat_axis=0, tiled=True)  35.2 us
    dot_general x12, matrix products, nt(): lax.dot_general(left_rows, right_rows, (((1,), (1,)), ((), ())), preferre...  34.7 us
    dot_general x6, matrix products, nn(): return jnp.dot(left_rows, right_cols, preferred_element_type=jnp.float32)  32.7 us
    all_to_all x1, waiting for transfers between devices, spread(): return lax.all_to_all(copies, 'dp', split_axis=0, concat_axis=0, tiled=True)  28.4 us
    all_to_all x3, waiting for transfers between devices, summed(): lax.all_to_all(blocks_of(one), 'dp', split_axis=0, concat_axis=0, tiled=T...  27.8 us
    pallas_call x1, Pallas kernels, run_gate(): pl.pallas_call(gate_kernel, grid=(hidden // part, tokens // GATE_ROWS), i...  27.1 us
  transfers between devices with their start and end apart: 26, of which 11 were waited for; matrix products, arithmetic and copies ran while one was open for 36% of the time, Pallas kernels for 8%

profile of v1, /device:TPU:0, one launch (start us, length us, event | category | flops | bytes accessed | tf_op | source)
XLA Modules:
  0.0 601.9 jit_solution(311718539834534718)
XLA Ops:
  11.2 37.1 %all_to_all.45 = bf16[8,3,24,768]{3,2,1,0:T(8,128)(2,1)S(1)} all-to-all(bf16[8,3,24,768]{3,2,1,0:T(8,128)(2,1)S(1)} %broadcast_in_dim.14), channel_id=1, replica_groups=mesh['seq'=4,'dp'=8] {'dp'}, dimensions={0} | all-to-all | bytes 1769472 | tf_op jit(solution)/shard_map/all_to_all | solution.py:292
  58.1 20.9 %collective-permute-done.2 = bf16[8,3,24,768]{3,2,0,1:T(8,128)(2,1)} collective-permute-done((bf16[8,3,24,768]{3,2,0,1:T(8,128)(2,1)}, bf16[8,3,24,768]{3,2,0,1:T(8,128)(2,1)}, u32[]{:S(2)}, u32[]{:S(2)}) %collective-permute-start.2) | collective-permute-done | bytes 884768 | tf_op jit(solution)/shard_map/ppermute | solution.py:282
  79.1 3.7 maximum_select_fusion.1
  86.0 3.3 fusion.6
  89.3 4.4 copy.153
  103.0 2.6 add_convert_fusion.7
  105.6 3.6 convolution_convert_fusion
  109.1 3.4 add_convert_fusion.3
  112.6 22.8 %attend_forward.1 = (bf16[2,512,768]{2,1,0:T(8,128)(2,1)}, f32[2,6,8,128]{3,2,1,0:T(8,128)}) custom-call(s32[2]{0:T(128)} %lengths.3, s32[1]{0:T(128)} %bitcast.1.base, bf16[2,512,768]{2,1,0:T(8,128)(2,1)} %bitcast.422, bf16[2,768,768]{2,1,0:T(8,128)(2,1)} %bitcast.415, bf16[2,768,768]{2,1,0:T(8,128)(2,1)} %bitcast.417), custom_call_target="tpu_custom_call" | custom-call | flops 2415919104 | bytes 7864320 | tf_op jit(solution)/shard_map/attend_forward/pallas_call | solution.py:176
  136.7 7.0 %fusion.134 = (bf16[32,96,768]{2,1,0:T(8,128)(2,1)S(1)}, bf16[32,96,768]{2,1,0:T(8,128)(2,1)}) fusion(bf16[32,216,768]{2,1,0:T(8,128)(2,1)} %bitcast.351), kind=kLoop, calls=%fused_computation.250 | loop fusion | bytes 18874368 | tf_op jit(solution)/shard_map/slice | solution.py:420
  143.7 3.0 fusion.140
  148.9 27.1 %gate.1 = (bf16[1024,3072]{1,0:T(8,128)(2,1)}, bf16[1024,3072]{1,0:T(8,128)(2,1)}) custom-call(bf16[1024,768]{1,0:T(8,128)(2,1)} %add_convert_fusion.6.rows_ref, bf16[3072,768]{1,0:T(8,128)(2,1)} %bitcast.372, f32[1,3072]{1,0:T(1,128)} %bitcast.411), custom_call_target="tpu_custom_call" | custom-call | flops 4831838208 | bytes 18874368 | tf_op jit(solution)/shard_map/gate/pallas_call | solution.py:254
  176.1 3.5 fusion.82
  179.6 3.0 fusion.85
  191.2 8.3 %convert_reduce_fusion = (f32[3072]{0:T(1024)}, bf16[1024,3072]{1,0:T(8,128)(2,1)S(1)}) fusion(bf16[1024,3072]{1,0:T(8,128)(2,1)} %get-tuple-element.29, bf16[1024,768]{1,0:T(8,128)(2,1)S(1)} %bitcast.349, bf16[768,3072]{1,0:T(8,128)(2,1)S(1)} %bitcast.368), kind=kOutput, calls=%fused_computation.2 | convolution fusion | flops 4847563776 | bytes 18886656 | tf_op jit(solution)/shard_map/dot_general | solution.py:45
  214.9 21.7 %collective-permute-done.9 = bf16[768,768]{1,0:T(8,128)(2,1)S(1)} collective-permute-done((bf16[768,768]{1,0:T(8,128)(2,1)S(1)}, bf16[768,768]{1,0:T(8,128)(2,1)S(1)}, u32[]{:S(2)}, u32[]{:S(2)}) %collective-permute-start.9) | collective-permute-done | bytes 1179680 | tf_op jit(solution)/shard_map/ppermute | solution.py:282
  238.1 4.3 all-to-all-start.5
  242.4 9.7 %multiply_reduce_fusion = (f32[768]{0:T(1024)S(1)}, f32[1024]{0:T(1024)S(1)}, f32[768]{0:T(1024)S(1)}, f32[1024,768]{1,0:T(8,128)S(1)}) fusion(f32[1024,768]{1,0:T(8,128)} %copy-done.1, f32[1024]{0:T(1024)S(1)} %fusion.125, f32[1024]{0:T(1024)S(1)} %broadcast_multiply_fusion.4, f32[768]{0:T(1024)S(1)} %get-tuple-element.147, ...), kind=kOutput, calls=%fused_computation.44 | convolution fusion | flops 4838126592 | bytes 17323008 | tf_op jit(solution)/shard_map/dot_general | solution.py:45
  254.6 6.5 %collective-permute-done.11 = bf16[768,768]{1,0:T(8,128)(2,1)} collective-permute-done((bf16[768,768]{1,0:T(8,128)(2,1)}, bf16[768,768]{1,0:T(8,128)(2,1)}, u32[]{:S(2)}, u32[]{:S(2)}) %collective-permute-start.11) | collective-permute-done | bytes 1179680 | tf_op jit(solution)/shard_map/ppermute | solution.py:282
  264.0 6.3 %all-to-all-done.5 = bf16[8,96,768]{2,1,0:T(8,128)(2,1)} async-done(((bf16[8,96,768]{2,1,0:T(8,128)(2,1)}), bf16[8,96,768]{2,1,0:T(8,128)(2,1)}, u32[]{:S(2)}, u32[]{:S(2)}) %all-to-all-start.5) | async-done | bytes 1179680 | tf_op jit(solution)/shard_map/all_to_all | solution.py:313
  270.3 4.4 all-to-all-start.6
  274.8 3.0 convert_reduce_fusion.4
  280.3 24.3 %attend_backward.1 = (bf16[2,512,768]{2,1,0:T(8,128)(2,1)}, bf16[2,768,768]{2,1,0:T(8,128)(2,1)}, bf16[2,768,768]{2,1,0:T(8,128)(2,1)}) custom-call(s32[2]{0:T(128)} %lengths.3, s32[1]{0:T(128)} %bitcast.1.base, bf16[2,512,768]{2,1,0:T(8,128)(2,1)} %bitcast.423, bf16[2,768,768]{2,1,0:T(8,128)(2,1)} %bitcast.416, bf16[2,768,768]{2,1,0:T(8,128)(2,1)} %bitcast.418, ...), custom_call_target="tpu_custom_call" | custom-call | flops 6039797760 | bytes 15728640 | tf_op jit(solution)/shard_map/attend_backward/pallas_call | solution.py:200
  304.6 2.7 pad_maximum_fusion.12
  323.3 3.4 fusion.94
  340.1 4.3 all-to-all-start.3
  346.4 17.1 %all-to-all-done.3 = bf16[4,240,768]{2,1,0:T(8,128)(2,1)} async-done(((bf16[4,240,768]{2,1,0:T(8,128)(2,1)}), bf16[4,240,768]{2,1,0:T(8,128)(2,1)}, u32[]{:S(2)}, u32[]{:S(2)}) %all-to-all-start.3) | async-done | bytes 1474592 | tf_op jit(solution)/shard_map/all_to_all | solution.py:286
  365.4 3.7 maximum_select_fusion
  375.3 3.7 all-gather.18.cloned.1.call-done
  378.9 2.8 fusion.137
  389.6 11.3 %collective-permute-done.7 = bf16[768,768]{1,0:T(8,128)(2,1)} collective-permute-done((bf16[768,768]{1,0:T(8,128)(2,1)}, bf16[768,768]{1,0:T(8,128)(2,1)}, u32[]{:S(2)}, u32[]{:S(2)}) %collective-permute-start.7) | collective-permute-done | bytes 1179680 | tf_op jit(solution)/shard_map/ppermute | solution.py:282
  404.5 5.9 all-to-all-start.1
  410.5 7.0 %fusion.131 = (f32[768]{0:T(1024)S(1)}, f32[1024]{0:T(1024)S(1)}, f32[1024,768]{1,0:T(8,128)S(1)}) fusion(f32[768]{0:T(1024)S(1)} %copy-done.65, f32[1024]{0:T(1024)S(1)} %bitcast.407, bf16[2,512,768]{2,1,0:T(8,128)(2,1)S(1)} %copy-done, bf16[2304,768]{1,0:T(8,128)(2,1)} %bitcast.374, bf16[1024,768]{1,0:T(8,128)(2,1)} %bitcast.390, ...), kind=kOutput, calls=%fused_computation.248 | convolution fusion | flops 3642751232 | bytes 12990464 | tf_op jit(solution)/shard_map/dot_general | solution.py:45
  422.2 21.5 %all-to-all-done.1 = bf16[8,4,24,768]{3,2,1,0:T(8,128)(2,1)S(1)} async-done(((bf16[8,4,24,768]{3,2,1,0:T(8,128)(2,1)}), bf16[8,4,24,768]{3,2,1,0:T(8,128)(2,1)S(1)}, u32[]{:S(2)}, u32[]{:S(2)}) %all-to-all-start.1) | async-done | bytes 1179680 | tf_op jit(solution)/shard_map/all_to_all | solution.py:313
  445.0 3.6 all-to-all-start.2
  449.5 28.4 %all-to-all-done.2 = bf16[8,4,24,768]{3,2,1,0:T(8,128)(2,1)S(1)} async-done(((bf16[8,4,24,768]{3,2,1,0:T(8,128)(2,1)}), bf16[8,4,24,768]{3,2,1,0:T(8,128)(2,1)S(1)}, u32[]{:S(2)}, u32[]{:S(2)}) %all-to-all-start.2) | async-done | bytes 1179680 | tf_op jit(solution)/shard_map/all_to_all | solution.py:292
  481.2 11.3 %reshape_reshape.3 = bf16[768,4,8,24]{3,2,1,0:T(8,128)(2,1)} reshape(bf16[4,8,24,768]{3,2,1,0:T(8,128)(2,1)S(1)} %bitcast.333) | data formatting | bytes 2359296 | tf_op jit(solution)/shard_map/reshape;reshape | solution.py:577
  492.5 5.5 constant_dynamic-slice_fusion
  498.1 3.3 copy.158
  507.0 3.5 all-to-all-start.4
  512.4 3.8 reshape_reshape_squeeze.3
  518.8 2.6 fusion.97
  523.9 2.6 fusion.95
  530.3 5.0 all-to-all-start.7
  535.3 10.1 %add_convert_fusion.5 = bf16[1024,768]{1,0:T(8,128)(2,1)} fusion(f32[1024,768]{1,0:T(8,128)} %copy-done.1, bf16[1024,3072]{1,0:T(8,128)(2,1)} %get-tuple-element.28, bf16[768,3072]{1,0:T(8,128)(2,1)} %bitcast.369, f32[768]{0:T(1024)S(1)} %copy-done.68), kind=kOutput, calls=%fused_computation.51 | convolution fusion | flops 4834197504 | bytes 15731712 | tf_op jit(solution)/shard_map/dot_general | solution.py:39
  545.5 2.6 add_convert_fusion.4
  556.9 18.0 %all-to-all-done.7 = bf16[4,456,768]{2,1,0:T(8,128)(2,1)} async-done(((bf16[4,456,768]{2,1,0:T(8,128)(2,1)}), bf16[4,456,768]{2,1,0:T(8,128)(2,1)}, u32[]{:S(2)}, u32[]{:S(2)}) %all-to-all-start.7) | async-done | bytes 2801696 | tf_op jit(solution)/shard_map/all_to_all | solution.py:286
  581.1 3.5 all-to-all-start.8
  (341 shorter events, 160.0 us)
Async XLA Ops:
  7.2 128.1 %all-gather.16.cloned.1.call-start = ((), (), s32[]{:S(2)}) async-start(), calls=%async_computation.11 | async-start | bytes 10948608 | tf_op jit(solution)/shard_map/all_gather | solution.py:380
  11.1 39.6 %copy-start = (bf16[2,512,768]{2,1,0:T(8,128)(2,1)S(1)}, bf16[2,512,768]{2,1,0:T(8,128)(2,1)}, u32[]{:S(2)}) copy-start(bf16[2,512,768]{2,1,0:T(8,128)(2,1)} %param.23) | copy-start | bytes 4718596
  49.2 29.8 %collective-permute-start.2 = (bf16[8,3,24,768]{3,2,0,1:T(8,128)(2,1)}, bf16[8,3,24,768]{3,2,0,1:T(8,128)(2,1)}, u32[]{:S(2)}, u32[]{:S(2)}) collective-permute-start(bf16[8,3,24,768]{3,2,0,1:T(8,128)(2,1)} %copy.207), channel_id=1, source_target_pairs={{0,16},{8,24},{16,0},{24,8},{1,17},{9,25},{17,1},{25,9},{2,18},{10... | collective-permute-start | bytes 2654216 | tf_op jit(solution)/shard_map/ppermute | solution.py:282
  52.5 30.3 %collective-permute-start = (bf16[2,128,768]{1,2,0:T(8,128)(2,1)}, bf16[2,128,768]{1,2,0:T(8,128)(2,1)S(1)}, u32[]{:S(2)}, u32[]{:S(2)}) collective-permute-start(bf16[2,128,768]{1,2,0:T(8,128)(2,1)} %get-tuple-element.180), channel_id=1, source_target_pairs={{0,8},{8,16},{16,24},{1,9},{9,17},{17,25},{2,10},{10,18},{18,26},{... | collective-permute-start | bytes 1179656 | tf_op jit(solution)/shard_map/ppermute | solution.py:387
  53.8 29.0 %collective-permute-start.1 = (bf16[2,128,768]{1,2,0:T(8,128)(2,1)}, bf16[2,128,768]{1,2,0:T(8,128)(2,1)}, u32[]{:S(2)}, u32[]{:S(2)}) collective-permute-start(bf16[2,128,768]{1,2,0:T(8,128)(2,1)} %get-tuple-element.181), channel_id=1, source_target_pairs={{8,0},{16,8},{24,16},{9,1},{17,9},{25,17},{10,2},{18,10},{26,18},{... | collective-permute-start | bytes 1179656 | tf_op jit(solution)/shard_map/ppermute | solution.py:390
  58.1 27.9 %copy-start.64 = (f32[768]{0:T(1024)}, f32[768]{0:T(1024)S(1)}, u32[]{:S(2)}) copy-start(f32[768]{0:T(1024)S(1)} %get-tuple-element.152) | copy-start | bytes 9220
  82.8 16.5 %collective-permute-start.3 = (bf16[2,8,3,24,768]{4,3,1,0,2:T(8,128)(2,1)}, bf16[2,8,3,24,768]{4,3,1,0,2:T(8,128)(2,1)}, u32[]{:S(2)}, u32[]{:S(2)}) collective-permute-start(bf16[2,8,3,24,768]{4,3,1,0,2:T(8,128)(2,1)} %maximum_select_fusion.1), channel_id=1, source_target_pairs={{0,8},{8,0},{16,24},{24,16},{1,9},{9,1},{17,25},{25,17},{2,10},{10... | collective-permute-start | bytes 5308424 | tf_op jit(solution)/shard_map/ppermute | solution.py:277
  136.7 7.0 %copy-start.45 = (bf16[32,24,768]{2,1,0:T(8,128)(2,1)}, bf16[32,24,768]{2,1,0:T(8,128)(2,1)S(1)}, u32[]{:S(2)}) copy-start(bf16[32,24,768]{2,1,0:T(8,128)(2,1)S(1)} %slice.297) | copy-start | bytes 3538948
  176.1 6.5 %slice-start.1 = ((s8[6291456]{0:T(1024)(128)(4,1)}), s8[4194304]{0:T(1024)(128)(4,1)S(1)}, s32[]{:S(2)}) async-start(s8[6291456]{0:T(1024)(128)(4,1)} %bitcast.425), calls=%async_computation.16 | async-start | bytes 8388608
  189.5 17.0 %collective-permute-start.8 = (bf16[2,768,768]{2,1,0:T(8,128)(2,1)S(1)}, bf16[2,768,768]{2,1,0:T(8,128)(2,1)S(1)}, u32[]{:S(2)}, u32[]{:S(2)}) collective-permute-start(bf16[2,768,768]{2,1,0:T(8,128)(2,1)S(1)} %broadcast_select_fusion.1), channel_id=1, source_target_pairs={{0,8},{8,0},{16,24},{24,16},{1,9},{9,1},{17,25},{25,17},{2,10},{10... | collective-permute-start | bytes 7077896 | tf_op jit(solution)/shard_map/ppermute | solution.py:277
  191.2 8.3 %copy-start.39 = (bf16[1024,768]{1,0:T(8,128)(2,1)S(1)}, bf16[1024,768]{1,0:T(8,128)(2,1)}, u32[]{:S(2)}) copy-start(bf16[1024,768]{1,0:T(8,128)(2,1)} %add_convert_fusion.6.rows_ref) | copy-start | bytes 4718596
  205.8 5.8 collective-permute-start.10
  207.7 28.9 %collective-permute-start.9 = (bf16[768,768]{1,0:T(8,128)(2,1)S(1)}, bf16[768,768]{1,0:T(8,128)(2,1)S(1)}, u32[]{:S(2)}, u32[]{:S(2)}) collective-permute-start(bf16[768,768]{1,0:T(8,128)(2,1)S(1)} %select_bitcast_fusion.1), channel_id=1, source_target_pairs={{0,16},{8,24},{16,0},{24,8},{1,17},{9,25},{17,1},{25,9},{2,18},{10... | collective-permute-start | bytes 3538952 | tf_op jit(solution)/shard_map/ppermute | solution.py:282
  212.6 25.5 %copy-start.7 = (bf16[2,768,768]{2,1,0:T(8,128)(2,1)}, bf16[2,768,768]{2,1,0:T(8,128)(2,1)S(1)}, u32[]{:S(2)}) copy-start(bf16[2,768,768]{2,1,0:T(8,128)(2,1)S(1)} %add_convert_fusion) | copy-start | bytes 7077892
  213.9 47.2 %collective-permute-start.11 = (bf16[768,768]{1,0:T(8,128)(2,1)}, bf16[768,768]{1,0:T(8,128)(2,1)}, u32[]{:S(2)}, u32[]{:S(2)}) collective-permute-start(bf16[768,768]{1,0:T(8,128)(2,1)} %select_bitcast_fusion), channel_id=1, source_target_pairs={{0,16},{8,24},{16,0},{24,8},{1,17},{9,25},{17,1},{25,9},{2,18},{10... | collective-permute-start | bytes 3538952 | tf_op jit(solution)/shard_map/ppermute | solution.py:282
  238.1 32.1 %all-to-all-start.5 = ((bf16[8,96,768]{2,1,0:T(8,128)(2,1)}), bf16[8,96,768]{2,1,0:T(8,128)(2,1)}, u32[]{:S(2)}, u32[]{:S(2)}) async-start(bf16[8,96,768]{2,1,0:T(8,128)(2,1)} %bitcast.363), calls=%async_computation.5 | async-start | bytes 2359296 | tf_op jit(solution)/shard_map/all_to_all | solution.py:313
  242.4 9.7 %copy-start.2 = (f32[1024,768]{1,0:T(8,128)S(1)}, f32[1024,768]{1,0:T(8,128)}, u32[]{:S(2)}) copy-start(f32[1024,768]{1,0:T(8,128)} %copy-done.1) | copy-start | bytes 9437188
  252.1 9.0 %copy-start.8 = (bf16[2,768,768]{2,1,0:T(8,128)(2,1)S(1)}, bf16[2,768,768]{2,1,0:T(8,128)(2,1)}, u32[]{:S(2)}) copy-start(bf16[2,768,768]{2,1,0:T(8,128)(2,1)} %copy-done.7) | copy-start | bytes 7077892
  270.3 47.0 %all-to-all-start.6 = ((bf16[8,4,24,768]{3,2,1,0:T(8,128)(2,1)}), bf16[8,4,24,768]{3,2,1,0:T(8,128)(2,1)}, u32[]{:S(2)}, u32[]{:S(2)}) async-start(bf16[8,4,24,768]{3,2,1,0:T(8,128)(2,1)} %bitcast.371), calls=%async_computation.6 | async-start | bytes 2359296 | tf_op jit(solution)/shard_map/all_to_all | solution.py:313
  274.7 104.2 %all-gather.18.cloned.1.call-start = ((), (), s32[]{:S(2)}) async-start(), calls=%async_computation.12 | async-start | bytes 2654208 | tf_op jit(solution)/shard_map/all_gather | solution.py:549
  304.6 6.2 %copy-start.70 = (bf16[2,512,768]{2,1,0:T(8,128)(2,1)S(1)}, bf16[2,512,768]{2,1,0:T(8,128)(2,1)}, u32[]{:S(2)}) copy-start(bf16[2,512,768]{2,1,0:T(8,128)(2,1)} %get-tuple-element.27) | copy-start | bytes 4718596
  307.4 19.5 %collective-permute-start.4 = (bf16[2,2,128,768]{3,2,1,0:T(8,128)(2,1)}, bf16[2,2,128,768]{3,2,1,0:T(8,128)(2,1)}, u32[]{:S(2)}, u32[]{:S(2)}) collective-permute-start(bf16[2,2,128,768]{3,2,1,0:T(8,128)(2,1)} %get-tuple-element.166), channel_id=1, source_target_pairs={{0,8},{8,16},{16,24},{1,9},{9,17},{17,25},{2,10},{10,18},{18,26},{... | collective-permute-start | bytes 2359304 | tf_op jit(solution)/shard_map/ppermute | solution.py:475
  309.6 17.3 %collective-permute-start.5 = (bf16[2,2,128,768]{3,2,1,0:T(8,128)(2,1)}, bf16[2,2,128,768]{3,2,1,0:T(8,128)(2,1)}, u32[]{:S(2)}, u32[]{:S(2)}) collective-permute-start(bf16[2,2,128,768]{3,2,1,0:T(8,128)(2,1)} %get-tuple-element.167), channel_id=1, source_target_pairs={{8,0},{16,8},{24,16},{9,1},{17,9},{25,17},{10,2},{18,10},{26,18},{... | collective-permute-start | bytes 2359304 | tf_op jit(solution)/shard_map/ppermute | solution.py:472
  326.7 8.0 %copy-start.22 = (bf16[1,768,768]{2,1,0:T(8,128)(2,1)}, bf16[1,768,768]{2,1,0:T(8,128)(2,1)S(1)}, u32[]{:S(2)}) copy-start(bf16[1,768,768]{2,1,0:T(8,128)(2,1)S(1)} %fusion.94) | copy-start | bytes 3538948
  336.9 32.2 %collective-permute-start.6 = (bf16[2,768,768]{2,1,0:T(8,128)(2,1)}, bf16[2,768,768]{2,1,0:T(8,128)(2,1)}, u32[]{:S(2)}, u32[]{:S(2)}) collective-permute-start(bf16[2,768,768]{2,1,0:T(8,128)(2,1)} %broadcast_select_fusion.2), channel_id=1, source_target_pairs={{0,8},{8,0},{16,24},{24,16},{1,9},{9,1},{17,25},{25,17},{2,10},{10... | collective-permute-start | bytes 7077896 | tf_op jit(solution)/shard_map/ppermute | solution.py:277
  340.1 23.4 %all-to-all-start.3 = ((bf16[4,240,768]{2,1,0:T(8,128)(2,1)}), bf16[4,240,768]{2,1,0:T(8,128)(2,1)}, u32[]{:S(2)}, u32[]{:S(2)}) async-start(bf16[4,240,768]{2,1,0:T(8,128)(2,1)} %pad_maximum_fusion.10), calls=%async_computation.3 | async-start | bytes 2949120 | tf_op jit(solution)/shard_map/all_to_all | solution.py:286
  344.5 158.4 %all-gather.12.cloned.1.call-start = ((), (), s32[]{:S(2)}) async-start(), calls=%async_computation.9 | async-start | bytes 1327104 | tf_op jit(solution)/shard_map/all_gather | solution.py:538
  365.3 150.9 %all-gather.20.cloned.1.call-start = ((), (), s32[]{:S(2)}) async-start(), calls=%async_computation.13 | async-start | bytes 1597440 | tf_op jit(solution)/shard_map/all_gather | solution.py:566
  373.5 27.4 %collective-permute-start.7 = (bf16[768,768]{1,0:T(8,128)(2,1)}, bf16[768,768]{1,0:T(8,128)(2,1)}, u32[]{:S(2)}, u32[]{:S(2)}) collective-permute-start(bf16[768,768]{1,0:T(8,128)(2,1)} %select_bitcast_fusion.2), channel_id=1, source_target_pairs={{0,16},{8,24},{16,0},{24,8},{1,17},{9,25},{17,1},{25,9},{2,18},{10... | collective-permute-start | bytes 3538952 | tf_op jit(solution)/shard_map/ppermute | solution.py:282
  381.7 6.8 %copy-start.33 = (bf16[96,768]{0,1:T(8,128)(2,1)S(1)}, bf16[96,768]{0,1:T(8,128)(2,1)}, u32[]{:S(2)}) copy-start(bf16[96,768]{0,1:T(8,128)(2,1)} %copy.163) | copy-start | bytes 442372
  381.8 21.5 %copy-start.18 = (bf16[4,8,24,768]{3,2,1,0:T(8,128)(2,1)}, bf16[4,8,24,768]{3,2,1,0:T(8,128)(2,1)S(1)}, u32[]{:S(2)}) copy-start(bf16[4,8,24,768]{3,2,1,0:T(8,128)(2,1)S(1)} %copy.167) | copy-start | bytes 3538948
  403.4 7.1 %copy-start.65 = (f32[768]{0:T(1024)S(1)}, f32[768]{0:T(1024)}, u32[]{:S(2)}) copy-start(f32[768]{0:T(1024)} %copy-done.64) | copy-start | bytes 9220
  404.5 39.2 %all-to-all-start.1 = ((bf16[8,4,24,768]{3,2,1,0:T(8,128)(2,1)}), bf16[8,4,24,768]{3,2,1,0:T(8,128)(2,1)S(1)}, u32[]{:S(2)}, u32[]{:S(2)}) async-start(bf16[8,4,24,768]{3,2,1,0:T(8,128)(2,1)} %bitcast.370), calls=%async_computation.1 | async-start | bytes 2359296 | tf_op jit(solution)/shard_map/all_to_all | solution.py:313
  410.4 137.7 %all-gather.22.cloned.1.call-start = ((), (), s32[]{:S(2)}) async-start(), calls=%async_computation.14 | async-start | bytes 1622016 | tf_op jit(solution)/shard_map/all_gather | solution.py:524
  422.2 26.7 %copy-start.62 = (f32[768,24]{0,1:T(8,128)S(1)}, f32[768,24]{0,1:T(8,128)}, u32[]{:S(2)}) copy-start(f32[768,24]{0,1:T(8,128)} %param.45) | copy-start | bytes 221188
  422.2 26.7 %copy-start.63 = (f32[24,768]{1,0:T(8,128)S(1)}, f32[24,768]{1,0:T(8,128)}, u32[]{:S(2)}) copy-start(f32[24,768]{1,0:T(8,128)} %param.38) | copy-start | bytes 221188
  445.0 33.0 %all-to-all-start.2 = ((bf16[8,4,24,768]{3,2,1,0:T(8,128)(2,1)}), bf16[8,4,24,768]{3,2,1,0:T(8,128)(2,1)S(1)}, u32[]{:S(2)}, u32[]{:S(2)}) async-start(bf16[8,4,24,768]{3,2,1,0:T(8,128)(2,1)} %broadcast_in_dim.19), calls=%async_computation.2 | async-start | bytes 2359296 | tf_op jit(solution)/shard_map/all_to_all | solution.py:292
  448.5 130.0 %all-gather.14.cloned.1.call-start = ((), (), s32[]{:S(2)}) async-start(), calls=%async_computation.10 | async-start | bytes 2433024 | tf_op jit(solution)/shard_map/all_gather | solution.py:541
  498.1 4.8 copy-start.50
  505.1 5.4 copy-start.17
  507.0 23.3 %all-to-all-start.4 = ((bf16[4,96,768]{2,1,0:T(8,128)(2,1)}), bf16[4,96,768]{2,1,0:T(8,128)(2,1)S(1)}, u32[]{:S(2)}, u32[]{:S(2)}) async-start(bf16[4,96,768]{2,1,0:T(8,128)(2,1)} %pad_maximum_fusion.13), calls=%async_computation.4 | async-start | bytes 1179648 | tf_op jit(solution)/shard_map/all_to_all | solution.py:286
  530.3 5.0 copy-start.68
  530.3 44.7 %all-to-all-start.7 = ((bf16[4,456,768]{2,1,0:T(8,128)(2,1)}), bf16[4,456,768]{2,1,0:T(8,128)(2,1)}, u32[]{:S(2)}, u32[]{:S(2)}) async-start(bf16[4,456,768]{2,1,0:T(8,128)(2,1)} %constant_dynamic-update-slice_fusion), calls=%async_computation.7 | async-start | bytes 5603328 | tf_op jit(solution)/shard_map/all_to_all | solution.py:286
  535.3 10.1 %copy-start.3 = (f32[1024,768]{1,0:T(8,128)S(1)}, f32[1024,768]{1,0:T(8,128)}, u32[]{:S(2)}) copy-start(f32[1024,768]{1,0:T(8,128)} %get-tuple-element.161) | copy-start | bytes 9437188
  535.3 10.1 %copy-start.13 = (bf16[2,512,768]{2,1,0:T(8,128)(2,1)S(1)}, bf16[2,512,768]{2,1,0:T(8,128)(2,1)}, u32[]{:S(2)}) copy-start(bf16[2,512,768]{2,1,0:T(8,128)(2,1)} %param.24) | copy-start | bytes 4718596
  535.3 10.1 %copy-start.15 = (f32[1024,768]{1,0:T(8,128)S(1)}, f32[1024,768]{1,0:T(8,128)}, u32[]{:S(2)}) copy-start(f32[1024,768]{1,0:T(8,128)} %copy-done.14) | copy-start | bytes 9437188
  545.5 4.9 copy-start.29
  581.1 12.2 %all-to-all-start.8 = ((bf16[32,24,96]{2,1,0:T(8,128)(2,1)}), bf16[32,24,96]{2,1,0:T(8,128)(2,1)S(1)}, u32[]{:S(2)}, u32[]{:S(2)}) async-start(bf16[32,24,96]{2,1,0:T(8,128)(2,1)} %bitcast.118), calls=%async_computation.8 | async-start | bytes 393216 | tf_op jit(solution)/shard_map/all_to_all | solution.py:633
  (53 other events, 141.8 us)
Sparse Core Ops, SparseCore 0:
  11.2 106.9 all-gather.15
  323.4 55.4 all-gather.17
  381.8 47.1 all-gather.11
  430.4 22.1 all-gather.19
  455.9 58.5 all-gather.21
  517.8 60.6 all-gather.13

commit v2 on v1

v2 whole, which is shorter than its diff:
```python
import functools
import math

import jax
import jax.numpy as jnp
from jax import lax
from jax.experimental import pallas as pl
from jax.experimental.pallas import tpu as pltpu
from jax.sharding import PartitionSpec as P

HEAD = 64
WIN = 128
PAIR = 2 * HEAD
KEYS = 3 * WIN
VMEM_BYTES = 56 * 1024 * 1024

EPSILON = 1e-05
STAT_EPSILON = 1e-06
MATRIX_RATE = 0.5
VECTOR_RATE = 0.3
MOMENTUM = 0.9
MASKED = -1e30

PHI_POLY = (
    0.7978849414608439,
    0.03633308457157131,
    -3.259497261642231e-05,
    -5.530619510506789e-05,
    3.964744703196676e-06,
    -1.3226336477723372e-07,
    1.7561715138424972e-09,
)


def nt(left_rows, right_rows):
    return lax.dot_general(
        left_rows, right_rows, (((1,), (1,)), ((), ())), preferred_element_type=jnp.float32
    )


def nn(left_rows, right_cols):
    return jnp.dot(left_rows, right_cols, preferred_element_type=jnp.float32)


def across(left_rows, right_rows):
    return lax.dot_general(
        left_rows, right_rows, (((0,), (0,)), ((), ())), preferred_element_type=jnp.float32
    )


def low(values):
    return values.astype(jnp.bfloat16)


def normalize(values, gain_row, bias_row):
    centre = values - jnp.mean(values, axis=-1, keepdims=True)
    spread = jnp.mean(centre * centre, axis=-1, keepdims=True)
    return centre * lax.rsqrt(spread + EPSILON) * gain_row + bias_row


def params():
    return pltpu.CompilerParams(vmem_limit_bytes=VMEM_BYTES)


def write_mask(bias_ref, length, base, blocks):
    for i in range(blocks):
        key = lax.broadcasted_iota(jnp.int32, (KEYS, WIN), 0)
        query = lax.broadcasted_iota(jnp.int32, (KEYS, WIN), 1)
        place = key + (base + (i - 1) * WIN)
        near = (key >= query) & (key <= query + 2 * WIN)
        seen = ((place >= 0) & (place < length)) | (key == query + WIN)
        bias_ref[i] = jnp.where(near & seen, 0.0, MASKED)


def stacked(rows, scale):
    lane = lax.broadcasted_iota(jnp.int32, rows.shape, 1)
    rows = rows.astype(jnp.float32) * scale
    first = jnp.where(lane < HEAD, rows, 0.0)
    second = jnp.where(lane < HEAD, 0.0, rows)
    return low(jnp.concatenate([first, second], axis=0))


def unstacked(turned):
    pair = jnp.concatenate([turned[:HEAD, :WIN], turned[HEAD:, WIN:]], axis=0)
    return pair.T


def attend_forward(blocks, lengths, base, q_ref, k_ref, v_ref, o_ref, total_ref, bias_ref):
    text = pl.program_id(0)

    @pl.when(pl.program_id(1) == 0)
    def _():
        write_mask(bias_ref, lengths[text], base[0], blocks)

    for i in range(blocks):
        keys = k_ref[0, i * WIN : i * WIN + KEYS, :]
        values = v_ref[0, i * WIN : i * WIN + KEYS, :]
        queries = stacked(q_ref[0, i * WIN : (i + 1) * WIN, :], 0.125)
        bias = bias_ref[i]
        scores = nt(keys, queries) + jnp.concatenate([bias, bias], axis=1)
        peak = jnp.max(scores, axis=0, keepdims=True)
        weights = jnp.exp(scores - peak)
        total = jnp.sum(weights, axis=0, keepdims=True)
        mixed = across(values, low(weights)) * (1.0 / total)
        o_ref[0, i * WIN : (i + 1) * WIN, :] = low(unstacked(mixed))
        log_total = peak + jnp.log(total)
        total_ref[0, 0, 2 * i : 2 * i + 1, :] = log_total[:, :WIN]
        total_ref[0, 0, 2 * i + 1 : 2 * i + 2, :] = log_total[:, WIN:]


def attend_backward(
    blocks,
    extra,
    lengths,
    base,
    q_ref,
    k_ref,
    v_ref,
    up_ref,
    total_ref,
    *rest,
):
    dq_ref, dk_ref, dv_ref, bias_ref, dk_sum, dv_sum = rest[extra:]
    text = pl.program_id(0)

    @pl.when(pl.program_id(1) == 0)
    def _():
        write_mask(bias_ref, lengths[text], base[0], blocks)

    dk_sum[...] = jnp.zeros_like(dk_sum)
    dv_sum[...] = jnp.zeros_like(dv_sum)
    for i in range(blocks):
        window = slice(i * WIN, i * WIN + KEYS)
        own = slice(i * WIN, (i + 1) * WIN)
        keys = k_ref[0, window, :]
        values = v_ref[0, window, :]
        queries = stacked(q_ref[0, own, :], 0.125)
        upstream = stacked(up_ref[0, own, :], 1.0)
        bias = bias_ref[i]
        log_total = jnp.concatenate(
            [total_ref[0, 0, 2 * i : 2 * i + 1, :], total_ref[0, 0, 2 * i + 1 : 2 * i + 2, :]],
            axis=1,
        )
        scores = nt(keys, queries) + jnp.concatenate([bias, bias], axis=1)
        weights = jnp.exp(scores - log_total)
        weight_grad = nt(values, upstream)
        product = weights * weight_grad
        score_grad = low(product - weights * jnp.sum(product, axis=0, keepdims=True))
        dv_sum[window, :] += nn(low(weights), upstream)
        dk_sum[window, :] += nn(score_grad, queries)
        dq_ref[0, own, :] = low(unstacked(across(keys, score_grad)) * 0.125)
    dk_ref[0] = low(dk_sum[...])
    dv_ref[0] = low(dv_sum[...])


def attention_specs(block_size):
    wide = block_size + 2 * WIN
    blocks = block_size // WIN
    own = pl.BlockSpec((1, block_size, PAIR), lambda t, g: (t, 0, g))
    ext = pl.BlockSpec((1, wide, PAIR), lambda t, g: (t, 0, g))
    sums = pl.BlockSpec((1, 1, 2 * blocks, WIN), lambda t, g: (t, g, 0, 0))
    smem = pl.BlockSpec(memory_space=pltpu.SMEM)
    return wide, blocks, own, ext, sums, smem


def run_forward(lengths, base, query, key_ext, value_ext):
    texts, block_size, width = query.shape
    wide, blocks, own, ext, sums, smem = attention_specs(block_size)
    work = texts * blocks * (width // PAIR)
    return pl.pallas_call(
        functools.partial(attend_forward, blocks),
        grid=(texts, width // PAIR),
        in_specs=[smem, smem, own, ext, ext],
        out_specs=[own, sums],
        out_shape=[
            jax.ShapeDtypeStruct(query.shape, jnp.bfloat16),
            jax.ShapeDtypeStruct((texts, width // PAIR, 2 * blocks, WIN), jnp.float32),
        ],
        scratch_shapes=[pltpu.VMEM((blocks, KEYS, WIN), jnp.float32)],
        compiler_params=params(),
        cost_estimate=pl.CostEstimate(
            flops=work * 4 * KEYS * PAIR * 2 * WIN,
            bytes_accessed=query.size * 2 * 5,
            transcendentals=work * KEYS * 2 * WIN,
        ),
        name="attend_forward",
    )(lengths, base, query, key_ext, value_ext)


def run_backward(pairs, lengths, base, query, key_ext, value_ext, upstream, totals, kept, first):
    texts, block_size, width = query.shape
    wide = block_size + 2 * WIN
    blocks = block_size // WIN
    low_pair, count = pairs
    own = pl.BlockSpec((1, block_size, PAIR), lambda t, g: (t, 0, low_pair + g))
    ext = pl.BlockSpec((1, wide, PAIR), lambda t, g: (t, 0, low_pair + g))
    sums = pl.BlockSpec((1, 1, 2 * blocks, WIN), lambda t, g: (t, low_pair + g, 0, 0))
    smem = pl.BlockSpec(memory_space=pltpu.SMEM)
    others = tuple(kept) + tuple(first)
    work = texts * blocks * count
    return pl.pallas_call(
        functools.partial(attend_backward, blocks, len(others)),
        grid=(texts, count),
        in_specs=[smem, smem, own, ext, ext, own, sums]
        + [pl.BlockSpec(memory_space=pl.ANY)] * len(others),
        out_specs=[own, ext, ext],
        out_shape=[
            jax.ShapeDtypeStruct(query.shape, jnp.bfloat16),
            jax.ShapeDtypeStruct(key_ext.shape, jnp.bfloat16),
            jax.ShapeDtypeStruct(key_ext.shape, jnp.bfloat16),
        ],
        scratch_shapes=[
            pltpu.VMEM((blocks, KEYS, WIN), jnp.float32),
            pltpu.VMEM((wide, PAIR), jnp.float32),
            pltpu.VMEM((wide, PAIR), jnp.float32),
        ],
        input_output_aliases={7 + i: i for i in range(len(kept))},
        compiler_params=params(),
        cost_estimate=pl.CostEstimate(
            flops=work * 10 * KEYS * PAIR * 2 * WIN,
            bytes_accessed=query.size * 10,
            transcendentals=work * KEYS * 2 * WIN,
        ),
        name="attend_backward",
    )(lengths, base, query, key_ext, value_ext, upstream, totals, *others)


GATE_ROWS = 256
GATE_COLS = 256
GATE_SLAB = 32
BELL = 1.0 / math.sqrt(2.0 * math.pi)


def gate_kernel(
    rows_ref,
    upstream_ref,
    in_ref,
    out_ref,
    bias_ref,
    gate_ref,
    grad_ref,
    sums_ref,
    forward_ref,
    back_ref,
    forward_sum,
    back_sum,
):
    panel, tile = pl.program_id(0), pl.program_id(1)
    part = rows_ref.shape[1]
    ones = jnp.ones((8, GATE_ROWS), jnp.bfloat16)
    chunks = part // GATE_COLS

    def products(c):
        cols = slice(c * GATE_COLS, (c + 1) * GATE_COLS)
        hidden = nt(rows_ref[...], in_ref[cols, :]) + bias_ref[:, cols]
        return hidden, nn(upstream_ref[...], out_ref[:, cols])

    later = products(0)
    for c in range(chunks):
        hidden, hidden_grad = later
        if c + 1 < chunks:
            later = products(c + 1)
        cols = slice(c * GATE_COLS, (c + 1) * GATE_COLS)
        for i in range(GATE_ROWS // GATE_SLAB):
            own = slice(i * GATE_SLAB, (i + 1) * GATE_SLAB)
            u = hidden[own, :]
            square = u * u
            poly = PHI_POLY[-1] * square + PHI_POLY[-2]
            for term in PHI_POLY[-3::-1]:
                poly = poly * square + term
            half = 0.5 * jnp.tanh(poly * u)
            phi = half + 0.5
            bell = jnp.exp2(square * (-0.5 * math.log2(math.e)))
            gate_ref[own, cols] = low(u * phi)
            grad_ref[own, cols] = low(hidden_grad[own, :] * (phi + (u * BELL) * bell))
        sums_ref[0, :, cols] = nn(ones, grad_ref[:, cols])
    slot = pl.ds(pl.multiple_of(tile * GATE_ROWS, GATE_ROWS), GATE_ROWS)
    forward = nt(gate_ref[...], out_ref[...])
    back = nn(grad_ref[...], in_ref[...])

    @pl.when(panel == 0)
    def _():
        forward_sum[slot, :] = forward
        back_sum[slot, :] = back

    @pl.when(panel > 0)
    def _():
        forward_sum[slot, :] += forward
        back_sum[slot, :] += back

    @pl.when(panel == pl.num_programs(0) - 1)
    def _():
        forward_ref[...] = forward_sum[slot, :]
        back_ref[...] = back_sum[slot, :]


def run_gate(rows, upstream, packed, bias):
    tokens, width = rows.shape
    hidden = bias.shape[1]
    groups = hidden // width
    tiles = tokens // GATE_ROWS
    row_spec = pl.BlockSpec((GATE_ROWS, width), lambda j, i: (i, 0))
    out_spec = pl.BlockSpec((GATE_ROWS, width), lambda j, i: (i, j))
    last_spec = pl.BlockSpec(
        (GATE_ROWS, width), lambda j, i: (jnp.where(j == groups - 1, i, 0), 0)
    )
    wide_out = jax.ShapeDtypeStruct((tokens, hidden), jnp.bfloat16)
    row_out = jax.ShapeDtypeStruct((tokens, width), jnp.float32)
    return pl.pallas_call(
        gate_kernel,
        grid=(groups, tiles),
        in_specs=[
            row_spec,
            row_spec,
            pl.BlockSpec((width, width), lambda j, i: (0, 1 + groups + j)),
            pl.BlockSpec((width, width), lambda j, i: (0, 1 + j)),
            pl.BlockSpec((1, width), lambda j, i: (0, j)),
        ],
        out_specs=[
            out_spec,
            out_spec,
            pl.BlockSpec((1, 8, width), lambda j, i: (i, 0, j)),
            last_spec,
            last_spec,
        ],
        out_shape=[
            wide_out,
            wide_out,
            jax.ShapeDtypeStruct((tiles, 8, hidden), jnp.float32),
            row_out,
            row_out,
        ],
        scratch_shapes=[pltpu.VMEM((tokens, width), jnp.float32)] * 2,
        compiler_params=params(),
        cost_estimate=pl.CostEstimate(
            flops=tokens * width * hidden,
            bytes_accessed=4 * (tokens * width + width * hidden + tokens * hidden),
            transcendentals=2 * tokens * hidden,
        ),
        name="gate",
    )(rows, upstream, packed, packed, bias)


def flip(blocks, axis, mask):
    count = lax.axis_size(axis)
    return lax.ppermute(blocks, axis, [(i, i ^ mask) for i in range(count)])


def swap(blocks):
    return lax.all_to_all(blocks, "seq", split_axis=0, concat_axis=0, tiled=True)


def spread(block, axis="dp"):
    copies = jnp.broadcast_to(block[None], (lax.axis_size(axis),) + block.shape)
    return lax.all_to_all(copies, axis, split_axis=0, concat_axis=0, tiled=True)


def ordered(bit, own, other, dim):
    return jnp.where(
        bit == 0, jnp.stack([own, other], axis=dim), jnp.stack([other, own], axis=dim)
    )


def after(value, *first):
    return lax.optimization_barrier((value,) + first)[0]


def add_low(left, right):
    return low(left.astype(jnp.float32) + right.astype(jnp.float32))


def dp_bits():
    return lax.axis_size("dp").bit_length() - 1


class Halving:
    def __init__(self, blocks, dims):
        self.blocks, self.dims = blocks, list(dims)

    def start(self, dim):
        place = self.dims.index(dim)
        axis, shift = ("seq", "cx".index(dim)) if isinstance(dim, str) else ("dp", dim)
        bit = lax.axis_index(axis) // (1 << shift) % 2
        sent = lax.dynamic_index_in_dim(self.blocks, 1 - bit, place, keepdims=False)
        self.kept = lax.dynamic_index_in_dim(self.blocks, bit, place, keepdims=False)
        self.got = flip(sent, axis, 1 << shift)
        self.dims.pop(place)

    def finish(self, last=False, first=None):
        got = self.got if first is None else after(self.got, first)
        total = self.kept.astype(jnp.float32) + got.astype(jnp.float32)
        self.blocks = total if last else low(total)


def rounds():
    bits = list(range(dp_bits()))
    return list(zip(["x"] + bits, bits + ["x"]))


def one_round(one, other, i, first=None):
    left, right = rounds()[i]
    last = i == len(rounds()) - 1
    one.start(left)
    other.start(right)
    one.finish(last, first)
    other.finish(last, first)
    return [mark(one.blocks), mark(other.blocks)]


def mark(array):
    return array.reshape(-1, array.shape[-1])[:8, :128]


def picker(count, block, dp_count, dp_index, width):
    row = lax.broadcasted_iota(jnp.int32, (count * block, width), 0)
    col = lax.broadcasted_iota(jnp.int32, (count * block, width), 1)
    found = jnp.zeros(row.shape, jnp.float32)
    for s in range(count):
        here = (row >= s * block) & (row < (s + 1) * block)
        place = row + (s * (dp_count - 1) + dp_index) * block
        found = jnp.where(here & (col == place), 1.0, found)
    return low(found)


def padded(rows):
    extra = -rows.shape[0] % 16
    if extra:
        rows = jnp.concatenate([rows, jnp.zeros((extra, rows.shape[1]), jnp.float32)])
    return low(rows)


def hidden_first(seq_count, block, dp_count, dp_index, panels, row_sets, expand_rc, shrink_rc, expand_lw):
    shrink, expand = panels[0], panels[1]
    width = shrink.shape[0]
    pick = picker(seq_count, block, dp_count, dp_index, width)
    shrink_cols = low(nt(pick, shrink))
    expand_cols = nt(pick, expand)
    turned = low(nt(shrink_rc, shrink))
    shrink_right = nn(shrink_cols, shrink)
    expand_left = nn(low(expand_cols), expand)
    expand_turned = nt(low(nn(expand_rc, expand)), expand_lw)
    owned = expand_rc.shape[0] // seq_count
    sums = [
        jnp.sum(jnp.sum(jnp.square(p.astype(jnp.float32)), axis=0, keepdims=True), axis=1, keepdims=True)
        for p in (shrink, expand)
    ]
    line = lax.broadcasted_iota(jnp.int32, (16, width), 0)
    marks = jnp.zeros((16, width), jnp.float32)
    for i, value in enumerate(sums):
        for j in range(3):
            piece = low(jnp.broadcast_to(value, (16, width))).astype(jnp.float32)
            marks = jnp.where(line == 3 * i + j, piece, marks)
            value = value - piece[:1, :1]
    pieces = []
    for s in range(seq_count):
        rows = slice(s * owned, (s + 1) * owned)
        few = slice(s * block, (s + 1) * block)
        pieces.append(
            [
                padded(nt(row_sets[s, 0], shrink)),
                padded(nt(row_sets[s, 1], expand)),
                padded(expand_turned[rows]),
                padded(shrink_right[few]),
                padded(expand_left[few]),
                padded(expand_cols[few]),
                low(marks),
            ]
        )
    return pieces, turned


def direction_rows(seq_count, block, turned, shrink_lw):
    rows = nt(turned, shrink_lw)
    return [rows[s * block : (s + 1) * block] for s in range(seq_count)]


def hidden_kernel(
    seq_count,
    block,
    dp_count,
    index_ref,
    panels_ref,
    rows_ref,
    expand_rc_ref,
    shrink_rc_ref,
    expand_lw_ref,
    shrink_lw_ref,
    token_ref,
    out_ref,
    turn_ref,
    turned_ref,
):
    step = pl.program_id(0)

    @pl.when(step == 0)
    def _():
        pieces, turned = hidden_first(
            seq_count,
            block,
            dp_count,
            index_ref[0],
            panels_ref,
            rows_ref,
            expand_rc_ref[...],
            shrink_rc_ref[...],
            expand_lw_ref[...],
        )
        turned_ref[...] = turned
        for s in range(seq_count):
            start = 0
            for piece in pieces[s]:
                out_ref[s, start : start + piece.shape[0], :] = piece
                start += piece.shape[0]

    for s, rows in enumerate(direction_rows(seq_count, block, turned_ref[...], shrink_lw_ref[0])):
        turn_ref[s, 0] = padded(rows)


def run_hidden(seq_count, block, dp_count, dp_index, panels, row_sets, rc, shrink_rc, lw, shrink_lw, token):
    width = panels.shape[1]
    groups = shrink_lw.shape[0]
    owned = rc.shape[0] // seq_count
    if owned % 16 or block % 8:
        pieces, turned = hidden_first(
            seq_count, block, dp_count, dp_index, panels, row_sets, rc, shrink_rc, lw
        )
        turns = [direction_rows(seq_count, block, turned, shrink_lw[i]) for i in range(groups)]
        return (
            jnp.stack([jnp.concatenate(piece) for piece in pieces]),
            jnp.stack(
                [jnp.stack([padded(turns[i][s]) for i in range(groups)]) for s in range(seq_count)]
            ),
        )
    few = block + -block % 16
    rows_out = 3 * owned + 3 * few + 16
    whole = lambda array: pl.BlockSpec(array.shape, lambda i: (0,) * array.ndim)
    return pl.pallas_call(
        functools.partial(hidden_kernel, seq_count, block, dp_count),
        grid=(groups,),
        in_specs=[
            pl.BlockSpec(memory_space=pltpu.SMEM),
            whole(panels),
            whole(row_sets),
            whole(rc),
            whole(shrink_rc),
            whole(lw),
            pl.BlockSpec((1, width, width), lambda i: (i, 0, 0)),
            pl.BlockSpec(memory_space=pl.ANY),
        ],
        out_specs=[
            pl.BlockSpec((seq_count, rows_out, width), lambda i: (0, 0, 0)),
            pl.BlockSpec((seq_count, 1, few, width), lambda i: (0, i, 0, 0)),
        ],
        out_shape=[
            jax.ShapeDtypeStruct((seq_count, rows_out, width), jnp.bfloat16),
            jax.ShapeDtypeStruct((seq_count, groups, few, width), jnp.bfloat16),
        ],
        scratch_shapes=[pltpu.VMEM(shrink_rc.shape, jnp.bfloat16)],
        compiler_params=params(),
        cost_estimate=pl.CostEstimate(
            flops=40 * owned * width * width, bytes_accessed=12 * width * width, transcendentals=0
        ),
        name="hidden_update",
    )(dp_index.reshape(1), panels, row_sets, rc, shrink_rc, lw, shrink_lw, token)


def attend_products(seq_count, block, dp_count, dp_index, scale, whole, own, rc, lw):
    width = whole.shape[0]
    pick = picker(seq_count, block, dp_count, dp_index, width)
    wide = whole.astype(jnp.float32)
    total = jnp.sum(jnp.sum(wide * wide, axis=0, keepdims=True), axis=1, keepdims=True)
    square = total * (scale * scale / (width * width)) + STAT_EPSILON
    gram = (0.5 * scale * scale / width) / square
    left = nt(low(own), whole) * gram
    right = nn(low(nt(pick, whole)), whole) * gram
    turned = nt(low(nt(rc, whole)), lw) * (scale * lax.rsqrt(square))
    return [
        [padded(piece[s * block : (s + 1) * block]) for piece in (left, right, turned, own)]
        for s in range(seq_count)
    ]


def attend_kernel(seq_count, block, dp_count, scale, index_ref, whole_ref, own_ref, rc_ref, lw_ref, token_ref, out_ref):
    pieces = attend_products(
        seq_count,
        block,
        dp_count,
        index_ref[0],
        scale,
        whole_ref[...],
        own_ref[...],
        rc_ref[...],
        lw_ref[...],
    )
    for s in range(seq_count):
        for i, piece in enumerate(pieces[s]):
            out_ref[s, i] = piece


def run_attend(seq_count, block, dp_count, dp_index, scale, whole, own, rc, lw, token):
    width = whole.shape[0]
    if block % 8:
        pieces = attend_products(
            seq_count, block, dp_count, dp_index, scale, whole, own, rc, lw
        )
        return jnp.stack([jnp.stack(piece) for piece in pieces])
    few = block + -block % 16
    vmem = pl.BlockSpec(memory_space=pltpu.VMEM)
    return pl.pallas_call(
        functools.partial(attend_kernel, seq_count, block, dp_count, scale),
        in_specs=[pl.BlockSpec(memory_space=pltpu.SMEM)]
        + [vmem] * 4
        + [pl.BlockSpec(memory_space=pl.ANY)],
        out_specs=vmem,
        out_shape=jax.ShapeDtypeStruct((seq_count, 4, few, width), jnp.bfloat16),
        compiler_params=params(),
        cost_estimate=pl.CostEstimate(
            flops=10 * own.shape[0] * width * width, bytes_accessed=6 * width * width, transcendentals=0
        ),
        name="attend_update",
    )(dp_index.reshape(1), whole, own, rc, lw, token)


def finish(direction, moment, weight, row_count):
    new_moment = MOMENTUM * moment + direction
    new_weight = weight - MATRIX_RATE / math.sqrt(row_count) * new_moment
    return (new_moment, new_weight)


def shards(
    characters,
    cotangent,
    lengths,
    vectors,
    vector_acc,
    attend_weight,
    attend_moment,
    attend_left,
    attend_right,
    attend_rootleft,
    attend_rootright,
    expand_weight,
    expand_moment,
    expand_left,
    expand_right,
    expand_rootleft,
    expand_rootright,
    shrink_weight,
    shrink_moment,
    shrink_left,
    shrink_right,
    shrink_rootleft,
    shrink_rootright,
):
    text_count, block_size, model_width = characters.shape
    token_rows = text_count * block_size
    both = ("seq", "dp")
    seq_count = lax.axis_size("seq")
    dp_count = lax.axis_size("dp")
    seq_index = lax.axis_index("seq")
    dp_index = lax.axis_index("dp")
    core = seq_index % 2
    chip = seq_index // 2
    tokens_all = token_rows * seq_count * dp_count
    grad_scale = 1.0 / math.sqrt(tokens_all)
    square_scale = grad_scale * grad_scale
    hidden = expand_weight.shape[1] * seq_count * dp_count
    part = hidden // seq_count
    block = model_width // (seq_count * dp_count)
    hidden_block = hidden // (seq_count * dp_count)
    rows_own = seq_count * block

    owners = seq_count * dp_count
    groups = hidden // model_width
    ends = seq_count - 1
    before = lax.ppermute(
        characters[:, block_size - WIN :], "seq", [(i, i + 1) for i in range(ends)]
    )
    follow = lax.ppermute(characters[:, :WIN], "seq", [(i + 1, i) for i in range(ends)])

    attend_t = attend_weight.transpose(1, 2, 0)
    expand_t = expand_weight.T
    shrink_t = shrink_weight.T
    packed = jnp.concatenate(
        [
            low(attend_t[3]),
            low(shrink_t)
            .reshape(block, owners, groups, block)
            .transpose(0, 2, 1, 3)
            .reshape(block, hidden),
            low(expand_t)
            .reshape(groups, block, model_width)
            .transpose(1, 0, 2)
            .reshape(block, hidden),
        ],
        axis=1,
    )
    packed_all = lax.all_gather(packed, both, axis=0, tiled=True)
    over_dp = spread(low(attend_t[:3])).transpose(1, 0, 2, 3)

    def panels_of(rows):
        return low(rows).reshape(rows.shape[0], seq_count, part).transpose(1, 0, 2)

    def copies_of(rows):
        return jnp.broadcast_to(low(rows)[None], (seq_count,) + rows.shape)

    root_parts = jnp.concatenate(
        [
            panels_of(expand_rootright.T),
            low(attend_rootright.transpose(1, 2, 0)),
            copies_of(shrink_rootright.T),
            panels_of(shrink_rootleft),
            low(attend_rootleft).transpose(1, 0, 2),
            copies_of(expand_rootleft),
        ],
        axis=1,
    )
    over_chip = ordered(chip, over_dp, flip(over_dp, "seq", 2), 1)

    input_ext = jnp.concatenate([before, characters, follow], axis=1)
    wide = block_size + 2 * WIN

    gain_one = vectors[0]
    bias_one = vectors[1]
    query_bias = vectors[2]
    value_bias = vectors[3]
    out_bias = vectors[4]
    gain_two = vectors[5]
    bias_two = vectors[6]
    shrink_bias = vectors[7]
    expand_bias = vectors[8:].reshape(owners, groups, block).transpose(1, 0, 2).reshape(1, -1)
    normed_ext = low(normalize(input_ext.astype(jnp.float32), gain_one, bias_one))
    over_chip, normed_ext, root_parts = lax.optimization_barrier(
        (over_chip, normed_ext, root_parts)
    )
    over_core = ordered(core, over_chip, flip(over_chip, "seq", 1), 2)
    qkv_t = over_core.reshape(3 * model_width, model_width)
    roots = swap(root_parts)
    normed_low = normed_ext[:, WIN : WIN + block_size].reshape(token_rows, model_width)
    ext_rows = normed_ext.reshape(text_count * wide, model_width)
    query_low = low(nt(normed_low, qkv_t[:model_width]) + query_bias).reshape(characters.shape)
    key_ext = low(nt(ext_rows, qkv_t[model_width : 2 * model_width])).reshape(
        text_count, wide, model_width
    )
    value_ext = low(nt(ext_rows, qkv_t[2 * model_width :]) + value_bias).reshape(
        text_count, wide, model_width
    )
    query_low, roots = lax.optimization_barrier((query_low, roots))
    cut = hidden_block + 2 * block
    root_all = lax.all_gather(roots[:, cut:], "dp", axis=1)
    base = (seq_index * block_size).astype(jnp.int32).reshape(1)
    attended, totals = run_forward(lengths, base, query_low, key_ext, value_ext)
    attended_low = attended.reshape(token_rows, model_width)

    out_t = packed_all[:, :model_width]
    layer_input = characters.astype(jnp.float32).reshape(token_rows, model_width)
    middle = layer_input + nt(attended_low, out_t) + out_bias
    normed_two_low = low(normalize(middle, gain_two, bias_two))
    upstream = cotangent.reshape(token_rows, model_width)
    gated_low, expanded_grad, expand_sums, forward, normed_two_grad = run_gate(
        normed_two_low, upstream, packed_all, expand_bias
    )
    layer_output = low(middle + forward + shrink_bias).reshape(characters.shape)

    bits = dp_bits()
    grid_dims = (2,) * (2 + bits)
    link_dims = ["x", "c"] + list(range(bits - 1, -1, -1))

    def hidden_sum(left_rows, right_rows):
        sums = low(across(left_rows, right_rows))
        return Halving(
            sums.reshape((groups,) + grid_dims + (block, model_width)), [None] + link_dims
        )

    shrink_sum = hidden_sum(gated_low, upstream)
    shrink_sum.start("c")
    expand_sum = hidden_sum(expanded_grad, normed_two_low)
    expand_sum.start("c")
    shrink_sum.finish()
    expand_sum.finish()
    marks = [mark(shrink_sum.blocks), mark(expand_sum.blocks)]

    upstream_float = upstream.astype(jnp.float32)
    grad_shrink_bias = jnp.sum(upstream_float, axis=0)
    grad_expand_bias = (
        jnp.sum(expand_sums[:, 0], axis=0)
        .reshape(groups, owners, block)
        .transpose(1, 0, 2)
        .reshape(groups, model_width)
    )

    unused_norm, norm_two_back = jax.vjp(normalize, middle, gain_two, bias_two)
    middle_part, grad_gain_two, grad_bias_two = norm_two_back(normed_two_grad)
    middle_grad = upstream_float + middle_part
    branch_grad = low(middle_grad)
    grad_out_bias = jnp.sum(branch_grad.astype(jnp.float32), axis=0)
    grad_out = low(across(attended_low, branch_grad))
    attended_grad = low(nn(branch_grad, out_t)).reshape(characters.shape)
    pairs = model_width // PAIR
    early = 2 * pairs // 3
    kept = run_backward(
        (0, early), lengths, base, query_low, key_ext, value_ext, attended_grad, totals, (), marks
    )
    marks = one_round(shrink_sum, expand_sum, 0) + [mark(root_all)]
    kept = run_backward(
        (early, pairs - early),
        lengths,
        base,
        query_low,
        key_ext,
        value_ext,
        attended_grad,
        totals,
        kept,
        marks,
    )
    query_grad, key_grad, value_grad = kept
    marks = one_round(shrink_sum, expand_sum, 1)

    pair_grad = jnp.stack([key_grad, value_grad])
    from_above = lax.ppermute(
        pair_grad[:, :, :WIN], "seq", [(i + 1, i) for i in range(ends)]
    )
    from_below = lax.ppermute(
        pair_grad[:, :, block_size + WIN :], "seq", [(i, i + 1) for i in range(ends)]
    )
    from_above = after(from_above, *marks)
    pair_own = pair_grad[:, :, WIN : WIN + block_size]
    pair_low = jnp.concatenate(
        [
            add_low(pair_own[:, :, :WIN], from_below),
            pair_own[:, :, WIN : block_size - WIN],
            add_low(pair_own[:, :, block_size - WIN :], from_above),
        ],
        axis=2,
    ).reshape(2, token_rows, model_width)
    query_rows = query_grad.reshape(token_rows, model_width)
    for i in range(2, len(rounds())):
        marks = one_round(shrink_sum, expand_sum, i)
    shrink_own, expand_own = shrink_sum.blocks, expand_sum.blocks
    hidden_own = jnp.stack(
        [low(own).reshape(hidden_block, model_width) for own in (shrink_own, expand_own)]
    )

    grads = jnp.stack(
        [
            low(across(normed_low, query_rows)),
            low(across(normed_low, pair_low[0])),
            low(across(normed_low, pair_low[1])),
            grad_out,
        ]
    ).reshape((2, 2) + (2, seq_count // 2) + (2,) * bits + (block, model_width))
    core_sum = Halving(grads, ["x", "c"])
    core_sum.start("c")
    core_sum.finish()
    halves = [
        Halving(core_sum.blocks[:, i], ["x", None] + list(range(bits - 1, -1, -1)))
        for i in range(2)
    ]
    for i in range(len(rounds())):
        one_round(*halves, i, jnp.stack(marks) if i == 0 else None)
    attend_own = jnp.concatenate([half.blocks for half in halves])
    grad_query_bias = jnp.sum(query_rows.astype(jnp.float32), axis=0)
    grad_value_bias = jnp.sum(pair_low[1].astype(jnp.float32), axis=0)
    normed_grad = (
        nn(query_rows, qkv_t[:model_width])
        + nn(pair_low[0], qkv_t[model_width : 2 * model_width])
        + nn(pair_low[1], qkv_t[2 * model_width :])
    )
    unused_first, norm_one_back = jax.vjp(normalize, layer_input, gain_one, bias_one)
    input_part, grad_gain_one, grad_bias_one = norm_one_back(normed_grad)
    characters_grad = low(middle_grad + input_part).reshape(characters.shape)
    vector_terms = jnp.concatenate(
        [
            jnp.stack(
                [
                    grad_gain_one,
                    grad_bias_one,
                    grad_query_bias,
                    grad_value_bias,
                    grad_out_bias,
                    grad_gain_two,
                    grad_bias_two,
                    grad_shrink_bias,
                ]
            ),
            grad_expand_bias.reshape(-1, model_width),
        ],
        axis=0,
    )
    whole = spread(low(attend_own)).transpose(1, 0, 2, 3).reshape(model_width, model_width)
    token = attend_own[0, 0, :128]
    vector_terms = after(vector_terms, token)
    vector_some = jnp.sum(spread(vector_terms), axis=0)

    expand_rc = roots[:, :hidden_block].reshape(seq_count * hidden_block, part)
    attend_rc = roots[:, hidden_block : hidden_block + block].reshape(rows_own, model_width)
    shrink_rc = roots[:, hidden_block + block : cut].reshape(rows_own, model_width)
    shrink_lw = root_all[:, :, :hidden_block].reshape(seq_count, part, part)
    attend_lw = root_all[:, :, hidden_block : hidden_block + block].reshape(
        model_width, model_width
    )
    expand_lw = root_all[:, :, hidden_block + block :].reshape(model_width, model_width)

    panels = lax.all_gather(hidden_own, "dp", axis=1, tiled=True)
    row_sets = spread(hidden_own, "seq")
    index = dp_index.astype(jnp.int32)
    products, turns = run_hidden(
        seq_count,
        block,
        dp_count,
        index,
        panels,
        row_sets,
        expand_rc,
        shrink_rc,
        expand_lw,
        shrink_lw,
        token,
    )
    back = swap(products)
    turned_back = swap(turns)
    to_return = run_attend(
        seq_count,
        block,
        dp_count,
        index,
        grad_scale,
        whole,
        attend_own.reshape(rows_own, model_width),
        attend_rc,
        attend_lw,
        products[0, 0, :128],
    )
    returned = swap(to_return)[:, :, :block].astype(jnp.float32)
    vector_some = after(vector_some, returned[0, 0, 0, :128])
    vector_sum = jnp.sum(spread(vector_some, "seq"), axis=0)
    vector_grad = vector_sum * grad_scale
    vector_newacc = vector_acc + vector_grad * vector_grad
    vector_new = vectors - VECTOR_RATE * vector_grad / (jnp.sqrt(vector_newacc) + 1e-08)

    few = block + -block % 16
    much = hidden_block + -hidden_block % 16
    starts = [0, much, 2 * much, 3 * much, 3 * much + few, 3 * much + 2 * few, 3 * much + 3 * few]
    sizes = [hidden_block] * 3 + [block] * 3 + [16]
    parts = [back[:, i : i + n] for i, n in zip(starts, sizes)]

    def unfold(blocks):
        return blocks.transpose(1, 0, 2).reshape(blocks.shape[1], -1)

    def total(blocks):
        return jnp.sum(blocks.astype(jnp.float32), axis=0)

    totals_all = jnp.sum(total(parts[6])[:6, 0].reshape(2, 3), axis=1)
    squares = totals_all * square_scale / (model_width * hidden) + STAT_EPSILON
    shrink_scale = square_scale / squares[0]
    expand_scale = square_scale / squares[1]
    shrink_newleft = 0.5 * shrink_left + unfold(parts[0]).astype(jnp.float32) * (
        0.5 * shrink_scale / model_width
    )
    shrink_newright_t = 0.5 * shrink_right.T + total(parts[3]) * (0.5 * shrink_scale / hidden)
    expand_newright_t = 0.5 * expand_right.T + unfold(parts[1]).astype(jnp.float32) * (
        0.5 * expand_scale / model_width
    )
    expand_newleft = 0.5 * expand_left + total(parts[4]) * (0.5 * expand_scale / hidden)
    expand_rows = unfold(parts[5]).astype(jnp.float32) * grad_scale
    expand_direction_t = total(parts[2]) * (grad_scale * lax.rsqrt(squares[1]))
    shrink_direction_t = unfold(total(turned_back)[:, :block]) * (
        grad_scale * lax.rsqrt(squares[0])
    )
    expand_newmoment_t, expand_newweight_t = finish(
        expand_direction_t, expand_moment.T, expand_t, model_width
    )
    shrink_newmoment_t, shrink_newweight_t = finish(
        shrink_direction_t, shrink_moment.T, shrink_t, hidden
    )
    shrink_grad = shrink_own.reshape(hidden_block, model_width) * grad_scale

    attend_newleft = 0.5 * attend_left + returned[:, 0].transpose(1, 0, 2)
    attend_newright_t = 0.5 * attend_right.transpose(1, 2, 0) + returned[:, 1]
    attend_rows = returned[:, 3].transpose(1, 0, 2) * grad_scale
    attend_newmoment_t, attend_newweight_t = finish(
        returned[:, 2], attend_moment.transpose(1, 2, 0), attend_t, model_width
    )
    return (
        layer_output,
        characters_grad,
        attend_rows,
        attend_newmoment_t.transpose(2, 0, 1),
        attend_newweight_t.transpose(2, 0, 1),
        attend_newleft,
        attend_newright_t.transpose(2, 0, 1),
        expand_rows,
        expand_newmoment_t.T,
        expand_newweight_t.T,
        expand_newleft,
        expand_newright_t.T,
        shrink_grad,
        shrink_newmoment_t.T,
        shrink_newweight_t.T,
        shrink_newleft,
        shrink_newright_t.T,
        vector_grad,
        vector_newacc,
        vector_new,
    )


def solution(mesh):
    return jax.shard_map(
        shards,
        mesh=mesh,
        in_specs=(
            P("dp", "seq", None),
            P("dp", "seq", None),
            P("dp"),
            P(),
            P(),
            P(None, None, ("seq", "dp")),
            P(None, None, ("seq", "dp")),
            P(("seq", "dp"), None, None),
            P(None, None, ("seq", "dp")),
            P(("seq", "dp"), None, None),
            P(None, None, ("seq", "dp")),
            P(None, ("seq", "dp")),
            P(None, ("seq", "dp")),
            P(("seq", "dp"), None),
            P(None, ("seq", "dp")),
            P(("seq", "dp"), None),
            P(None, ("seq", "dp")),
            P(None, ("seq", "dp")),
            P(None, ("seq", "dp")),
            P(("seq", "dp"), None),
            P(None, ("seq", "dp")),
            P(("seq", "dp"), None),
            P(None, ("seq", "dp")),
        ),
        out_specs=(
            P("dp", "seq", None),
            P("dp", "seq", None),
            P(("seq", "dp"), None, None),
            P(None, None, ("seq", "dp")),
            P(None, None, ("seq", "dp")),
            P(("seq", "dp"), None, None),
            P(None, None, ("seq", "dp")),
            P(("seq", "dp"), None),
            P(None, ("seq", "dp")),
            P(None, ("seq", "dp")),
            P(("seq", "dp"), None),
            P(None, ("seq", "dp")),
            P(("seq", "dp"), None),
            P(None, ("seq", "dp")),
            P(None, ("seq", "dp")),
            P(("seq", "dp"), None),
            P(None, ("seq", "dp")),
            P(),
            P(),
            P(),
        ),
        check_vma=False,
    )
```

time: 608 us -> 600 us (0.987)
  matrix products: 94.5 us -> 50.4 us
  blocking collectives: 37.1 us -> 0 us
  waiting for transfers between devices: 158 us -> 194 us
  Pallas kernels: 74.2 us -> 105 us
  starting transfers between devices: 48.8 us -> 73.5 us
  other arithmetic: 87.3 us -> 68.4 us
    all_to_all x1 -> x0, blocking collectives: 37.1 us -> none  [spread(): return lax.all_to_all(copies, 'dp', split_axis=0, concat_axis=0, tiled=True)]
    pallas_call x2 -> x5, Pallas kernels: 51.5 us -> 82.4 us  [the longest x1 38.7 us: run_gate(): pl.pallas_call(gate_kernel, grid=(groups, tiles), in_specs=[row_spec, row...]
    dot_general x6 -> x4, matrix products: 32.7 us -> 9.23 us  [nn(): return jnp.dot(left_rows, right_cols, preferred_element_type=jnp.float32)]
    all_to_all x3 -> x4, waiting for transfers between devices: 35.2 us -> 57.9 us  [swap(): lax.all_to_all(blocks, 'seq', split_axis=0, concat_axis=0, tiled=True)]
    ppermute x8 -> x21, waiting for transfers between devices: 60.4 us -> 81.3 us  [flip(): return lax.ppermute(blocks, axis, [(i, i ^ mask) for i in range(count)])]
    dot_general x12 -> x4, matrix products: 34.7 us -> 15 us  [nt(): lax.dot_general(left_rows, right_rows, (((1,), (1,)), ((), ())), preferre...]
    another operation x5 -> x1, local copies, waits for them, and re-layouts: 17.8 us -> 0.08 us  [shards(): totals_all = jnp.sum(total(parts[6])[:6, 0].reshape(2, 3), axis=1)]
    all_to_all x5, waiting for transfers between devices: 56.2 us -> 41.2 us  [spread(): return lax.all_to_all(copies, axis, split_axis=0, concat_axis=0, tiled=True)]
  transfers between devices with their start and end apart: 26 -> 37, of which waited for: 11 -> 20; matrix products, arithmetic and copies ran while one was open for 36% -> 28% of each run, Pallas kernels for 8% -> 16%
where the time goes in v2:
time: 600 us; the launch traced here: 590 us
  waiting for transfers between devices  194 us (32%)
  Pallas kernels  105 us (18%)
  local copies, waits for them, and re-layouts  80 us (13%)
  starting transfers between devices  73.5 us (12%)
  other arithmetic  68.4 us (11%)
  matrix products  50.4 us (8%)
  between operations  18.6 us (3%)
    ppermute x21, waiting for transfers between devices, flip(): return lax.ppermute(blocks, axis, [(i, i ^ mask) for i in range(count)])  81.3 us
    all_to_all x4, waiting for transfers between devices, swap(): lax.all_to_all(blocks, 'seq', split_axis=0, concat_axis=0, tiled=True)  57.9 us
    all_to_all x5, waiting for transfers between devices, spread(): return lax.all_to_all(copies, axis, split_axis=0, concat_axis=0, tiled=True)  41.2 us
    pallas_call x1, Pallas kernels, run_gate(): pl.pallas_call(gate_kernel, grid=(groups, tiles), in_specs=[row_spec, row...  38.7 us
    all_to_all x5, starting transfers between devices, spread(): return lax.all_to_all(copies, axis, split_axis=0, concat_axis=0, tiled=True)  28.2 us
    pallas_call x2, Pallas kernels, run_backward(): pl.pallas_call(functools.partial(attend_backward, blocks, len(others)), g...  26.7 us
    dot_general x6, matrix products, across(): lax.dot_general(left_rows, right_rows, (((0,), (0,)), ((), ())), preferre...  26.1 us
    convert_element_type x27, other arithmetic, low(): return values.astype(jnp.bfloat16)  25.9 us
  transfers between devices with their start and end apart: 37, of which 20 were waited for; matrix products, arithmetic and copies ran while one was open for 28% of the time, Pallas kernels for 16%

profile of v2, /device:TPU:0, one launch (start us, length us, event | category | flops | bytes accessed | tf_op | source)
XLA Modules:
  0.0 590.0 jit_solution(17757217968583408460)
XLA Ops:
  13.8 7.3 %all-to-all-start = ((bf16[8,3,24,768]{3,2,1,0:T(8,128)(2,1)}), bf16[8,3,24,768]{3,2,1,0:T(8,128)(2,1)}, u32[]{:S(2)}, u32[]{:S(2)}) async-start(bf16[8,3,24,768]{3,2,1,0:T(8,128)(2,1)} %broadcast_in_dim.22), calls=%async_computation | async-start | bytes 1769472 | tf_op jit(solution)/shard_map/all_to_all | solution.py:355
  34.7 16.0 %all-to-all-done = bf16[8,3,24,768]{3,2,1,0:T(8,128)(2,1)} async-done(((bf16[8,3,24,768]{3,2,1,0:T(8,128)(2,1)}), bf16[8,3,24,768]{3,2,1,0:T(8,128)(2,1)}, u32[]{:S(2)}, u32[]{:S(2)}) %all-to-all-start) | async-done | bytes 884768 | tf_op jit(solution)/shard_map/all_to_all | solution.py:355
  55.2 3.1 fusion.5
  58.4 23.0 %collective-permute-done = bf16[3,8,24,768]{3,2,1,0:T(8,128)(2,1)S(1)} collective-permute-done((bf16[3,8,24,768]{3,2,1,0:T(8,128)(2,1)S(1)}, bf16[3,8,24,768]{3,2,1,0:T(8,128)(2,1)S(1)}, u32[]{:S(2)}, u32[]{:S(2)}) %collective-permute-start) | collective-permute-done | bytes 884768 | tf_op jit(solution)/shard_map/ppermute | solution.py:346
  82.8 4.5 all-to-all-start.1
  90.3 3.5 maximum_select_fusion
  98.7 25.8 %all-to-all-done.1 = bf16[4,288,768]{2,1,0:T(8,128)(2,1)} async-done(((bf16[4,288,768]{2,1,0:T(8,128)(2,1)}), bf16[4,288,768]{2,1,0:T(8,128)(2,1)}, u32[]{:S(2)}, u32[]{:S(2)}) %all-to-all-start.1) | async-done | bytes 1769504 | tf_op jit(solution)/shard_map/all_to_all | solution.py:350
  128.7 4.5 copy.196
  133.2 5.7 convolution_convert_fusion.2
  138.8 3.5 add_convert_fusion
  142.3 22.7 %attend_forward.1 = (bf16[2,512,768]{2,1,0:T(8,128)(2,1)}, f32[2,6,8,128]{3,2,1,0:T(8,128)}) custom-call(s32[2]{0:T(128)} %lengths.5, s32[1]{0:T(128)} %bitcast.1.base, bf16[2,512,768]{2,1,0:T(8,128)(2,1)} %bitcast.415, bf16[2,768,768]{2,1,0:T(8,128)(2,1)} %bitcast.402, bf16[2,768,768]{2,1,0:T(8,128)(2,1)} %bitcast.405), custom_call_target="tpu_custom_call" | custom-call | flops 2415919104 | bytes 7864320 | tf_op jit(solution)/shard_map/attend_forward/pallas_call | solution.py:170
  165.1 3.3 fusion.68
  170.8 38.7 %gate.1 = (bf16[1024,3072]{1,0:T(8,128)(2,1)}, bf16[1024,3072]{1,0:T(8,128)(2,1)}, f32[4,8,3072]{2,1,0:T(8,128)}, f32[1024,768]{1,0:T(8,128)}, f32[1024,768]{1,0:T(8,128)}) custom-call(bf16[1024,768]{1,0:T(8,128)(2,1)} %add_convert_fusion.3.rows_ref, bf16[1024,768]{1,0:T(8,128)(2,1)} %bitcast.369, ...), custom_call_target="tpu_custom_call" | custom-call | flops 2415919104 | bytes 25165824 | tf_op jit(solution)/shard_map/gate/pallas_call | solution.py:309
  209.5 9.9 %convolution_convert_fusion = bf16[3072,768]{1,0:T(8,128)(2,1)} fusion(bf16[1024,3072]{1,0:T(8,128)(2,1)} %get-tuple-element.52, bf16[1024,768]{1,0:T(8,128)(2,1)S(1)} %copy-done.18), kind=kOutput, calls=%fused_computation.8 | convolution fusion | flops 4834197504 | bytes 12582912 | tf_op jit(solution)/shard_map/dot_general | solution.py:46
  219.4 7.3 %convolution_convert_fusion.1 = bf16[3072,768]{1,0:T(8,128)(2,1)} fusion(bf16[1024,3072]{1,0:T(8,128)(2,1)S(1)} %copy-done.65, bf16[1024,768]{1,0:T(8,128)(2,1)S(1)} %bitcast.370), kind=kOutput, calls=%fused_computation.9 | convolution fusion | flops 4834197504 | bytes 12582912 | tf_op jit(solution)/shard_map/dot_general | solution.py:46
  226.8 5.6 constant_dynamic-slice_fusion.3
  234.3 13.6 %all-gather.9.cloned.1.call-done = bf16[4,1152,768]{2,1,0:T(8,128)(2,1)} async-done(((bf16[4,144,768]{2,1,0:T(8,128)(2,1)}), bf16[4,1152,768]{2,1,0:T(8,128)(2,1)}) %all-gather.9.cloned.1.call-update) | async-done | bytes 7077904 | tf_op jit(solution)/shard_map/all_gather | solution.py:750
  259.7 4.5 convolution_convert_fusion.3
  273.8 4.5 fusion.24
  281.4 17.1 %attend_backward.2 = (bf16[2,512,768]{2,1,0:T(8,128)(2,1)}, bf16[2,768,768]{2,1,0:T(8,128)(2,1)}, bf16[2,768,768]{2,1,0:T(8,128)(2,1)}) custom-call(s32[2]{0:T(128)} %lengths.5, s32[1]{0:T(128)} %bitcast.1.base, bf16[2,512,768]{2,1,0:T(8,128)(2,1)} %bitcast.416, bf16[2,768,768]{2,1,0:T(8,128)(2,1)} %bitcast.403, bf16[2,768,768]{2,1,0:T(8,128)(2,1)} %bitcast.406, ...), custom_call_target="tpu_custom_call" | custom-call | flops 4026531840 | bytes 7864320 | tf_op jit(solution)/shard_map/attend_backward/pallas_call | solution.py:201
  304.1 9.6 %attend_backward.3 = (bf16[2,512,768]{2,1,0:T(8,128)(2,1)}, bf16[2,768,768]{2,1,0:T(8,128)(2,1)}, bf16[2,768,768]{2,1,0:T(8,128)(2,1)}) custom-call(s32[2]{0:T(128)} %lengths.5, s32[1]{0:T(128)} %bitcast.1.base, bf16[2,512,768]{2,1,0:T(8,128)(2,1)} %bitcast.417, ...), custom_call_target="tpu_custom_call", output_to_operand_aliasing={{0}: (7, {}), {1}: (8, {}), {2}: (9, {})} | custom-call | flops 2013265920 | bytes 7864320 | tf_op jit(solution)/shard_map/attend_backward/pallas_call | solution.py:201
  324.7 8.2 %collective-permute-done.12 = bf16[4,2,2,24,768]{4,3,0,1,2:T(8,128)(2,1)S(1)} collective-permute-done((bf16[4,2,2,24,768]{4,3,0,1,2:T(8,128)(2,1)S(1)}, bf16[4,2,2,24,768]{4,3,0,1,2:T(8,128)(2,1)S(1)}, u32[]{:S(2)}, u32[]{:S(2)}) %collective-permute-start.12) | collective-permute-done | bytes 589856 | tf_op jit(solution)/shard_map/ppermute | solution.py:346
  352.3 3.9 collective-permute-done.17
  356.3 4.0 collective-permute-done.14
  363.8 12.9 %collective-permute-done.11 = bf16[2,2,2,2,24,768]{5,4,0,1,2,3:T(8,128)(2,1)S(1)} collective-permute-done((bf16[2,2,2,2,24,768]{5,4,0,1,2,3:T(8,128)(2,1)S(1)}, bf16[2,2,2,2,24,768]{5,4,0,1,2,3:T(8,128)(2,1)S(1)}, u32[]{:S(2)}, u32[]{:S(2)}) %collective-permute-start.11) | collective-permute-done | bytes 589856 | tf_op jit(solution)/shard_map/ppermute | solution.py:346
  380.9 5.4 collective-permute-done.18
  389.4 7.0 %collective-permute-done.19 = bf16[2,2,24,768]{3,2,0,1:T(8,128)(2,1)S(1)} collective-permute-done((bf16[2,2,24,768]{3,2,0,1:T(8,128)(2,1)S(1)}, bf16[2,2,24,768]{3,2,0,1:T(8,128)(2,1)S(1)}, u32[]{:S(2)}, u32[]{:S(2)}) %collective-permute-start.19) | collective-permute-done | bytes 147488 | tf_op jit(solution)/shard_map/ppermute | solution.py:346
  396.5 5.3 collective-permute-start.20
  402.5 3.4 collective-permute-start.22
  407.9 8.0 %all-to-all-start.7 = ((f32[8,12,768]{2,1,0:T(8,128)}), f32[8,12,768]{2,1,0:T(8,128)}, u32[]{:S(2)}, u32[]{:S(2)}) async-start(f32[8,12,768]{2,1,0:T(8,128)} %broadcast_in_dim.31), calls=%async_computation.7 | async-start | bytes 786432 | tf_op jit(solution)/shard_map/all_to_all | solution.py:355
  417.7 16.0 %all-to-all-done.7 = f32[8,12,768]{2,1,0:T(8,128)} async-done(((f32[8,12,768]{2,1,0:T(8,128)}), f32[8,12,768]{2,1,0:T(8,128)}, u32[]{:S(2)}, u32[]{:S(2)}) %all-to-all-start.7) | async-done | bytes 294944 | tf_op jit(solution)/shard_map/all_to_all | solution.py:355
  434.8 4.4 all-to-all-start.3
  440.3 8.7 %collective-permute-done.23 = bf16[2,2,24,768]{3,2,1,0:T(8,128)(2,1)S(1)} collective-permute-done((bf16[2,2,24,768]{3,2,1,0:T(8,128)(2,1)S(1)}, bf16[2,2,24,768]{3,2,1,0:T(8,128)(2,1)S(1)}, u32[]{:S(2)}, u32[]{:S(2)}) %collective-permute-start.23) | collective-permute-done | bytes 147488 | tf_op jit(solution)/shard_map/ppermute | solution.py:346
  451.7 5.0 collective-permute-done.24
  458.4 4.0 all-to-all-start.8
  463.1 4.7 all-to-all-done.8
  469.8 4.5 all-to-all-start.2
  478.0 4.8 slice.296
  482.8 3.2 fusion.61
  486.0 12.6 %hidden_update.1 = (bf16[4,400,768]{2,1,0:T(8,128)(2,1)}, bf16[4,4,32,768]{3,2,1,0:T(8,128)(2,1)}) custom-call(s32[1]{0:T(128)} %bitcast.55.index_ref, bf16[2,768,768]{2,1,0:T(8,128)(2,1)} %all-gather.7.cloned.1.call-done.panels_ref, bf16[4,2,96,768]{3,2,1,0:T(8,128)(2,1)} %all-to-all-done.3.rows_ref, bf16[384,768]{1,0:T(8,128)(2,1)} %bitcast.401, ...), custom_call_target="tpu_custom_call" | custom-call | flops 2264924160 | bytes 7077888 | tf_op jit(solution)/shard_map/hidden_update/pallas_call | solution.py:537
  498.5 4.5 all-to-all-done.2
  503.0 4.2 all-to-all-start.6
  511.5 4.5 attend_update.1
  518.9 4.2 all-to-all-start.4
  523.1 11.7 %all-to-all-done.4 = bf16[4,4,32,768]{3,2,1,0:T(8,128)(2,1)} async-done(((bf16[4,4,32,768]{3,2,1,0:T(8,128)(2,1)}), bf16[4,4,32,768]{3,2,1,0:T(8,128)(2,1)}, u32[]{:S(2)}, u32[]{:S(2)}) %all-to-all-start.4) | async-done | bytes 786464 | tf_op jit(solution)/shard_map/all_to_all | solution.py:350
  534.8 4.5 all-to-all-start.5
  539.4 4.5 add_convert_fusion.1
  551.6 17.4 %all-to-all-done.5 = bf16[4,400,768]{2,1,0:T(8,128)(2,1)} async-done(((bf16[4,400,768]{2,1,0:T(8,128)(2,1)}), bf16[4,400,768]{2,1,0:T(8,128)(2,1)}, u32[]{:S(2)}, u32[]{:S(2)}) %all-to-all-start.5) | async-done | bytes 2457632 | tf_op jit(solution)/shard_map/all_to_all | solution.py:350
  (366 shorter events, 156.4 us)
Async XLA Ops:
  7.2 157.8 %all-gather.5.cloned.1.call-start = ((), (), s32[]{:S(2)}) async-start(), calls=%async_computation.9 | async-start | bytes 10948608 | tf_op jit(solution)/shard_map/all_gather | solution.py:698
  13.8 36.8 %all-to-all-start = ((bf16[8,3,24,768]{3,2,1,0:T(8,128)(2,1)}), bf16[8,3,24,768]{3,2,1,0:T(8,128)(2,1)}, u32[]{:S(2)}, u32[]{:S(2)}) async-start(bf16[8,3,24,768]{3,2,1,0:T(8,128)(2,1)} %broadcast_in_dim.22), calls=%async_computation | async-start | bytes 1769472 | tf_op jit(solution)/shard_map/all_to_all | solution.py:355
  22.9 10.4 %collective-permute-start.1 = (bf16[2,128,768]{1,2,0:T(8,128)(2,1)}, bf16[2,128,768]{1,2,0:T(8,128)(2,1)S(1)}, u32[]{:S(2)}, u32[]{:S(2)}) collective-permute-start(bf16[2,128,768]{1,2,0:T(8,128)(2,1)} %get-tuple-element.240), channel_id=1, source_target_pairs={{0,8},{8,16},{16,24},{1,9},{9,17},{17,25},{2,10},{10,18},{18,26},{... | collective-permute-start | bytes 1179656 | tf_op jit(solution)/shard_map/ppermute | solution.py:676
  24.5 8.8 %collective-permute-start.2 = (bf16[2,128,768]{1,2,0:T(8,128)(2,1)}, bf16[2,128,768]{1,2,0:T(8,128)(2,1)}, u32[]{:S(2)}, u32[]{:S(2)}) collective-permute-start(bf16[2,128,768]{1,2,0:T(8,128)(2,1)} %get-tuple-element.241), channel_id=1, source_target_pairs={{8,0},{16,8},{24,16},{9,1},{17,9},{25,17},{10,2},{18,10},{26,18},{... | collective-permute-start | bytes 1179656 | tf_op jit(solution)/shard_map/ppermute | solution.py:679
  51.9 29.4 %collective-permute-start = (bf16[3,8,24,768]{3,2,1,0:T(8,128)(2,1)S(1)}, bf16[3,8,24,768]{3,2,1,0:T(8,128)(2,1)S(1)}, u32[]{:S(2)}, u32[]{:S(2)}) collective-permute-start(bf16[3,8,24,768]{3,2,1,0:T(8,128)(2,1)S(1)} %bitcast.390), channel_id=1, source_target_pairs={{0,16},{8,24},{16,0},{24,8},{1,17},{9,25},{17,1},{25,9},{2,18},{10... | collective-permute-start | bytes 2654216 | tf_op jit(solution)/shard_map/ppermute | solution.py:346
  82.8 7.5 %collective-permute-start.3 = (bf16[3,2,8,24,768]{4,3,2,1,0:T(8,128)(2,1)}, bf16[3,2,8,24,768]{4,3,2,1,0:T(8,128)(2,1)}, u32[]{:S(2)}, u32[]{:S(2)}) collective-permute-start(bf16[3,2,8,24,768]{4,3,2,1,0:T(8,128)(2,1)} %maximum_select_fusion.1), channel_id=1, source_target_pairs={{0,8},{8,0},{16,24},{24,16},{1,9},{9,1},{17,25},{25,17},{2,10},{10... | collective-permute-start | bytes 5308424 | tf_op jit(solution)/shard_map/ppermute | solution.py:346
  82.8 41.7 %all-to-all-start.1 = ((bf16[4,288,768]{2,1,0:T(8,128)(2,1)}), bf16[4,288,768]{2,1,0:T(8,128)(2,1)}, u32[]{:S(2)}, u32[]{:S(2)}) async-start(bf16[4,288,768]{2,1,0:T(8,128)(2,1)} %broadcast_dynamic-update-slice_fusion), calls=%async_computation.1 | async-start | bytes 3538944 | tf_op jit(solution)/shard_map/all_to_all | solution.py:350
  87.3 160.6 %all-gather.9.cloned.1.call-start = ((), (), s32[]{:S(2)}) async-start(), calls=%async_computation.11 | async-start | bytes 7962624 | tf_op jit(solution)/shard_map/all_gather | solution.py:750
  95.1 43.7 %copy-start.20 = (bf16[1,2,2,8,24,768]{5,4,3,2,1,0:T(8,128)(2,1)}, bf16[1,2,2,8,24,768]{5,4,3,2,1,0:T(8,128)(2,1)S(1)}, u32[]{:S(2)}) copy-start(bf16[1,2,2,8,24,768]{5,4,3,2,1,0:T(8,128)(2,1)S(1)} %get-tuple-element.226) | copy-start | bytes 3538948
  98.7 28.1 %slice-start.3 = ((f32[12,768]{1,0:T(8,128)}), f32[4,768]{1,0:T(4,128)S(1)}, s32[]{:S(2)}) async-start(f32[12,768]{1,0:T(8,128)} %param.26), calls=%async_computation.15 | async-start | bytes 24576 | tf_op jit(solution)/shard_map/slice | solution.py:731
  126.7 359.3 %all-gather.7.cloned.1.call-start = ((), (), s32[]{:S(2)}) async-start(), calls=%async_computation.10 | async-start | bytes 2654208 | tf_op jit(solution)/shard_map/all_gather | solution.py:905
  142.3 22.8 %copy-start.62 = (f32[768]{0:T(1024)S(1)}, f32[768]{0:T(1024)}, u32[]{:S(2)}) copy-start(f32[768]{0:T(1024)} %get-tuple-element.198) | copy-start | bytes 9220
  170.8 38.7 %copy-start.18 = (bf16[1024,768]{1,0:T(8,128)(2,1)S(1)}, bf16[1024,768]{1,0:T(8,128)(2,1)}, u32[]{:S(2)}) copy-start(bf16[1024,768]{1,0:T(8,128)(2,1)} %add_convert_fusion.3.rows_ref) | copy-start | bytes 4718596
  209.4 10.0 %copy-start.7 = (bf16[2,512,768]{2,1,0:T(8,128)(2,1)S(1)}, bf16[2,512,768]{2,1,0:T(8,128)(2,1)}, u32[]{:S(2)}) copy-start(bf16[2,512,768]{2,1,0:T(8,128)(2,1)} %param.24) | copy-start | bytes 4718596
  209.5 10.0 %copy-start.65 = (bf16[1024,3072]{1,0:T(8,128)(2,1)S(1)}, bf16[1024,3072]{1,0:T(8,128)(2,1)}, u32[]{:S(2)}) copy-start(bf16[1024,3072]{1,0:T(8,128)(2,1)} %get-tuple-element.51) | copy-start | bytes 18874372
  234.0 30.2 %collective-permute-start.4 = (bf16[4,2,2,2,2,24,768]{6,5,0,2,3,4,1:T(8,128)(2,1)}, bf16[4,2,2,2,2,24,768]{6,5,0,2,3,4,1:T(8,128)(2,1)}, u32[]{:S(2)}, u32[]{:S(2)}) collective-permute-start(bf16[4,2,2,2,2,24,768]{6,5,0,2,3,4,1:T(8,128)(2,1)} %bitcast.361), channel_id=1, source_target_pairs={{0,8},{8,0},{16,24},{24,16},{1,9},{9,1},{17,25},{25,17},{2,10},{10... | collective-permute-start | bytes 7077896 | tf_op jit(solution)/shard_map/ppermute | solution.py:346
  251.2 17.8 %collective-permute-start.5 = (bf16[4,2,2,2,2,24,768]{6,5,0,1,2,3,4:T(8,128)(2,1)S(1)}, bf16[4,2,2,2,2,24,768]{6,5,0,1,2,3,4:T(8,128)(2,1)S(1)}, u32[]{:S(2)}, u32[]{:S(2)}) collective-permute-start(bf16[4,2,2,2,2,24,768]{6,5,0,1,2,3,4:T(8,128)(2,1)S(1)} %bitcast.398), channel_id=1, source_target_pairs={{0,8},{8,0},{16,24},{24,16},{1,9},{9,1},{17,25},{25,17},{2,10},{10... | collective-permute-start | bytes 7077896 | tf_op jit(solution)/shard_map/ppermute | solution.py:346
  267.6 31.0 %collective-permute-start.6 = (bf16[4,2,2,2,24,768]{5,4,0,1,2,3:T(8,128)(2,1)}, bf16[4,2,2,2,24,768]{5,4,0,1,2,3:T(8,128)(2,1)}, u32[]{:S(2)}, u32[]{:S(2)}) collective-permute-start(bf16[4,2,2,2,24,768]{5,4,0,1,2,3:T(8,128)(2,1)} %dynamic-slice_bitcast_fusion.1), channel_id=1, source_target_pairs={{0,16},{8,24},{16,0},{24,8},{1,17},{9,25},{17,1},{25,9},{2,18},{10... | collective-permute-start | bytes 3538952 | tf_op jit(solution)/shard_map/ppermute | solution.py:346
  271.9 29.3 %collective-permute-start.7 = (bf16[4,2,2,2,24,768]{5,4,0,1,2,3:T(8,128)(2,1)}, bf16[4,2,2,2,24,768]{5,4,0,1,2,3:T(8,128)(2,1)}, u32[]{:S(2)}, u32[]{:S(2)}) collective-permute-start(bf16[4,2,2,2,24,768]{5,4,0,1,2,3:T(8,128)(2,1)} %dynamic-slice_bitcast_fusion), channel_id=1, source_target_pairs={{0,1},{1,0},{2,3},{3,2},{4,5},{5,4},{6,7},{7,6},{8,9},{9,8},{10,11... | collective-permute-start | bytes 3538952 | tf_op jit(solution)/shard_map/ppermute | solution.py:346
  315.3 20.9 %collective-permute-start.9 = (bf16[2,2,128,768]{3,2,1,0:T(8,128)(2,1)S(1)}, bf16[2,2,128,768]{3,2,1,0:T(8,128)(2,1)S(1)}, u32[]{:S(2)}, u32[]{:S(2)}) collective-permute-start(bf16[2,2,128,768]{3,2,1,0:T(8,128)(2,1)S(1)} %get-tuple-element.221), channel_id=1, source_target_pairs={{8,0},{16,8},{24,16},{9,1},{17,9},{25,17},{10,2},{18,10},{26,18},{... | collective-permute-start | bytes 2359304 | tf_op jit(solution)/shard_map/ppermute | solution.py:821
  316.8 16.1 %collective-permute-start.12 = (bf16[4,2,2,24,768]{4,3,0,1,2:T(8,128)(2,1)S(1)}, bf16[4,2,2,24,768]{4,3,0,1,2:T(8,128)(2,1)S(1)}, u32[]{:S(2)}, u32[]{:S(2)}) collective-permute-start(bf16[4,2,2,24,768]{4,3,0,1,2:T(8,128)(2,1)S(1)} %copy-done.46), channel_id=1, source_target_pairs={{0,1},{1,0},{2,3},{3,2},{4,5},{5,4},{6,7},{7,6},{8,9},{9,8},{10,11... | collective-permute-start | bytes 1769480 | tf_op jit(solution)/shard_map/ppermute | solution.py:346
  318.3 16.1 %collective-permute-start.15 = (bf16[4,2,2,24,768]{4,3,0,1,2:T(8,128)(2,1)S(1)}, bf16[4,2,2,24,768]{4,3,0,1,2:T(8,128)(2,1)S(1)}, u32[]{:S(2)}, u32[]{:S(2)}) collective-permute-start(bf16[4,2,2,24,768]{4,3,0,1,2:T(8,128)(2,1)S(1)} %dynamic-slice_bitcast_fusion.3), channel_id=1, source_target_pairs={{0,2},{1,3},{2,0},{3,1},{4,6},{5,7},{6,4},{7,5},{8,10},{9,11},{10,... | collective-permute-start | bytes 1769480 | tf_op jit(solution)/shard_map/ppermute | solution.py:346
  321.6 11.3 %copy-start.15 = (bf16[4,2,2,2,24,768]{5,4,0,1,2,3:T(8,128)(2,1)S(1)}, bf16[4,2,2,2,24,768]{5,4,0,1,2,3:T(8,128)(2,1)}, u32[]{:S(2)}) copy-start(bf16[4,2,2,2,24,768]{5,4,0,1,2,3:T(8,128)(2,1)} %copy-done.14) | copy-start | bytes 3538948
  321.6 14.7 %collective-permute-start.8 = (bf16[2,2,128,768]{3,2,1,0:T(8,128)(2,1)S(1)}, bf16[2,2,128,768]{3,2,1,0:T(8,128)(2,1)S(1)}, u32[]{:S(2)}, u32[]{:S(2)}) collective-permute-start(bf16[2,2,128,768]{3,2,1,0:T(8,128)(2,1)S(1)} %get-tuple-element.220), channel_id=1, source_target_pairs={{0,8},{8,16},{16,24},{1,9},{9,17},{17,25},{2,10},{10,18},{18,26},{... | collective-permute-start | bytes 2359304 | tf_op jit(solution)/shard_map/ppermute | solution.py:824
  333.1 19.0 %collective-permute-start.13 = (bf16[4,2,24,768]{3,2,0,1:T(8,128)(2,1)S(1)}, bf16[4,2,24,768]{3,2,0,1:T(8,128)(2,1)S(1)}, u32[]{:S(2)}, u32[]{:S(2)}) collective-permute-start(bf16[4,2,24,768]{3,2,0,1:T(8,128)(2,1)S(1)} %dynamic-slice_bitcast_fusion.9), channel_id=1, source_target_pairs={{0,2},{1,3},{2,0},{3,1},{4,6},{5,7},{6,4},{7,5},{8,10},{9,11},{10,... | collective-permute-start | bytes 884744 | tf_op jit(solution)/shard_map/ppermute | solution.py:346
  334.7 16.2 %collective-permute-start.16 = (bf16[4,2,24,768]{3,2,0,1:T(8,128)(2,1)S(1)}, bf16[4,2,24,768]{3,2,0,1:T(8,128)(2,1)S(1)}, u32[]{:S(2)}, u32[]{:S(2)}) collective-permute-start(bf16[4,2,24,768]{3,2,0,1:T(8,128)(2,1)S(1)} %dynamic-slice_bitcast_fusion.8), channel_id=1, source_target_pairs={{0,4},{1,5},{2,6},{3,7},{4,0},{5,1},{6,2},{7,3},{8,12},{9,13},{10,... | collective-permute-start | bytes 884744 | tf_op jit(solution)/shard_map/ppermute | solution.py:346
  344.2 16.8 %collective-permute-start.10 = (bf16[2,2,2,2,2,2,24,768]{7,6,2,0,3,4,5,1:T(8,128)(2,1)S(1)}, bf16[2,2,2,2,2,2,24,768]{7,6,2,0,3,4,5,1:T(8,128)(2,1)S(1)}, u32[]{:S(2)}, u32[]{:S(2)}) collective-permute-start(bf16[2,2,2,2,2,2,24,768]{7,6,2,0,3,4,5,1:T(8,128)(2,1)S(1)} %bitcast.397), channel_id=1, source_target_pairs={{0,8},{8,0},{16,24},{24,16},{1,9},{9,1},{17,25},{25,17},{2,10},{10... | collective-permute-start | bytes 7077896 | tf_op jit(solution)/shard_map/ppermute | solution.py:346
  351.0 5.2 collective-permute-start.17
  352.2 8.1 %collective-permute-start.14 = (bf16[4,24,768]{2,1,0:T(8,128)(2,1)S(1)}, bf16[4,24,768]{2,1,0:T(8,128)(2,1)S(1)}, u32[]{:S(2)}, u32[]{:S(2)}) collective-permute-start(bf16[4,24,768]{2,1,0:T(8,128)(2,1)S(1)} %dynamic-slice_bitcast_fusion.13), channel_id=1, source_target_pairs={{0,4},{1,5},{2,6},{3,7},{4,0},{5,1},{6,2},{7,3},{8,12},{9,13},{10,... | collective-permute-start | bytes 442376 | tf_op jit(solution)/shard_map/ppermute | solution.py:346
  361.9 16.5 %copy-start.22 = (bf16[2,1,2,2,2,2,24,768]{7,6,2,0,3,4,5,1:T(8,128)(2,1)}, bf16[2,1,2,2,2,2,24,768]{7,6,2,0,3,4,5,1:T(8,128)(2,1)S(1)}, u32[]{:S(2)}) copy-start(bf16[2,1,2,2,2,2,24,768]{7,6,2,0,3,4,5,1:T(8,128)(2,1)S(1)} %get-tuple-element.237) | copy-start | bytes 3538948
  361.9 14.8 %collective-permute-start.11 = (bf16[2,2,2,2,24,768]{5,4,0,1,2,3:T(8,128)(2,1)S(1)}, bf16[2,2,2,2,24,768]{5,4,0,1,2,3:T(8,128)(2,1)S(1)}, u32[]{:S(2)}, u32[]{:S(2)}) collective-permute-start(bf16[2,2,2,2,24,768]{5,4,0,1,2,3:T(8,128)(2,1)S(1)} %dynamic-slice_bitcast_fusion.5), channel_id=1, source_target_pairs={{0,16},{8,24},{16,0},{24,8},{1,17},{9,25},{17,1},{25,9},{2,18},{10... | collective-permute-start | bytes 1769480 | tf_op jit(solution)/shard_map/ppermute | solution.py:346
  363.7 17.2 %collective-permute-start.21 = (bf16[2,2,2,2,24,768]{5,4,1,0,2,3:T(8,128)(2,1)}, bf16[2,2,2,2,24,768]{5,4,1,0,2,3:T(8,128)(2,1)}, u32[]{:S(2)}, u32[]{:S(2)}) collective-permute-start(bf16[2,2,2,2,24,768]{5,4,1,0,2,3:T(8,128)(2,1)} %dynamic-slice_bitcast_fusion.2), channel_id=1, source_target_pairs={{0,1},{1,0},{2,3},{3,2},{4,5},{5,4},{6,7},{7,6},{8,9},{9,8},{10,11... | collective-permute-start | bytes 1769480 | tf_op jit(solution)/shard_map/ppermute | solution.py:346
  378.4 7.9 %collective-permute-start.18 = (bf16[2,2,2,24,768]{4,3,0,1,2:T(8,128)(2,1)}, bf16[2,2,2,24,768]{4,3,0,1,2:T(8,128)(2,1)}, u32[]{:S(2)}, u32[]{:S(2)}) collective-permute-start(bf16[2,2,2,24,768]{4,3,0,1,2:T(8,128)(2,1)} %dynamic-slice_bitcast_fusion.7), channel_id=1, source_target_pairs={{0,1},{1,0},{2,3},{3,2},{4,5},{5,4},{6,7},{7,6},{8,9},{9,8},{10,11... | collective-permute-start | bytes 884744 | tf_op jit(solution)/shard_map/ppermute | solution.py:346
  387.4 46.3 %copy-start.24 = (bf16[2,96,768]{2,1,0:T(8,128)(2,1)S(1)}, bf16[2,96,768]{2,1,0:T(8,128)(2,1)}, u32[]{:S(2)}) copy-start(bf16[2,96,768]{2,1,0:T(8,128)(2,1)} %pad_maximum_fusion.7) | copy-start | bytes 884740
  387.4 9.0 %collective-permute-start.19 = (bf16[2,2,24,768]{3,2,0,1:T(8,128)(2,1)S(1)}, bf16[2,2,24,768]{3,2,0,1:T(8,128)(2,1)S(1)}, u32[]{:S(2)}, u32[]{:S(2)}) collective-permute-start(bf16[2,2,24,768]{3,2,0,1:T(8,128)(2,1)S(1)} %dynamic-slice_bitcast_fusion.11), channel_id=1, source_target_pairs={{0,2},{1,3},{2,0},{3,1},{4,6},{5,7},{6,4},{7,5},{8,10},{9,11},{10,... | collective-permute-start | bytes 442376 | tf_op jit(solution)/shard_map/ppermute | solution.py:346
  389.4 12.4 %copy-start.27 = (bf16[2,2,2,2,24,768]{5,4,1,0,2,3:T(8,128)(2,1)}, bf16[2,2,2,2,24,768]{5,4,1,0,2,3:T(8,128)(2,1)S(1)}, u32[]{:S(2)}) copy-start(bf16[2,2,2,2,24,768]{5,4,1,0,2,3:T(8,128)(2,1)S(1)} %fusion.26) | copy-start | bytes 1769476
  396.5 9.4 %collective-permute-start.20 = (bf16[2,24,768]{2,1,0:T(8,128)(2,1)S(1)}, bf16[2,24,768]{2,1,0:T(8,128)(2,1)S(1)}, u32[]{:S(2)}, u32[]{:S(2)}) collective-permute-start(bf16[2,24,768]{2,1,0:T(8,128)(2,1)S(1)} %dynamic-slice_bitcast_fusion.15), channel_id=1, source_target_pairs={{0,4},{1,5},{2,6},{3,7},{4,0},{5,1},{6,2},{7,3},{8,12},{9,13},{10,... | collective-permute-start | bytes 221192 | tf_op jit(solution)/shard_map/ppermute | solution.py:346
  402.5 13.3 %collective-permute-start.22 = (bf16[2,2,2,24,768]{4,3,1,0,2:T(8,128)(2,1)}, bf16[2,2,2,24,768]{4,3,1,0,2:T(8,128)(2,1)}, u32[]{:S(2)}, u32[]{:S(2)}) collective-permute-start(bf16[2,2,2,24,768]{4,3,1,0,2:T(8,128)(2,1)} %dynamic-slice_bitcast_fusion.6), channel_id=1, source_target_pairs={{0,2},{1,3},{2,0},{3,1},{4,6},{5,7},{6,4},{7,5},{8,10},{9,11},{10,... | collective-permute-start | bytes 884744 | tf_op jit(solution)/shard_map/ppermute | solution.py:346
  407.9 25.8 %all-to-all-start.7 = ((f32[8,12,768]{2,1,0:T(8,128)}), f32[8,12,768]{2,1,0:T(8,128)}, u32[]{:S(2)}, u32[]{:S(2)}) async-start(f32[8,12,768]{2,1,0:T(8,128)} %broadcast_in_dim.31), calls=%async_computation.7 | async-start | bytes 786432 | tf_op jit(solution)/shard_map/all_to_all | solution.py:355
  434.8 27.6 %copy-start.32 = (f32[2,24,768]{2,1,0:T(8,128)S(1)}, f32[2,24,768]{2,1,0:T(8,128)}, u32[]{:S(2)}) copy-start(f32[2,24,768]{2,1,0:T(8,128)} %copy-done.31) | copy-start | bytes 442372
  434.8 22.9 %all-to-all-start.3 = ((bf16[4,2,96,768]{3,2,1,0:T(8,128)(2,1)}), bf16[4,2,96,768]{3,2,1,0:T(8,128)(2,1)}, u32[]{:S(2)}, u32[]{:S(2)}) async-start(bf16[4,2,96,768]{3,2,1,0:T(8,128)(2,1)} %broadcast_in_dim.30), calls=%async_computation.3 | async-start | bytes 2359296 | tf_op jit(solution)/shard_map/all_to_all | solution.py:355
  440.2 8.8 %collective-permute-start.23 = (bf16[2,2,24,768]{3,2,1,0:T(8,128)(2,1)S(1)}, bf16[2,2,24,768]{3,2,1,0:T(8,128)(2,1)S(1)}, u32[]{:S(2)}, u32[]{:S(2)}) collective-permute-start(bf16[2,2,24,768]{3,2,1,0:T(8,128)(2,1)S(1)} %dynamic-slice_bitcast_fusion.10), channel_id=1, source_target_pairs={{0,4},{1,5},{2,6},{3,7},{4,0},{5,1},{6,2},{7,3},{8,12},{9,13},{10,... | collective-permute-start | bytes 442376 | tf_op jit(solution)/shard_map/ppermute | solution.py:346
  450.0 6.7 %collective-permute-start.24 = (bf16[2,24,768]{2,1,0:T(8,128)(2,1)S(1)}, bf16[2,24,768]{2,1,0:T(8,128)(2,1)S(1)}, u32[]{:S(2)}, u32[]{:S(2)}) collective-permute-start(bf16[2,24,768]{2,1,0:T(8,128)(2,1)S(1)} %dynamic-slice_bitcast_fusion.14), channel_id=1, source_target_pairs={{0,16},{8,24},{16,0},{24,8},{1,17},{9,25},{17,1},{25,9},{2,18},{10... | collective-permute-start | bytes 221192 | tf_op jit(solution)/shard_map/ppermute | solution.py:346
  458.4 9.4 %all-to-all-start.8 = ((f32[4,12,768]{2,1,0:T(8,128)}), f32[4,12,768]{2,1,0:T(8,128)}, u32[]{:S(2)}, u32[]{:S(2)}) async-start(f32[4,12,768]{2,1,0:T(8,128)} %broadcast_in_dim.32), calls=%async_computation.8 | async-start | bytes 393216 | tf_op jit(solution)/shard_map/all_to_all | solution.py:355
  469.8 33.2 %all-to-all-start.2 = ((bf16[8,4,24,768]{3,2,1,0:T(8,128)(2,1)}), bf16[8,4,24,768]{3,2,1,0:T(8,128)(2,1)}, u32[]{:S(2)}, u32[]{:S(2)}) async-start(bf16[8,4,24,768]{3,2,1,0:T(8,128)(2,1)} %broadcast_in_dim.29), calls=%async_computation.2 | async-start | bytes 2359296 | tf_op jit(solution)/shard_map/all_to_all | solution.py:355
  503.0 15.9 %all-to-all-start.6 = ((bf16[4,4,32,768]{3,2,1,0:T(8,128)(2,1)}), bf16[4,4,32,768]{3,2,1,0:T(8,128)(2,1)}, u32[]{:S(2)}, u32[]{:S(2)}) async-start(bf16[4,4,32,768]{3,2,1,0:T(8,128)(2,1)} %get-tuple-element.63), calls=%async_computation.6 | async-start | bytes 1572864 | tf_op jit(solution)/shard_map/all_to_all | solution.py:350
  518.9 15.9 %all-to-all-start.4 = ((bf16[4,4,32,768]{3,2,1,0:T(8,128)(2,1)}), bf16[4,4,32,768]{3,2,1,0:T(8,128)(2,1)}, u32[]{:S(2)}, u32[]{:S(2)}) async-start(bf16[4,4,32,768]{3,2,1,0:T(8,128)(2,1)} %attend_update.1), calls=%async_computation.4 | async-start | bytes 1572864 | tf_op jit(solution)/shard_map/all_to_all | solution.py:350
  534.8 34.1 %all-to-all-start.5 = ((bf16[4,400,768]{2,1,0:T(8,128)(2,1)}), bf16[4,400,768]{2,1,0:T(8,128)(2,1)}, u32[]{:S(2)}, u32[]{:S(2)}) async-start(bf16[4,400,768]{2,1,0:T(8,128)(2,1)} %get-tuple-element.62), calls=%async_computation.5 | async-start | bytes 4915200 | tf_op jit(solution)/shard_map/all_to_all | solution.py:350
  (59 other events, 200.1 us)
Sparse Core Ops, SparseCore 0:
  12.9 124.2 all-gather.4
  140.0 107.8 all-gather.8
  381.0 59.6 all-gather.6

commit v3 on v2

--- a/solution.py
+++ b/solution.py
@@ -92,20 +92,30 @@
     def _():
         write_mask(bias_ref, lengths[text], base[0], blocks)
 
-    for i in range(blocks):
-        keys = k_ref[0, i * WIN : i * WIN + KEYS, :]
-        values = v_ref[0, i * WIN : i * WIN + KEYS, :]
-        queries = stacked(q_ref[0, i * WIN : (i + 1) * WIN, :], 0.125)
+    def window(ref, i):
+        return ref[0, i * WIN : i * WIN + KEYS, :]
+
+    def own(i):
+        return slice(i * WIN, (i + 1) * WIN)
+
+    every = range(blocks)
+    scores = [nt(window(k_ref, i), stacked(q_ref[0, own(i), :], 0.125)) for i in every]
+    weights = []
+    totals = []
+    for i in every:
         bias = bias_ref[i]
-        scores = nt(keys, queries) + jnp.concatenate([bias, bias], axis=1)
-        peak = jnp.max(scores, axis=0, keepdims=True)
-        weights = jnp.exp(scores - peak)
-        total = jnp.sum(weights, axis=0, keepdims=True)
-        mixed = across(values, low(weights)) * (1.0 / total)
-        o_ref[0, i * WIN : (i + 1) * WIN, :] = low(unstacked(mixed))
+        masked = scores[i] + jnp.concatenate([bias, bias], axis=1)
+        peak = jnp.max(masked, axis=0, keepdims=True)
+        weight = jnp.exp(masked - peak)
+        total = jnp.sum(weight, axis=0, keepdims=True)
+        weights.append(low(weight))
+        totals.append(1.0 / total)
         log_total = peak + jnp.log(total)
         total_ref[0, 0, 2 * i : 2 * i + 1, :] = log_total[:, :WIN]
         total_ref[0, 0, 2 * i + 1 : 2 * i + 2, :] = log_total[:, WIN:]
+    mixed = [across(window(v_ref, i), weights[i]) for i in every]
+    for i in every:
+        o_ref[0, own(i), :] = low(unstacked(mixed[i] * totals[i]))
 
 
 def attend_backward(
@@ -127,28 +137,39 @@
     def _():
         write_mask(bias_ref, lengths[text], base[0], blocks)
 
-    dk_sum[...] = jnp.zeros_like(dk_sum)
-    dv_sum[...] = jnp.zeros_like(dv_sum)
-    for i in range(blocks):
-        window = slice(i * WIN, i * WIN + KEYS)
-        own = slice(i * WIN, (i + 1) * WIN)
-        keys = k_ref[0, window, :]
-        values = v_ref[0, window, :]
-        queries = stacked(q_ref[0, own, :], 0.125)
-        upstream = stacked(up_ref[0, own, :], 1.0)
+    def window(i):
+        return slice(i * WIN, i * WIN + KEYS)
+
+    def own(i):
+        return slice(i * WIN, (i + 1) * WIN)
+
+    every = range(blocks)
+    queries = [stacked(q_ref[0, own(i), :], 0.125) for i in every]
+    upstream = [stacked(up_ref[0, own(i), :], 1.0) for i in every]
+    scores = [nt(k_ref[0, window(i), :], queries[i]) for i in every]
+    weight_grads = [nt(v_ref[0, window(i), :], upstream[i]) for i in every]
+    weights = []
+    score_grads = []
+    for i in every:
         bias = bias_ref[i]
         log_total = jnp.concatenate(
             [total_ref[0, 0, 2 * i : 2 * i + 1, :], total_ref[0, 0, 2 * i + 1 : 2 * i + 2, :]],
             axis=1,
         )
-        scores = nt(keys, queries) + jnp.concatenate([bias, bias], axis=1)
-        weights = jnp.exp(scores - log_total)
-        weight_grad = nt(values, upstream)
-        product = weights * weight_grad
-        score_grad = low(product - weights * jnp.sum(product, axis=0, keepdims=True))
-        dv_sum[window, :] += nn(low(weights), upstream)
-        dk_sum[window, :] += nn(score_grad, queries)
-        dq_ref[0, own, :] = low(unstacked(across(keys, score_grad)) * 0.125)
+        weight = jnp.exp(scores[i] + jnp.concatenate([bias, bias], axis=1) - log_total)
+        product = weight * weight_grads[i]
+        score_grads.append(
+            low(product - weight * jnp.sum(product, axis=0, keepdims=True))
+        )
+        weights.append(low(weight))
+    dk_sum[...] = jnp.zeros_like(dk_sum)
+    dv_sum[...] = jnp.zeros_like(dv_sum)
+    for i in every:
+        dv_sum[window(i), :] += nn(weights[i], upstream[i])
+        dk_sum[window(i), :] += nn(score_grads[i], queries[i])
+    turned = [across(k_ref[0, window(i), :], score_grads[i]) for i in every]
+    for i in every:
+        dq_ref[0, own(i), :] = low(unstacked(turned[i]) * 0.125)
     dk_ref[0] = low(dk_sum[...])
     dv_ref[0] = low(dv_sum[...])
 
@@ -225,7 +246,7 @@
     )(lengths, base, query, key_ext, value_ext, upstream, totals, *others)
 
 
-GATE_ROWS = 256
+GATE_ROWS = 512
 GATE_COLS = 256
 GATE_SLAB = 32
 BELL = 1.0 / math.sqrt(2.0 * math.pi)
@@ -429,13 +450,15 @@
     return low(rows)
 
 
-def hidden_first(seq_count, block, dp_count, dp_index, panels, row_sets, expand_rc, shrink_rc, expand_lw):
+def hidden_products(
+    seq_count, block, dp_count, dp_index, panels, row_sets, expand_rc, expand_lw, shrink_lr, shrink_rt
+):
     shrink, expand = panels[0], panels[1]
     width = shrink.shape[0]
     pick = picker(seq_count, block, dp_count, dp_index, width)
     shrink_cols = low(nt(pick, shrink))
     expand_cols = nt(pick, expand)
-    turned = low(nt(shrink_rc, shrink))
+    turned = low(nt(shrink_rt, low(nn(shrink_lr, shrink))))
     shrink_right = nn(shrink_cols, shrink)
     expand_left = nn(low(expand_cols), expand)
     expand_turned = nt(low(nn(expand_rc, expand)), expand_lw)
@@ -469,11 +492,6 @@
     return pieces, turned
 
 
-def direction_rows(seq_count, block, turned, shrink_lw):
-    rows = nt(turned, shrink_lw)
-    return [rows[s * block : (s + 1) * block] for s in range(seq_count)]
-
-
 def hidden_kernel(
     seq_count,
     block,
@@ -482,86 +500,73 @@
     panels_ref,
     rows_ref,
     expand_rc_ref,
-    shrink_rc_ref,
     expand_lw_ref,
-    shrink_lw_ref,
+    shrink_lr_ref,
+    shrink_rt_ref,
     token_ref,
     out_ref,
     turn_ref,
-    turned_ref,
 ):
-    step = pl.program_id(0)
-
-    @pl.when(step == 0)
-    def _():
-        pieces, turned = hidden_first(
-            seq_count,
-            block,
-            dp_count,
-            index_ref[0],
-            panels_ref,
-            rows_ref,
-            expand_rc_ref[...],
-            shrink_rc_ref[...],
-            expand_lw_ref[...],
-        )
-        turned_ref[...] = turned
-        for s in range(seq_count):
-            start = 0
-            for piece in pieces[s]:
-                out_ref[s, start : start + piece.shape[0], :] = piece
-                start += piece.shape[0]
-
-    for s, rows in enumerate(direction_rows(seq_count, block, turned_ref[...], shrink_lw_ref[0])):
-        turn_ref[s, 0] = padded(rows)
-
-
-def run_hidden(seq_count, block, dp_count, dp_index, panels, row_sets, rc, shrink_rc, lw, shrink_lw, token):
+    pieces, turned = hidden_products(
+        seq_count,
+        block,
+        dp_count,
+        index_ref[0],
+        panels_ref,
+        rows_ref,
+        expand_rc_ref[...],
+        expand_lw_ref[...],
+        shrink_lr_ref[...],
+        shrink_rt_ref[...],
+    )
+    turn_ref[...] = turned
+    for s in range(seq_count):
+        start = 0
+        for piece in pieces[s]:
+            out_ref[s, start : start + piece.shape[0], :] = piece
+            start += piece.shape[0]
+
+
+def run_hidden(seq_count, block, dp_count, dp_index, panels, row_sets, rc, lw, lr, rt, token):
     width = panels.shape[1]
-    groups = shrink_lw.shape[0]
     owned = rc.shape[0] // seq_count
     if owned % 16 or block % 8:
-        pieces, turned = hidden_first(
-            seq_count, block, dp_count, dp_index, panels, row_sets, rc, shrink_rc, lw
+        pieces, turned = hidden_products(
+            seq_count, block, dp_count, dp_index, panels, row_sets, rc, lw, lr, rt
         )
-        turns = [direction_rows(seq_count, block, turned, shrink_lw[i]) for i in range(groups)]
-        return (
-            jnp.stack([jnp.concatenate(piece) for piece in pieces]),
-            jnp.stack(
-                [jnp.stack([padded(turns[i][s]) for i in range(groups)]) for s in range(seq_count)]
-            ),
-        )
+        return jnp.stack([jnp.concatenate(piece) for piece in pieces]), turned
     few = block + -block % 16
     rows_out = 3 * owned + 3 * few + 16
-    whole = lambda array: pl.BlockSpec(array.shape, lambda i: (0,) * array.ndim)
+    vmem = pl.BlockSpec(memory_space=pltpu.VMEM)
     return pl.pallas_call(
         functools.partial(hidden_kernel, seq_count, block, dp_count),
-        grid=(groups,),
-        in_specs=[
-            pl.BlockSpec(memory_space=pltpu.SMEM),
-            whole(panels),
-            whole(row_sets),
-            whole(rc),
-            whole(shrink_rc),
-            whole(lw),
-            pl.BlockSpec((1, width, width), lambda i: (i, 0, 0)),
-            pl.BlockSpec(memory_space=pl.ANY),
-        ],
-        out_specs=[
-            pl.BlockSpec((seq_count, rows_out, width), lambda i: (0, 0, 0)),
-            pl.BlockSpec((seq_count, 1, few, width), lambda i: (0, i, 0, 0)),
-        ],
+        in_specs=[pl.BlockSpec(memory_space=pltpu.SMEM)]
+        + [vmem] * 6
+        + [pl.BlockSpec(memory_space=pl.ANY)],
+        out_specs=[vmem, vmem],
         out_shape=[
             jax.ShapeDtypeStruct((seq_count, rows_out, width), jnp.bfloat16),
-            jax.ShapeDtypeStruct((seq_count, groups, few, width), jnp.bfloat16),
+            jax.ShapeDtypeStruct((width, seq_count * owned), jnp.bfloat16),
         ],
-        scratch_shapes=[pltpu.VMEM(shrink_rc.shape, jnp.bfloat16)],
         compiler_params=params(),
         cost_estimate=pl.CostEstimate(
             flops=40 * owned * width * width, bytes_accessed=12 * width * width, transcendentals=0
         ),
         name="hidden_update",
-    )(dp_index.reshape(1), panels, row_sets, rc, shrink_rc, lw, shrink_lw, token)
+    )(dp_index.reshape(1), panels, row_sets, rc, lw, lr, rt, token)
+
+
+def halves_of(values, keep=lambda high: high):
+    extra = 16 - values.shape[0]
+    if extra:
+        values = jnp.concatenate([values, jnp.zeros((extra, values.shape[1]), jnp.float32)])
+    high = keep(low(values))
+    return jnp.concatenate([high, low(values - high.astype(jnp.float32))])
+
+
+def from_halves(parts):
+    total = jnp.sum(parts.astype(jnp.float32), axis=0)
+    return total[:16] + total[16:]
 
 
 def attend_products(seq_count, block, dp_count, dp_index, scale, whole, own, rc, lw):
@@ -580,7 +585,21 @@
     ]
 
 
-def attend_kernel(seq_count, block, dp_count, scale, index_ref, whole_ref, own_ref, rc_ref, lw_ref, token_ref, out_ref):
+def attend_kernel(
+    seq_count,
+    block,
+    dp_count,
+    scale,
+    index_ref,
+    whole_ref,
+    own_ref,
+    rc_ref,
+    lw_ref,
+    vector_ref,
+    token_ref,
+    out_ref,
+):
+    vectors = halves_of(from_halves(vector_ref[...]))
     pieces = attend_products(
         seq_count,
         block,
@@ -595,30 +614,35 @@
     for s in range(seq_count):
         for i, piece in enumerate(pieces[s]):
             out_ref[s, i] = piece
-
-
-def run_attend(seq_count, block, dp_count, dp_index, scale, whole, own, rc, lw, token):
+        out_ref[s, len(pieces[s])] = vectors
+
+
+def run_attend(seq_count, block, dp_count, dp_index, scale, whole, own, rc, lw, vectors, token):
     width = whole.shape[0]
-    if block % 8:
+    few = block + -block % 16
+    if few != 32 or block % 8:
         pieces = attend_products(
             seq_count, block, dp_count, dp_index, scale, whole, own, rc, lw
         )
-        return jnp.stack([jnp.stack(piece) for piece in pieces])
-    few = block + -block % 16
+        sums = halves_of(from_halves(vectors), lax.optimization_barrier)
+        fill = ((0, 32 - few), (0, 0))
+        return jnp.stack(
+            [jnp.stack([jnp.pad(p, fill) for p in piece] + [sums]) for piece in pieces]
+        )
     vmem = pl.BlockSpec(memory_space=pltpu.VMEM)
     return pl.pallas_call(
         functools.partial(attend_kernel, seq_count, block, dp_count, scale),
         in_specs=[pl.BlockSpec(memory_space=pltpu.SMEM)]
-        + [vmem] * 4
+        + [vmem] * 5
         + [pl.BlockSpec(memory_space=pl.ANY)],
         out_specs=vmem,
-        out_shape=jax.ShapeDtypeStruct((seq_count, 4, few, width), jnp.bfloat16),
+        out_shape=jax.ShapeDtypeStruct((seq_count, 5, few, width), jnp.bfloat16),
         compiler_params=params(),
         cost_estimate=pl.CostEstimate(
             flops=10 * own.shape[0] * width * width, bytes_accessed=6 * width * width, transcendentals=0
         ),
         name="attend_update",
-    )(dp_index.reshape(1), whole, own, rc, lw, token)
+    )(dp_index.reshape(1), whole, own, rc, lw, vectors, token)
 
 
 def finish(direction, moment, weight, row_count):
@@ -708,10 +732,10 @@
         [
             panels_of(expand_rootright.T),
             low(attend_rootright.transpose(1, 2, 0)),
-            copies_of(shrink_rootright.T),
             panels_of(shrink_rootleft),
             low(attend_rootleft).transpose(1, 0, 2),
             copies_of(expand_rootleft),
+            copies_of(shrink_rootright.T),
         ],
         axis=1,
     )
@@ -730,12 +754,9 @@
     shrink_bias = vectors[7]
     expand_bias = vectors[8:].reshape(owners, groups, block).transpose(1, 0, 2).reshape(1, -1)
     normed_ext = low(normalize(input_ext.astype(jnp.float32), gain_one, bias_one))
-    over_chip, normed_ext, root_parts = lax.optimization_barrier(
-        (over_chip, normed_ext, root_parts)
-    )
+    over_chip, normed_ext = lax.optimization_barrier((over_chip, normed_ext))
     over_core = ordered(core, over_chip, flip(over_chip, "seq", 1), 2)
     qkv_t = over_core.reshape(3 * model_width, model_width)
-    roots = swap(root_parts)
     normed_low = normed_ext[:, WIN : WIN + block_size].reshape(token_rows, model_width)
     ext_rows = normed_ext.reshape(text_count * wide, model_width)
     query_low = low(nt(normed_low, qkv_t[:model_width]) + query_bias).reshape(characters.shape)
@@ -745,9 +766,7 @@
     value_ext = low(nt(ext_rows, qkv_t[2 * model_width :]) + value_bias).reshape(
         text_count, wide, model_width
     )
-    query_low, roots = lax.optimization_barrier((query_low, roots))
-    cut = hidden_block + 2 * block
-    root_all = lax.all_gather(roots[:, cut:], "dp", axis=1)
+    roots = swap(after(root_parts, mark(query_low)))
     base = (seq_index * block_size).astype(jnp.int32).reshape(1)
     attended, totals = run_forward(lengths, base, query_low, key_ext, value_ext)
     attended_low = attended.reshape(token_rows, model_width)
@@ -756,6 +775,9 @@
     layer_input = characters.astype(jnp.float32).reshape(token_rows, model_width)
     middle = layer_input + nt(attended_low, out_t) + out_bias
     normed_two_low = low(normalize(middle, gain_two, bias_two))
+    normed_two_low, roots = lax.optimization_barrier((normed_two_low, roots))
+    cut = 2 * hidden_block + block
+    root_all = lax.all_gather(roots[:, cut:], "dp", axis=1)
     upstream = cotangent.reshape(token_rows, model_width)
     gated_low, expanded_grad, expand_sums, forward, normed_two_grad = run_gate(
         normed_two_low, upstream, packed_all, expand_bias
@@ -801,7 +823,7 @@
     kept = run_backward(
         (0, early), lengths, base, query_low, key_ext, value_ext, attended_grad, totals, (), marks
     )
-    marks = one_round(shrink_sum, expand_sum, 0) + [mark(root_all)]
+    marks = one_round(shrink_sum, expand_sum, 0)
     kept = run_backward(
         (early, pairs - early),
         lengths,
@@ -824,7 +846,7 @@
     from_below = lax.ppermute(
         pair_grad[:, :, block_size + WIN :], "seq", [(i, i + 1) for i in range(ends)]
     )
-    from_above = after(from_above, *marks)
+    from_above = after(from_above, mark(root_all), *marks)
     pair_own = pair_grad[:, :, WIN : WIN + block_size]
     pair_low = jnp.concatenate(
         [
@@ -835,13 +857,6 @@
         axis=2,
     ).reshape(2, token_rows, model_width)
     query_rows = query_grad.reshape(token_rows, model_width)
-    for i in range(2, len(rounds())):
-        marks = one_round(shrink_sum, expand_sum, i)
-    shrink_own, expand_own = shrink_sum.blocks, expand_sum.blocks
-    hidden_own = jnp.stack(
-        [low(own).reshape(hidden_block, model_width) for own in (shrink_own, expand_own)]
-    )
-
     grads = jnp.stack(
         [
             low(across(normed_low, query_rows)),
@@ -853,6 +868,15 @@
     core_sum = Halving(grads, ["x", "c"])
     core_sum.start("c")
     core_sum.finish()
+    for i in range(2, len(rounds())):
+        marks = one_round(
+            shrink_sum, expand_sum, i, mark(core_sum.kept if i == 2 else core_sum.blocks)
+        )
+    shrink_own, expand_own = shrink_sum.blocks, expand_sum.blocks
+    hidden_own = jnp.stack(
+        [low(own).reshape(hidden_block, model_width) for own in (shrink_own, expand_own)]
+    )
+
     halves = [
         Halving(core_sum.blocks[:, i], ["x", None] + list(range(bits - 1, -1, -1)))
         for i in range(2)
@@ -888,24 +912,37 @@
         ],
         axis=0,
     )
-    whole = spread(low(attend_own)).transpose(1, 0, 2, 3).reshape(model_width, model_width)
-    token = attend_own[0, 0, :128]
-    vector_terms = after(vector_terms, token)
-    vector_some = jnp.sum(spread(vector_terms), axis=0)
+    token = attend_own[0, :1, :128] + attend_own[-1, :1, :128]
+    attend_all = lax.all_gather(
+        jnp.concatenate(
+            [
+                low(attend_own).reshape(rows_own, model_width),
+                halves_of(vector_terms, lax.optimization_barrier),
+            ]
+        ),
+        "dp",
+        axis=0,
+    )
+    whole = (
+        attend_all[:, :rows_own]
+        .reshape(dp_count, seq_count, block, model_width)
+        .transpose(1, 0, 2, 3)
+        .reshape(model_width, model_width)
+    )
 
     expand_rc = roots[:, :hidden_block].reshape(seq_count * hidden_block, part)
     attend_rc = roots[:, hidden_block : hidden_block + block].reshape(rows_own, model_width)
-    shrink_rc = roots[:, hidden_block + block : cut].reshape(rows_own, model_width)
-    shrink_lw = root_all[:, :, :hidden_block].reshape(seq_count, part, part)
-    attend_lw = root_all[:, :, hidden_block : hidden_block + block].reshape(
-        model_width, model_width
-    )
-    expand_lw = root_all[:, :, hidden_block + block :].reshape(model_width, model_width)
+    shrink_lr = roots[:, hidden_block + block : cut].reshape(seq_count * hidden_block, part)
+    attend_lw = root_all[:, :, :block].reshape(model_width, model_width)
+    expand_lw = root_all[:, :, block : 2 * block].reshape(model_width, model_width)
+    shrink_rt = root_all[:, :, 2 * block :].transpose(1, 0, 2, 3).reshape(model_width, model_width)
 
     panels = lax.all_gather(hidden_own, "dp", axis=1, tiled=True)
-    row_sets = spread(hidden_own, "seq")
+    row_sets = ordered(chip, hidden_own, flip(hidden_own, "seq", 2), 0)
+    row_sets = ordered(core, row_sets, flip(row_sets, "seq", 1), 1)
+    row_sets = row_sets.reshape((seq_count,) + hidden_own.shape)
     index = dp_index.astype(jnp.int32)
-    products, turns = run_hidden(
+    products, turned = run_hidden(
         seq_count,
         block,
         dp_count,
@@ -913,13 +950,26 @@
         panels,
         row_sets,
         expand_rc,
-        shrink_rc,
         expand_lw,
-        shrink_lw,
+        shrink_lr,
+        shrink_rt,
         token,
     )
-    back = swap(products)
-    turned_back = swap(turns)
+    turned = lax.all_to_all(
+        turned.reshape(dp_count, rows_own, seq_count * hidden_block),
+        "dp",
+        split_axis=0,
+        concat_axis=0,
+        tiled=True,
+    )
+    pack = model_width // (seq_count * hidden_block)
+    turned = (
+        turned.reshape(dp_count // pack, pack, seq_count, block, seq_count * hidden_block)
+        .transpose(2, 0, 3, 1, 4)
+        .reshape(seq_count, hidden_block, model_width)
+    )
+    to_owners = jnp.concatenate([products, turned], axis=1)
+    back = swap(to_owners)
     to_return = run_attend(
         seq_count,
         block,
@@ -930,11 +980,12 @@
         attend_own.reshape(rows_own, model_width),
         attend_rc,
         attend_lw,
-        products[0, 0, :128],
-    )
-    returned = swap(to_return)[:, :, :block].astype(jnp.float32)
-    vector_some = after(vector_some, returned[0, 0, 0, :128])
-    vector_sum = jnp.sum(spread(vector_some, "seq"), axis=0)
+        attend_all[:, rows_own:],
+        mark(to_owners),
+    )
+    returned = swap(to_return)
+    vector_sum = from_halves(returned[:, 4])[: vectors.shape[0]]
+    returned = returned[:, :4, :block].astype(jnp.float32)
     vector_grad = vector_sum * grad_scale
     vector_newacc = vector_acc + vector_grad * vector_grad
     vector_new = vectors - VECTOR_RATE * vector_grad / (jnp.sqrt(vector_newacc) + 1e-08)
@@ -965,9 +1016,12 @@
     expand_newleft = 0.5 * expand_left + total(parts[4]) * (0.5 * expand_scale / hidden)
     expand_rows = unfold(parts[5]).astype(jnp.float32) * grad_scale
     expand_direction_t = total(parts[2]) * (grad_scale * lax.rsqrt(squares[1]))
-    shrink_direction_t = unfold(total(turned_back)[:, :block]) * (
-        grad_scale * lax.rsqrt(squares[0])
-    )
+    shrink_direction_t = (
+        total(back[:, starts[-1] + 16 :])
+        .reshape(dp_count // pack, block, pack, seq_count, hidden_block)
+        .transpose(1, 3, 0, 2, 4)
+        .reshape(block, hidden)
+    ) * (grad_scale * lax.rsqrt(squares[0]))
     expand_newmoment_t, expand_newweight_t = finish(
         expand_direction_t, expand_moment.T, expand_t, model_width
     )

time: 600 us -> 577 us (0.962)
  Pallas kernels: 105 us -> 89.2 us
  starting transfers between devices: 73.5 us -> 59 us
  other arithmetic: 68.4 us -> 79.6 us
  local copies, waits for them, and re-layouts: 80 us -> 90.8 us
  waiting for transfers between devices: 194 us -> 185 us
    all_to_all x5 -> x1, waiting for transfers between devices: 41.2 us -> 15.3 us  [spread(): return lax.all_to_all(copies, axis, split_axis=0, concat_axis=0, tiled=True)]
    all_gather x0 -> x1, waiting for transfers between devices: none -> 22.8 us  [shards(): lax.all_gather(jnp.concatenate([low(attend_own).reshape(rows_own, model_w...]
    all_to_all x5 -> x1, starting transfers between devices: 28.2 us -> 7.28 us  [spread(): return lax.all_to_all(copies, axis, split_axis=0, concat_axis=0, tiled=True)]
    ppermute x21 -> x23, waiting for transfers between devices: 81.3 us -> 101 us  [flip(): return lax.ppermute(blocks, axis, [(i, i ^ mask) for i in range(count)])]
    all_to_all x4 -> x3, waiting for transfers between devices: 57.9 us -> 38.7 us  [swap(): lax.all_to_all(blocks, 'seq', split_axis=0, concat_axis=0, tiled=True)]
    all_gather x1, waiting for transfers between devices: 13.6 us -> 0.01 us  [shards(): root_all = lax.all_gather(roots[:, cut:], 'dp', axis=1)]
    pallas_call x1, Pallas kernels: 22.7 us -> 14.6 us  [run_forward(): pl.pallas_call(functools.partial(attend_forward, blocks), grid=(texts, wi...]
    ppermute x21 -> x23, starting transfers between devices: 20.3 us -> 27.6 us  [flip(): return lax.ppermute(blocks, axis, [(i, i ^ mask) for i in range(count)])]
  transfers between devices with their start and end apart: 37 -> 36, of which waited for: 20 -> 19; matrix products, arithmetic and copies ran while one was open for 28% -> 26% of each run, Pallas kernels for 16% -> 8%
where the time goes in v3:
time: 577 us; the launch traced here: 569 us
  waiting for transfers between devices  185 us (32%)
  local copies, waits for them, and re-layouts  90.8 us (16%)
  Pallas kernels  89.2 us (15%)
  other arithmetic  79.6 us (14%)
  starting transfers between devices  59 us (10%)
  matrix products  47.8 us (8%)
  between operations  18.3 us (3%)
    ppermute x23, waiting for transfers between devices, flip(): return lax.ppermute(blocks, axis, [(i, i ^ mask) for i in range(count)])  101 us
    all_to_all x3, waiting for transfers between devices, swap(): lax.all_to_all(blocks, 'seq', split_axis=0, concat_axis=0, tiled=True)  38.7 us
    pallas_call x1, Pallas kernels, run_gate(): pl.pallas_call(gate_kernel, grid=(groups, tiles), in_specs=[row_spec, row...  37.3 us
    convert_element_type x29, other arithmetic, low(): return values.astype(jnp.bfloat16)  28.7 us
    ppermute x23, starting transfers between devices, flip(): return lax.ppermute(blocks, axis, [(i, i ^ mask) for i in range(count)])  27.6 us
    dot_general x6, matrix products, across(): lax.dot_general(left_rows, right_rows, (((0,), (0,)), ((), ())), preferre...  25.7 us
    all_gather x1, waiting for transfers between devices, shards(): lax.all_gather(jnp.concatenate([low(attend_own).reshape(rows_own, model_w...  22.8 us
    pallas_call x2, Pallas kernels, run_backward(): pl.pallas_call(functools.partial(attend_backward, blocks, len(others)), g...  22.3 us
  transfers between devices with their start and end apart: 36, of which 19 were waited for; matrix products, arithmetic and copies ran while one was open for 26% of the time, Pallas kernels for 8%

profile of v3, /device:TPU:0, one launch (start us, length us, event | category | flops | bytes accessed | tf_op | source)
XLA Modules:
  0.0 569.4 jit_solution(1256302803931294142)
XLA Ops:
  13.8 7.3 %all-to-all-start = ((bf16[8,3,24,768]{3,2,1,0:T(8,128)(2,1)}), bf16[8,3,24,768]{3,2,1,0:T(8,128)(2,1)}, u32[]{:S(2)}, u32[]{:S(2)}) async-start(bf16[8,3,24,768]{3,2,1,0:T(8,128)(2,1)} %broadcast_in_dim.16), calls=%async_computation | async-start | bytes 1769472 | tf_op jit(solution)/shard_map/all_to_all | solution.py:376
  35.4 15.3 %all-to-all-done = bf16[8,3,24,768]{3,2,1,0:T(8,128)(2,1)} async-done(((bf16[8,3,24,768]{3,2,1,0:T(8,128)(2,1)}), bf16[8,3,24,768]{3,2,1,0:T(8,128)(2,1)}, u32[]{:S(2)}, u32[]{:S(2)}) %all-to-all-start) | async-done | bytes 884768 | tf_op jit(solution)/shard_map/all_to_all | solution.py:376
  55.3 3.2 fusion.5
  58.4 22.9 %collective-permute-done = bf16[3,8,24,768]{3,2,1,0:T(8,128)(2,1)S(1)} collective-permute-done((bf16[3,8,24,768]{3,2,1,0:T(8,128)(2,1)S(1)}, bf16[3,8,24,768]{3,2,1,0:T(8,128)(2,1)S(1)}, u32[]{:S(2)}, u32[]{:S(2)}) %collective-permute-start) | collective-permute-done | bytes 884768 | tf_op jit(solution)/shard_map/ppermute | solution.py:367
  84.9 4.4 all-to-all-start.1
  91.5 4.3 copy.176
  98.8 3.4 maximum_select_fusion
  104.1 2.6 add_convert_fusion.4
  106.7 3.5 convolution_convert_fusion.2
  110.2 3.5 add_convert_fusion
  113.7 14.6 %attend_forward.1 = (bf16[2,512,768]{2,1,0:T(8,128)(2,1)}, f32[2,6,8,128]{3,2,1,0:T(8,128)}) custom-call(s32[2]{0:T(128)} %lengths.5, s32[1]{0:T(128)} %bitcast.1.base, bf16[2,512,768]{2,1,0:T(8,128)(2,1)} %bitcast.425, bf16[2,768,768]{2,1,0:T(8,128)(2,1)} %bitcast.414, bf16[2,768,768]{2,1,0:T(8,128)(2,1)} %bitcast.417), custom_call_target="tpu_custom_call" | custom-call | flops 2415919104 | bytes 7864320 | tf_op jit(solution)/shard_map/attend_forward/pallas_call | solution.py:191
  128.3 6.9 %all-gather.7.cloned.1.call-done.in_ref.out_ref = bf16[768,6912]{1,0:T(8,128)(2,1)} async-done(((bf16[24,6912]{1,0:T(8,128)(2,1)}), bf16[768,6912]{1,0:T(8,128)(2,1)}) %all-gather.7.cloned.1.call-update) | async-done | bytes 10616848 | tf_op jit(solution)/shard_map/all_gather | solution.py:722
  135.2 3.3 fusion.69
  141.9 37.3 %gate.1 = (bf16[1024,3072]{1,0:T(8,128)(2,1)}, bf16[1024,3072]{1,0:T(8,128)(2,1)}, f32[2,8,3072]{2,1,0:T(8,128)}, f32[1024,768]{1,0:T(8,128)}, f32[1024,768]{1,0:T(8,128)}) custom-call(bf16[1024,768]{1,0:T(8,128)(2,1)} %add_convert_fusion.3.rows_ref, bf16[1024,768]{1,0:T(8,128)(2,1)} %bitcast.388, ...), custom_call_target="tpu_custom_call" | custom-call | flops 2415919104 | bytes 25165824 | tf_op jit(solution)/shard_map/gate/pallas_call | solution.py:330
  179.3 10.0 %convolution_convert_fusion = bf16[3072,768]{1,0:T(8,128)(2,1)} fusion(bf16[1024,3072]{1,0:T(8,128)(2,1)} %get-tuple-element.53, bf16[1024,768]{1,0:T(8,128)(2,1)S(1)} %copy-done.19), kind=kOutput, calls=%fused_computation.8 | convolution fusion | flops 4834197504 | bytes 12582912 | tf_op jit(solution)/shard_map/dot_general | solution.py:46
  189.3 6.9 %convolution_convert_fusion.1 = bf16[3072,768]{1,0:T(8,128)(2,1)} fusion(bf16[1024,3072]{1,0:T(8,128)(2,1)S(1)} %copy-done.73, bf16[1024,768]{1,0:T(8,128)(2,1)S(1)} %bitcast.389), kind=kOutput, calls=%fused_computation.9 | convolution fusion | flops 4834197504 | bytes 12582912 | tf_op jit(solution)/shard_map/dot_general | solution.py:46
  196.2 5.6 constant_dynamic-slice_fusion.4
  204.1 3.5 copy.240
  207.9 2.9 multiply_reduce_fusion
  212.7 5.5 fusion.61
  219.9 4.4 convolution_convert_fusion.3
  236.3 4.5 fusion.24
  244.0 14.1 %attend_backward.2 = (bf16[2,512,768]{2,1,0:T(8,128)(2,1)}, bf16[2,768,768]{2,1,0:T(8,128)(2,1)}, bf16[2,768,768]{2,1,0:T(8,128)(2,1)}) custom-call(s32[2]{0:T(128)} %lengths.5, s32[1]{0:T(128)} %bitcast.1.base, bf16[2,512,768]{2,1,0:T(8,128)(2,1)} %bitcast.426, bf16[2,768,768]{2,1,0:T(8,128)(2,1)} %bitcast.415, bf16[2,768,768]{2,1,0:T(8,128)(2,1)} %bitcast.418, ...), custom_call_target="tpu_custom_call" | custom-call | flops 4026531840 | bytes 7864320 | tf_op jit(solution)/shard_map/attend_backward/pallas_call | solution.py:222
  260.8 19.2 %collective-permute-done.7 = bf16[4,2,2,2,24,768]{5,4,0,1,2,3:T(8,128)(2,1)} collective-permute-done((bf16[4,2,2,2,24,768]{5,4,0,1,2,3:T(8,128)(2,1)}, bf16[4,2,2,2,24,768]{5,4,0,1,2,3:T(8,128)(2,1)}, u32[]{:S(2)}, u32[]{:S(2)}) %collective-permute-start.7) | collective-permute-done | bytes 1179680 | tf_op jit(solution)/shard_map/ppermute | solution.py:367
  282.8 8.2 %attend_backward.3 = (bf16[2,512,768]{2,1,0:T(8,128)(2,1)}, bf16[2,768,768]{2,1,0:T(8,128)(2,1)}, bf16[2,768,768]{2,1,0:T(8,128)(2,1)}) custom-call(s32[2]{0:T(128)} %lengths.5, s32[1]{0:T(128)} %bitcast.1.base, bf16[2,512,768]{2,1,0:T(8,128)(2,1)} %bitcast.427, ...), custom_call_target="tpu_custom_call", output_to_operand_aliasing={{0}: (7, {}), {1}: (8, {}), {2}: (9, {})} | custom-call | flops 2013265920 | bytes 7864320 | tf_op jit(solution)/shard_map/attend_backward/pallas_call | solution.py:222
  303.6 7.9 %collective-permute-done.12 = bf16[4,2,2,24,768]{4,3,0,1,2:T(8,128)(2,1)S(1)} collective-permute-done((bf16[4,2,2,24,768]{4,3,0,1,2:T(8,128)(2,1)S(1)}, bf16[4,2,2,24,768]{4,3,0,1,2:T(8,128)(2,1)S(1)}, u32[]{:S(2)}, u32[]{:S(2)}) %collective-permute-start.12) | collective-permute-done | bytes 589856 | tf_op jit(solution)/shard_map/ppermute | solution.py:367
  332.7 4.6 fusion.6
  342.8 3.9 collective-permute-done.14
  354.5 11.1 %collective-permute-done.11 = bf16[2,2,2,2,24,768]{5,4,0,1,2,3:T(8,128)(2,1)S(1)} collective-permute-done((bf16[2,2,2,2,24,768]{5,4,0,1,2,3:T(8,128)(2,1)S(1)}, bf16[2,2,2,2,24,768]{5,4,0,1,2,3:T(8,128)(2,1)S(1)}, u32[]{:S(2)}, u32[]{:S(2)}) %collective-permute-start.11) | collective-permute-done | bytes 589856 | tf_op jit(solution)/shard_map/ppermute | solution.py:367
  367.6 4.6 collective-permute-done.21
  373.1 3.6 collective-permute-done.18
  377.6 4.0 collective-permute-done.22
  384.1 5.7 collective-permute-done.19
  390.4 9.9 %collective-permute-done.23 = bf16[2,2,24,768]{3,2,1,0:T(8,128)(2,1)S(1)} collective-permute-done((bf16[2,2,24,768]{3,2,1,0:T(8,128)(2,1)S(1)}, bf16[2,2,24,768]{3,2,1,0:T(8,128)(2,1)S(1)}, u32[]{:S(2)}, u32[]{:S(2)}) %collective-permute-start.23) | collective-permute-done | bytes 147488 | tf_op jit(solution)/shard_map/ppermute | solution.py:367
  400.4 3.2 collective-permute-start.24
  409.7 4.9 collective-permute-done.25
  419.6 3.7 slice_bitcast_fusion
  428.4 10.4 %hidden_update.1 = (bf16[4,400,768]{2,1,0:T(8,128)(2,1)}, bf16[768,384]{1,0:T(8,128)(2,1)}) custom-call(s32[1]{0:T(128)} %bitcast.54.index_ref, bf16[2,768,768]{2,1,0:T(8,128)(2,1)} %all-gather.9.cloned.1.call-done.panels_ref, bf16[4,2,96,768]{3,2,1,0:T(8,128)(2,1)} %bitcast.448, bf16[384,768]{1,0:T(8,128)(2,1)} %bitcast.461, bf16[768,768]{1,0:T(8,128)(2,1)} %bitcast.446, ...), custom_call_target="tpu_custom_call" | custom-call | flops 2264924160 | bytes 7077888 | tf_op jit(solution)/shard_map/hidden_update/pallas_call | solution.py:541
  438.8 4.2 all-to-all-start.2
  444.6 22.8 %all-gather.11.cloned.1.call-done = bf16[1024,768]{1,0:T(8,128)(2,1)} async-done(((bf16[128,768]{1,0:T(8,128)(2,1)}), bf16[1024,768]{1,0:T(8,128)(2,1)}) %all-gather.11.cloned.1.call-update) | async-done | bytes 1572880 | tf_op jit(solution)/shard_map/all_gather | solution.py:916
  475.7 2.8 reshape.523
  481.7 4.6 attend_update.1
  486.3 4.2 all-to-all-start.3
  490.5 13.8 %all-to-all-done.3 = bf16[4,5,32,768]{3,2,1,0:T(8,128)(2,1)} async-done(((bf16[4,5,32,768]{3,2,1,0:T(8,128)(2,1)}), bf16[4,5,32,768]{3,2,1,0:T(8,128)(2,1)}, u32[]{:S(2)}, u32[]{:S(2)}) %all-to-all-start.3) | async-done | bytes 983072 | tf_op jit(solution)/shard_map/all_to_all | solution.py:371
  504.3 4.8 all-to-all-start.4
  509.2 4.5 add_convert_fusion.1
  520.1 25.0 %all-to-all-done.4 = bf16[4,496,768]{2,1,0:T(8,128)(2,1)} async-done(((bf16[4,496,768]{2,1,0:T(8,128)(2,1)}), bf16[4,496,768]{2,1,0:T(8,128)(2,1)}, u32[]{:S(2)}, u32[]{:S(2)}) %all-to-all-start.4) | async-done | bytes 3047456 | tf_op jit(solution)/shard_map/all_to_all | solution.py:371
  549.7 3.0 convert_reduce_fusion.6
  (391 shorter events, 166.4 us)
Async XLA Ops:
  7.2 128.0 %all-gather.7.cloned.1.call-start = ((), (), s32[]{:S(2)}) async-start(), calls=%async_computation.5 | async-start | bytes 10948608 | tf_op jit(solution)/shard_map/all_gather | solution.py:722
  13.8 36.8 %all-to-all-start = ((bf16[8,3,24,768]{3,2,1,0:T(8,128)(2,1)}), bf16[8,3,24,768]{3,2,1,0:T(8,128)(2,1)}, u32[]{:S(2)}, u32[]{:S(2)}) async-start(bf16[8,3,24,768]{3,2,1,0:T(8,128)(2,1)} %broadcast_in_dim.16), calls=%async_computation | async-start | bytes 1769472 | tf_op jit(solution)/shard_map/all_to_all | solution.py:376
  22.9 10.5 %collective-permute-start.1 = (bf16[2,128,768]{1,2,0:T(8,128)(2,1)}, bf16[2,128,768]{1,2,0:T(8,128)(2,1)S(1)}, u32[]{:S(2)}, u32[]{:S(2)}) collective-permute-start(bf16[2,128,768]{1,2,0:T(8,128)(2,1)} %get-tuple-element.226), channel_id=1, source_target_pairs={{0,8},{8,16},{16,24},{1,9},{9,17},{17,25},{2,10},{10,18},{18,26},{... | collective-permute-start | bytes 1179656 | tf_op jit(solution)/shard_map/ppermute | solution.py:700
  24.3 9.0 %collective-permute-start.2 = (bf16[2,128,768]{1,2,0:T(8,128)(2,1)}, bf16[2,128,768]{1,2,0:T(8,128)(2,1)}, u32[]{:S(2)}, u32[]{:S(2)}) collective-permute-start(bf16[2,128,768]{1,2,0:T(8,128)(2,1)} %get-tuple-element.227), channel_id=1, source_target_pairs={{8,0},{16,8},{24,16},{9,1},{17,9},{25,17},{10,2},{18,10},{26,18},{... | collective-permute-start | bytes 1179656 | tf_op jit(solution)/shard_map/ppermute | solution.py:703
  51.9 29.4 %collective-permute-start = (bf16[3,8,24,768]{3,2,1,0:T(8,128)(2,1)S(1)}, bf16[3,8,24,768]{3,2,1,0:T(8,128)(2,1)S(1)}, u32[]{:S(2)}, u32[]{:S(2)}) collective-permute-start(bf16[3,8,24,768]{3,2,1,0:T(8,128)(2,1)S(1)} %bitcast.408), channel_id=1, source_target_pairs={{0,16},{8,24},{16,0},{24,8},{1,17},{9,25},{17,1},{25,9},{2,18},{10... | collective-permute-start | bytes 2654216 | tf_op jit(solution)/shard_map/ppermute | solution.py:367
  58.4 24.4 %copy-start.63 = (f32[768,24]{0,1:T(8,128)S(1)}, f32[768,24]{0,1:T(8,128)}, u32[]{:S(2)}) copy-start(f32[768,24]{0,1:T(8,128)} %param.45) | copy-start | bytes 221188
  58.4 24.4 %copy-start.48 = (bf16[4,24,768]{2,0,1:T(4,128)(2,1)S(1)}, bf16[4,24,768]{2,0,1:T(4,128)(2,1)}, u32[]{:S(2)}) copy-start(bf16[4,24,768]{2,0,1:T(4,128)(2,1)} %convert_bitcast_fusion) | copy-start | bytes 442372
  58.4 25.1 %copy-start.60 = (bf16[24,768]{1,0:T(8,128)(2,1)S(1)}, bf16[24,768]{1,0:T(8,128)(2,1)}, u32[]{:S(2)}) copy-start(bf16[24,768]{1,0:T(8,128)(2,1)} %convert_element_type.416) | copy-start | bytes 110596
  82.9 16.0 %collective-permute-start.3 = (bf16[3,2,8,24,768]{4,3,2,1,0:T(8,128)(2,1)}, bf16[3,2,8,24,768]{4,3,2,1,0:T(8,128)(2,1)}, u32[]{:S(2)}, u32[]{:S(2)}) collective-permute-start(bf16[3,2,8,24,768]{4,3,2,1,0:T(8,128)(2,1)} %maximum_select_fusion.1), channel_id=1, source_target_pairs={{0,8},{8,0},{16,24},{24,16},{1,9},{9,1},{17,25},{25,17},{2,10},{10... | collective-permute-start | bytes 5308424 | tf_op jit(solution)/shard_map/ppermute | solution.py:367
  84.9 57.0 %all-to-all-start.1 = ((bf16[4,288,768]{2,1,0:T(8,128)(2,1)}), bf16[4,288,768]{2,1,0:T(8,128)(2,1)}, u32[]{:S(2)}, u32[]{:S(2)}) async-start(bf16[4,288,768]{2,1,0:T(8,128)(2,1)} %broadcast_dynamic-update-slice_fusion), calls=%async_computation.1 | async-start | bytes 3538944 | tf_op jit(solution)/shard_map/all_to_all | solution.py:371
  89.3 330.3 %all-gather.13.cloned.1.call-start = ((), (), s32[]{:S(2)}) async-start(), calls=%async_computation.8 | async-start | bytes 3981312 | tf_op jit(solution)/shard_map/all_gather | solution.py:780
  113.7 21.5 %copy-start.70 = (f32[768]{0:T(1024)S(1)}, f32[768]{0:T(1024)}, u32[]{:S(2)}) copy-start(f32[768]{0:T(1024)} %get-tuple-element.184) | copy-start | bytes 9220
  141.9 37.3 %copy-start.19 = (bf16[1024,768]{1,0:T(8,128)(2,1)S(1)}, bf16[1024,768]{1,0:T(8,128)(2,1)}, u32[]{:S(2)}) copy-start(bf16[1024,768]{1,0:T(8,128)(2,1)} %add_convert_fusion.3.rows_ref) | copy-start | bytes 4718596
  179.3 10.0 %copy-start.7 = (bf16[2,512,768]{2,1,0:T(8,128)(2,1)S(1)}, bf16[2,512,768]{2,1,0:T(8,128)(2,1)}, u32[]{:S(2)}) copy-start(bf16[2,512,768]{2,1,0:T(8,128)(2,1)} %param.24) | copy-start | bytes 4718596
  179.3 10.0 %copy-start.73 = (bf16[1024,3072]{1,0:T(8,128)(2,1)S(1)}, bf16[1024,3072]{1,0:T(8,128)(2,1)}, u32[]{:S(2)}) copy-start(bf16[1024,3072]{1,0:T(8,128)(2,1)} %get-tuple-element.52) | copy-start | bytes 18874372
  203.5 20.8 %collective-permute-start.4 = (bf16[4,2,2,2,2,24,768]{6,5,0,2,3,4,1:T(8,128)(2,1)}, bf16[4,2,2,2,2,24,768]{6,5,0,2,3,4,1:T(8,128)(2,1)}, u32[]{:S(2)}, u32[]{:S(2)}) collective-permute-start(bf16[4,2,2,2,2,24,768]{6,5,0,2,3,4,1:T(8,128)(2,1)} %bitcast.378), channel_id=1, source_target_pairs={{0,8},{8,0},{16,24},{24,16},{1,9},{9,1},{17,25},{25,17},{2,10},{10... | collective-permute-start | bytes 7077896 | tf_op jit(solution)/shard_map/ppermute | solution.py:367
  207.6 21.0 %collective-permute-start.5 = (bf16[4,2,2,2,2,24,768]{6,5,0,1,2,3,4:T(8,128)(2,1)}, bf16[4,2,2,2,2,24,768]{6,5,0,1,2,3,4:T(8,128)(2,1)}, u32[]{:S(2)}, u32[]{:S(2)}) collective-permute-start(bf16[4,2,2,2,2,24,768]{6,5,0,1,2,3,4:T(8,128)(2,1)} %bitcast.377), channel_id=1, source_target_pairs={{0,8},{8,0},{16,24},{24,16},{1,9},{9,1},{17,25},{25,17},{2,10},{10... | collective-permute-start | bytes 7077896 | tf_op jit(solution)/shard_map/ppermute | solution.py:367
  212.6 215.7 %all-gather.9.cloned.1.call-start = ((), (), s32[]{:S(2)}) async-start(), calls=%async_computation.6 | async-start | bytes 2654208 | tf_op jit(solution)/shard_map/all_gather | solution.py:940
  227.7 30.3 %collective-permute-start.6 = (bf16[4,2,2,2,24,768]{5,4,0,1,2,3:T(8,128)(2,1)}, bf16[4,2,2,2,24,768]{5,4,0,1,2,3:T(8,128)(2,1)}, u32[]{:S(2)}, u32[]{:S(2)}) collective-permute-start(bf16[4,2,2,2,24,768]{5,4,0,1,2,3:T(8,128)(2,1)} %dynamic-slice_bitcast_fusion.2), channel_id=1, source_target_pairs={{0,16},{8,24},{16,0},{24,8},{1,17},{9,25},{17,1},{25,9},{2,18},{10... | collective-permute-start | bytes 3538952 | tf_op jit(solution)/shard_map/ppermute | solution.py:367
  233.6 46.3 %collective-permute-start.7 = (bf16[4,2,2,2,24,768]{5,4,0,1,2,3:T(8,128)(2,1)}, bf16[4,2,2,2,24,768]{5,4,0,1,2,3:T(8,128)(2,1)}, u32[]{:S(2)}, u32[]{:S(2)}) collective-permute-start(bf16[4,2,2,2,24,768]{5,4,0,1,2,3:T(8,128)(2,1)} %dynamic-slice_bitcast_fusion.1), channel_id=1, source_target_pairs={{0,1},{1,0},{2,3},{3,2},{4,5},{5,4},{6,7},{7,6},{8,9},{9,8},{10,11... | collective-permute-start | bytes 3538952 | tf_op jit(solution)/shard_map/ppermute | solution.py:367
  259.6 21.9 %copy-start.14 = (bf16[4,2,2,2,24,768]{5,4,0,1,2,3:T(8,128)(2,1)}, bf16[4,2,2,2,24,768]{5,4,0,1,2,3:T(8,128)(2,1)S(1)}, u32[]{:S(2)}) copy-start(bf16[4,2,2,2,24,768]{5,4,0,1,2,3:T(8,128)(2,1)S(1)} %fusion.19) | copy-start | bytes 3538948
  292.6 19.1 %collective-permute-start.8 = (bf16[2,2,128,768]{3,2,1,0:T(8,128)(2,1)S(1)}, bf16[2,2,128,768]{3,2,1,0:T(8,128)(2,1)S(1)}, u32[]{:S(2)}, u32[]{:S(2)}) collective-permute-start(bf16[2,2,128,768]{3,2,1,0:T(8,128)(2,1)S(1)} %get-tuple-element.204), channel_id=1, source_target_pairs={{0,8},{8,16},{16,24},{1,9},{9,17},{17,25},{2,10},{10,18},{18,26},{... | collective-permute-start | bytes 2359304 | tf_op jit(solution)/shard_map/ppermute | solution.py:846
  294.0 17.8 %collective-permute-start.9 = (bf16[2,2,128,768]{3,2,1,0:T(8,128)(2,1)S(1)}, bf16[2,2,128,768]{3,2,1,0:T(8,128)(2,1)S(1)}, u32[]{:S(2)}, u32[]{:S(2)}) collective-permute-start(bf16[2,2,128,768]{3,2,1,0:T(8,128)(2,1)S(1)} %get-tuple-element.205), channel_id=1, source_target_pairs={{8,0},{16,8},{24,16},{9,1},{17,9},{25,17},{10,2},{18,10},{26,18},{... | collective-permute-start | bytes 2359304 | tf_op jit(solution)/shard_map/ppermute | solution.py:843
  295.5 16.1 %collective-permute-start.12 = (bf16[4,2,2,24,768]{4,3,0,1,2:T(8,128)(2,1)S(1)}, bf16[4,2,2,24,768]{4,3,0,1,2:T(8,128)(2,1)S(1)}, u32[]{:S(2)}, u32[]{:S(2)}) collective-permute-start(bf16[4,2,2,24,768]{4,3,0,1,2:T(8,128)(2,1)S(1)} %copy-done.49), channel_id=1, source_target_pairs={{0,1},{1,0},{2,3},{3,2},{4,5},{5,4},{6,7},{7,6},{8,9},{9,8},{10,11... | collective-permute-start | bytes 1769480 | tf_op jit(solution)/shard_map/ppermute | solution.py:367
  298.1 23.9 %collective-permute-start.15 = (bf16[4,2,2,24,768]{4,3,0,1,2:T(8,128)(2,1)S(1)}, bf16[4,2,2,24,768]{4,3,0,1,2:T(8,128)(2,1)S(1)}, u32[]{:S(2)}, u32[]{:S(2)}) collective-permute-start(bf16[4,2,2,24,768]{4,3,0,1,2:T(8,128)(2,1)S(1)} %dynamic-slice_bitcast_fusion.4), channel_id=1, source_target_pairs={{0,2},{1,3},{2,0},{3,1},{4,6},{5,7},{6,4},{7,5},{8,10},{9,11},{10,... | collective-permute-start | bytes 1769480 | tf_op jit(solution)/shard_map/ppermute | solution.py:367
  302.2 9.3 %copy-start.15 = (bf16[4,2,2,2,24,768]{5,4,0,1,2,3:T(8,128)(2,1)S(1)}, bf16[4,2,2,2,24,768]{5,4,0,1,2,3:T(8,128)(2,1)}, u32[]{:S(2)}) copy-start(bf16[4,2,2,2,24,768]{5,4,0,1,2,3:T(8,128)(2,1)} %copy-done.14) | copy-start | bytes 3538948
  311.7 9.5 %copy-start.25 = (bf16[4,2,2,24,768]{4,3,0,1,2:T(8,128)(2,1)}, bf16[4,2,2,24,768]{4,3,0,1,2:T(8,128)(2,1)S(1)}, u32[]{:S(2)}) copy-start(bf16[4,2,2,24,768]{4,3,0,1,2:T(8,128)(2,1)S(1)} %fusion.28) | copy-start | bytes 1769476
  320.4 12.3 %collective-permute-start.10 = (bf16[2,2,2,2,2,2,24,768]{7,6,5,4,3,2,1,0:T(8,128)(2,1)}, bf16[2,2,2,2,2,2,24,768]{7,6,5,4,3,2,1,0:T(8,128)(2,1)}, u32[]{:S(2)}, u32[]{:S(2)}) collective-permute-start(bf16[2,2,2,2,2,2,24,768]{7,6,5,4,3,2,1,0:T(8,128)(2,1)} %dynamic-slice_bitcast_fusion), channel_id=1, source_target_pairs={{0,8},{8,0},{16,24},{24,16},{1,9},{9,1},{17,25},{25,17},{2,10},{10... | collective-permute-start | bytes 7077896 | tf_op jit(solution)/shard_map/ppermute | solution.py:367
  321.9 15.4 %collective-permute-start.13 = (bf16[4,2,24,768]{3,2,0,1:T(8,128)(2,1)}, bf16[4,2,24,768]{3,2,0,1:T(8,128)(2,1)S(1)}, u32[]{:S(2)}, u32[]{:S(2)}) collective-permute-start(bf16[4,2,24,768]{3,2,0,1:T(8,128)(2,1)} %dynamic-slice_bitcast_fusion.9), channel_id=1, source_target_pairs={{0,2},{1,3},{2,0},{3,1},{4,6},{5,7},{6,4},{7,5},{8,10},{9,11},{10,... | collective-permute-start | bytes 884744 | tf_op jit(solution)/shard_map/ppermute | solution.py:367
  323.6 16.5 %collective-permute-start.16 = (bf16[4,2,24,768]{3,2,0,1:T(8,128)(2,1)}, bf16[4,2,24,768]{3,2,0,1:T(8,128)(2,1)}, u32[]{:S(2)}, u32[]{:S(2)}) collective-permute-start(bf16[4,2,24,768]{3,2,0,1:T(8,128)(2,1)} %dynamic-slice_bitcast_fusion.8), channel_id=1, source_target_pairs={{0,4},{1,5},{2,6},{3,7},{4,0},{5,1},{6,2},{7,3},{8,12},{9,13},{10,... | collective-permute-start | bytes 884744 | tf_op jit(solution)/shard_map/ppermute | solution.py:367
  337.4 9.3 %collective-permute-start.14 = (bf16[4,24,768]{2,1,0:T(8,128)(2,1)S(1)}, bf16[4,24,768]{2,1,0:T(8,128)(2,1)S(1)}, u32[]{:S(2)}, u32[]{:S(2)}) collective-permute-start(bf16[4,24,768]{2,1,0:T(8,128)(2,1)S(1)} %dynamic-slice_bitcast_fusion.13), channel_id=1, source_target_pairs={{0,4},{1,5},{2,6},{3,7},{4,0},{5,1},{6,2},{7,3},{8,12},{9,13},{10,... | collective-permute-start | bytes 442376 | tf_op jit(solution)/shard_map/ppermute | solution.py:367
  341.2 5.5 collective-permute-start.17
  348.5 118.9 %all-gather.11.cloned.1.call-start = ((), (), s32[]{:S(2)}) async-start(), calls=%async_computation.7 | async-start | bytes 1769472 | tf_op jit(solution)/shard_map/all_gather | solution.py:916
  351.0 14.7 %collective-permute-start.11 = (bf16[2,2,2,2,24,768]{5,4,0,1,2,3:T(8,128)(2,1)S(1)}, bf16[2,2,2,2,24,768]{5,4,0,1,2,3:T(8,128)(2,1)S(1)}, u32[]{:S(2)}, u32[]{:S(2)}) collective-permute-start(bf16[2,2,2,2,24,768]{5,4,0,1,2,3:T(8,128)(2,1)S(1)} %bitcast.457), channel_id=1, source_target_pairs={{0,16},{8,24},{16,0},{24,8},{1,17},{9,25},{17,1},{25,9},{2,18},{10... | collective-permute-start | bytes 1769480 | tf_op jit(solution)/shard_map/ppermute | solution.py:367
  352.7 19.5 %collective-permute-start.21 = (bf16[2,2,2,2,24,768]{5,4,3,2,1,0:T(8,128)(2,1)S(1)}, bf16[2,2,2,2,24,768]{5,4,3,2,1,0:T(8,128)(2,1)S(1)}, u32[]{:S(2)}, u32[]{:S(2)}) collective-permute-start(bf16[2,2,2,2,24,768]{5,4,3,2,1,0:T(8,128)(2,1)S(1)} %dynamic-slice_bitcast_fusion.3), channel_id=1, source_target_pairs={{0,1},{1,0},{2,3},{3,2},{4,5},{5,4},{6,7},{7,6},{8,9},{9,8},{10,11... | collective-permute-start | bytes 1769480 | tf_op jit(solution)/shard_map/ppermute | solution.py:367
  365.8 10.9 %collective-permute-start.18 = (bf16[2,2,2,24,768]{4,3,0,1,2:T(8,128)(2,1)S(1)}, bf16[2,2,2,24,768]{4,3,0,1,2:T(8,128)(2,1)S(1)}, u32[]{:S(2)}, u32[]{:S(2)}) collective-permute-start(bf16[2,2,2,24,768]{4,3,0,1,2:T(8,128)(2,1)S(1)} %dynamic-slice_bitcast_fusion.7), channel_id=1, source_target_pairs={{0,1},{1,0},{2,3},{3,2},{4,5},{5,4},{6,7},{7,6},{8,9},{9,8},{10,11... | collective-permute-start | bytes 884744 | tf_op jit(solution)/shard_map/ppermute | solution.py:367
  372.4 9.2 %collective-permute-start.22 = (bf16[2,2,2,24,768]{4,3,2,1,0:T(8,128)(2,1)S(1)}, bf16[2,2,2,24,768]{4,3,2,1,0:T(8,128)(2,1)S(1)}, u32[]{:S(2)}, u32[]{:S(2)}) collective-permute-start(bf16[2,2,2,24,768]{4,3,2,1,0:T(8,128)(2,1)S(1)} %dynamic-slice_bitcast_fusion.6), channel_id=1, source_target_pairs={{0,2},{1,3},{2,0},{3,1},{4,6},{5,7},{6,4},{7,5},{8,10},{9,11},{10,... | collective-permute-start | bytes 884744 | tf_op jit(solution)/shard_map/ppermute | solution.py:367
  376.8 13.0 %collective-permute-start.19 = (bf16[2,2,24,768]{3,2,0,1:T(8,128)(2,1)S(1)}, bf16[2,2,24,768]{3,2,0,1:T(8,128)(2,1)S(1)}, u32[]{:S(2)}, u32[]{:S(2)}) collective-permute-start(bf16[2,2,24,768]{3,2,0,1:T(8,128)(2,1)S(1)} %dynamic-slice_bitcast_fusion.11), channel_id=1, source_target_pairs={{0,2},{1,3},{2,0},{3,1},{4,6},{5,7},{6,4},{7,5},{8,10},{9,11},{10,... | collective-permute-start | bytes 442376 | tf_op jit(solution)/shard_map/ppermute | solution.py:367
  381.7 18.6 %collective-permute-start.23 = (bf16[2,2,24,768]{3,2,1,0:T(8,128)(2,1)S(1)}, bf16[2,2,24,768]{3,2,1,0:T(8,128)(2,1)S(1)}, u32[]{:S(2)}, u32[]{:S(2)}) collective-permute-start(bf16[2,2,24,768]{3,2,1,0:T(8,128)(2,1)S(1)} %dynamic-slice_bitcast_fusion.10), channel_id=1, source_target_pairs={{0,4},{1,5},{2,6},{3,7},{4,0},{5,1},{6,2},{7,3},{8,12},{9,13},{10,... | collective-permute-start | bytes 442376 | tf_op jit(solution)/shard_map/ppermute | solution.py:367
  389.8 14.8 %collective-permute-start.20 = (bf16[2,24,768]{2,1,0:T(8,128)(2,1)S(1)}, bf16[2,24,768]{2,1,0:T(8,128)(2,1)S(1)}, u32[]{:S(2)}, u32[]{:S(2)}) collective-permute-start(bf16[2,24,768]{2,1,0:T(8,128)(2,1)S(1)} %dynamic-slice_bitcast_fusion.15), channel_id=1, source_target_pairs={{0,4},{1,5},{2,6},{3,7},{4,0},{5,1},{6,2},{7,3},{8,12},{9,13},{10,... | collective-permute-start | bytes 221192 | tf_op jit(solution)/shard_map/ppermute | solution.py:367
  400.4 5.6 collective-permute-start.24
  406.7 16.6 %copy-start.22 = (f32[4,24,768]{2,1,0:T(8,128)}, f32[4,24,768]{2,1,0:T(8,128)S(1)}, u32[]{:S(2)}) copy-start(f32[4,24,768]{2,1,0:T(8,128)S(1)} %pad_maximum_fusion.6) | copy-start | bytes 884740
  407.5 7.1 %collective-permute-start.25 = (bf16[2,96,768]{2,1,0:T(8,128)(2,1)}, bf16[2,96,768]{2,1,0:T(8,128)(2,1)S(1)}, u32[]{:S(2)}, u32[]{:S(2)}) collective-permute-start(bf16[2,96,768]{2,1,0:T(8,128)(2,1)} %get-tuple-element.239), channel_id=1, source_target_pairs={{0,16},{8,24},{16,0},{24,8},{1,17},{9,25},{17,1},{25,9},{2,18},{10... | collective-permute-start | bytes 884744 | tf_op jit(solution)/shard_map/ppermute | solution.py:367
  417.2 7.4 %collective-permute-start.26 = (bf16[2,2,96,768]{3,2,1,0:T(8,128)(2,1)}, bf16[2,2,96,768]{3,2,1,0:T(8,128)(2,1)}, u32[]{:S(2)}, u32[]{:S(2)}) collective-permute-start(bf16[2,2,96,768]{3,2,1,0:T(8,128)(2,1)} %maximum_select_fusion.4), channel_id=1, source_target_pairs={{0,8},{8,0},{16,24},{24,16},{1,9},{9,1},{17,25},{25,17},{2,10},{10... | collective-permute-start | bytes 1769480 | tf_op jit(solution)/shard_map/ppermute | solution.py:367
  438.8 34.6 %all-to-all-start.2 = ((bf16[8,96,384]{2,1,0:T(8,128)(2,1)}), bf16[8,96,384]{2,1,0:T(8,128)(2,1)}, u32[]{:S(2)}, u32[]{:S(2)}) async-start(bf16[8,96,384]{2,1,0:T(8,128)(2,1)} %bitcast.456), calls=%async_computation.2 | async-start | bytes 1179648 | tf_op jit(solution)/shard_map/all_to_all | solution.py:958
  486.3 18.1 %all-to-all-start.3 = ((bf16[4,5,32,768]{3,2,1,0:T(8,128)(2,1)}), bf16[4,5,32,768]{3,2,1,0:T(8,128)(2,1)}, u32[]{:S(2)}, u32[]{:S(2)}) async-start(bf16[4,5,32,768]{3,2,1,0:T(8,128)(2,1)} %attend_update.1), calls=%async_computation.3 | async-start | bytes 1966080 | tf_op jit(solution)/shard_map/all_to_all | solution.py:371
  490.5 18.6 %copy-start.67 = (f32[1024]{0:T(1024)S(1)}, f32[1024]{0:T(1024)}, u32[]{:S(2)}) copy-start(f32[1024]{0:T(1024)} %copy-done.66) | copy-start | bytes 12292
  504.3 40.8 %all-to-all-start.4 = ((bf16[4,496,768]{2,1,0:T(8,128)(2,1)}), bf16[4,496,768]{2,1,0:T(8,128)(2,1)}, u32[]{:S(2)}, u32[]{:S(2)}) async-start(bf16[4,496,768]{2,1,0:T(8,128)(2,1)} %constant_dynamic-update-slice_fusion), calls=%async_computation.4 | async-start | bytes 6094848 | tf_op jit(solution)/shard_map/all_to_all | solution.py:371
  (66 other events, 236.4 us)
Sparse Core Ops, SparseCore 0:
  12.9 122.2 all-gather.6
  212.7 79.9 all-gather.12
  348.6 62.1 all-gather.8
  413.5 53.8 all-gather.10

commit v4 on v3

--- a/solution.py
+++ b/solution.py
@@ -382,12 +382,25 @@
     )
 
 
-def after(value, *first):
-    return lax.optimization_barrier((value,) + first)[0]
-
-
 def add_low(left, right):
     return low(left.astype(jnp.float32) + right.astype(jnp.float32))
+
+
+def copy_kernel(value_ref, *rest):
+    rest[-1][...] = value_ref[...]
+
+
+def behind(value, *first):
+    rows = value.reshape(-1, value.shape[-1])
+    vmem = pl.BlockSpec(memory_space=pltpu.VMEM)
+    return pl.pallas_call(
+        copy_kernel,
+        in_specs=[vmem] + [pl.BlockSpec(memory_space=pl.ANY)] * len(first),
+        out_specs=vmem,
+        out_shape=jax.ShapeDtypeStruct(rows.shape, rows.dtype),
+        compiler_params=params(),
+        name="behind",
+    )(rows, *first).reshape(value.shape)
 
 
 def dp_bits():
@@ -407,9 +420,8 @@
         self.got = flip(sent, axis, 1 << shift)
         self.dims.pop(place)
 
-    def finish(self, last=False, first=None):
-        got = self.got if first is None else after(self.got, first)
-        total = self.kept.astype(jnp.float32) + got.astype(jnp.float32)
+    def finish(self, last=False):
+        total = self.kept.astype(jnp.float32) + self.got.astype(jnp.float32)
         self.blocks = total if last else low(total)
 
 
@@ -418,13 +430,15 @@
     return list(zip(["x"] + bits, bits + ["x"]))
 
 
-def one_round(one, other, i, first=None):
+def one_round(one, other, i, ready=()):
     left, right = rounds()[i]
     last = i == len(rounds()) - 1
     one.start(left)
     other.start(right)
-    one.finish(last, first)
-    other.finish(last, first)
+    if ready:
+        one.got = behind(one.got, *ready)
+    one.finish(last)
+    other.finish(last)
     return [mark(one.blocks), mark(other.blocks)]
 
 
@@ -754,7 +768,6 @@
     shrink_bias = vectors[7]
     expand_bias = vectors[8:].reshape(owners, groups, block).transpose(1, 0, 2).reshape(1, -1)
     normed_ext = low(normalize(input_ext.astype(jnp.float32), gain_one, bias_one))
-    over_chip, normed_ext = lax.optimization_barrier((over_chip, normed_ext))
     over_core = ordered(core, over_chip, flip(over_chip, "seq", 1), 2)
     qkv_t = over_core.reshape(3 * model_width, model_width)
     normed_low = normed_ext[:, WIN : WIN + block_size].reshape(token_rows, model_width)
@@ -766,18 +779,16 @@
     value_ext = low(nt(ext_rows, qkv_t[2 * model_width :]) + value_bias).reshape(
         text_count, wide, model_width
     )
-    roots = swap(after(root_parts, mark(query_low)))
     base = (seq_index * block_size).astype(jnp.int32).reshape(1)
     attended, totals = run_forward(lengths, base, query_low, key_ext, value_ext)
+    roots = swap(behind(root_parts, attended))
     attended_low = attended.reshape(token_rows, model_width)
 
     out_t = packed_all[:, :model_width]
     layer_input = characters.astype(jnp.float32).reshape(token_rows, model_width)
     middle = layer_input + nt(attended_low, out_t) + out_bias
     normed_two_low = low(normalize(middle, gain_two, bias_two))
-    normed_two_low, roots = lax.optimization_barrier((normed_two_low, roots))
     cut = 2 * hidden_block + block
-    root_all = lax.all_gather(roots[:, cut:], "dp", axis=1)
     upstream = cotangent.reshape(token_rows, model_width)
     gated_low, expanded_grad, expand_sums, forward, normed_two_grad = run_gate(
         normed_two_low, upstream, packed_all, expand_bias
@@ -824,6 +835,7 @@
         (0, early), lengths, base, query_low, key_ext, value_ext, attended_grad, totals, (), marks
     )
     marks = one_round(shrink_sum, expand_sum, 0)
+    root_all = lax.all_gather(behind(roots[:, cut:], *marks), "dp", axis=1)
     kept = run_backward(
         (early, pairs - early),
         lengths,
@@ -837,7 +849,7 @@
         marks,
     )
     query_grad, key_grad, value_grad = kept
-    marks = one_round(shrink_sum, expand_sum, 1)
+    one_round(shrink_sum, expand_sum, 1)
 
     pair_grad = jnp.stack([key_grad, value_grad])
     from_above = lax.ppermute(
@@ -846,7 +858,6 @@
     from_below = lax.ppermute(
         pair_grad[:, :, block_size + WIN :], "seq", [(i, i + 1) for i in range(ends)]
     )
-    from_above = after(from_above, mark(root_all), *marks)
     pair_own = pair_grad[:, :, WIN : WIN + block_size]
     pair_low = jnp.concatenate(
         [
@@ -869,9 +880,7 @@
     core_sum.start("c")
     core_sum.finish()
     for i in range(2, len(rounds())):
-        marks = one_round(
-            shrink_sum, expand_sum, i, mark(core_sum.kept if i == 2 else core_sum.blocks)
-        )
+        one_round(shrink_sum, expand_sum, i)
     shrink_own, expand_own = shrink_sum.blocks, expand_sum.blocks
     hidden_own = jnp.stack(
         [low(own).reshape(hidden_block, model_width) for own in (shrink_own, expand_own)]
@@ -881,8 +890,20 @@
         Halving(core_sum.blocks[:, i], ["x", None] + list(range(bits - 1, -1, -1)))
         for i in range(2)
     ]
+    expand_rc = roots[:, :hidden_block].reshape(seq_count * hidden_block, part)
+    attend_rc = roots[:, hidden_block : hidden_block + block].reshape(rows_own, model_width)
+    shrink_lr = roots[:, hidden_block + block : cut].reshape(seq_count * hidden_block, part)
+    attend_lw = root_all[:, :, :block].reshape(model_width, model_width)
+    expand_lw = root_all[:, :, block : 2 * block].reshape(model_width, model_width)
+    shrink_rt = root_all[:, :, 2 * block :].transpose(1, 0, 2, 3).reshape(model_width, model_width)
+
+    panels = lax.all_gather(hidden_own, "dp", axis=1, tiled=True)
+    row_sets = ordered(chip, hidden_own, flip(hidden_own, "seq", 2), 0)
+    row_sets = ordered(core, row_sets, flip(row_sets, "seq", 1), 1)
+    row_sets = row_sets.reshape((seq_count,) + hidden_own.shape)
+    ready = (row_sets, expand_rc, expand_lw, shrink_lr, shrink_rt, attend_rc, attend_lw)
     for i in range(len(rounds())):
-        one_round(*halves, i, jnp.stack(marks) if i == 0 else None)
+        one_round(*halves, i, ready=ready if i == len(rounds()) - 1 else ())
     attend_own = jnp.concatenate([half.blocks for half in halves])
     grad_query_bias = jnp.sum(query_rows.astype(jnp.float32), axis=0)
     grad_value_bias = jnp.sum(pair_low[1].astype(jnp.float32), axis=0)
@@ -930,17 +951,6 @@
         .reshape(model_width, model_width)
     )
 
-    expand_rc = roots[:, :hidden_block].reshape(seq_count * hidden_block, part)
-    attend_rc = roots[:, hidden_block : hidden_block + block].reshape(rows_own, model_width)
-    shrink_lr = roots[:, hidden_block + block : cut].reshape(seq_count * hidden_block, part)
-    attend_lw = root_all[:, :, :block].reshape(model_width, model_width)
-    expand_lw = root_all[:, :, block : 2 * block].reshape(model_width, model_width)
-    shrink_rt = root_all[:, :, 2 * block :].transpose(1, 0, 2, 3).reshape(model_width, model_width)
-
-    panels = lax.all_gather(hidden_own, "dp", axis=1, tiled=True)
-    row_sets = ordered(chip, hidden_own, flip(hidden_own, "seq", 2), 0)
-    row_sets = ordered(core, row_sets, flip(row_sets, "seq", 1), 1)
-    row_sets = row_sets.reshape((seq_count,) + hidden_own.shape)
     index = dp_index.astype(jnp.int32)
     products, turned = run_hidden(
         seq_count,
@@ -981,7 +991,7 @@
         attend_rc,
         attend_lw,
         attend_all[:, rows_own:],
-        mark(to_owners),
+        mark(back),
     )
     returned = swap(to_return)
     vector_sum = from_halves(returned[:, 4])[: vectors.shape[0]]

time: 577 us -> 562 us (0.974)
  matrix products: 47.8 us -> 56 us
  starting transfers between devices: 59 us -> 51.2 us
  local copies, waits for them, and re-layouts: 90.8 us -> 83.6 us
  other arithmetic: 79.6 us -> 72.8 us
  waiting for transfers between devices: 185 us -> 179 us
    all_to_all x1, waiting for transfers between devices: 0.01 us -> 10.1 us  [shards(): lax.all_to_all(turned.reshape(dp_count, rows_own, seq_count * hidden_bloc...]
    ppermute x23, starting transfers between devices: 27.6 us -> 18.9 us  [flip(): return lax.ppermute(blocks, axis, [(i, i ^ mask) for i in range(count)])]
    dot_general x4, matrix products: 9.19 us -> 17.6 us  [nn(): return jnp.dot(left_rows, right_cols, preferred_element_type=jnp.float32)]
    convert_element_type x29, other arithmetic: 28.7 us -> 21.2 us  [low(): return values.astype(jnp.bfloat16)]
    all_to_all x3, waiting for transfers between devices: 38.7 us -> 31.2 us  [swap(): lax.all_to_all(blocks, 'seq', split_axis=0, concat_axis=0, tiled=True)]
    all_gather x1, waiting for transfers between devices: 6.91 us -> 0.01 us  [shards(): packed_all = lax.all_gather(packed, both, axis=0, tiled=True)]
    pallas_call x0 -> x3, Pallas kernels: none -> 6.18 us  [behind(): pl.pallas_call(copy_kernel, in_specs=[vmem] + [pl.BlockSpec(memory_space=...]
    unnamed x164 -> x156, local copies, waits for them, and re-layouts: 21 us -> 19.4 us
  transfers between devices with their start and end apart: 36 -> 36, of which waited for: 19 -> 18; matrix products, arithmetic and copies ran while one was open for 26% -> 27% of each run, Pallas kernels for 8% -> 7%
where the time goes in v4:
time: 562 us; the launch traced here: 556 us
  waiting for transfers between devices  179 us (32%)
  Pallas kernels  94.9 us (17%)
  local copies, waits for them, and re-layouts  83.6 us (15%)
  other arithmetic  72.8 us (13%)
  matrix products  56 us (10%)
  starting transfers between devices  51.2 us (9%)
  between operations  18.4 us (3%)
    ppermute x23, waiting for transfers between devices, flip(): return lax.ppermute(blocks, axis, [(i, i ^ mask) for i in range(count)])  102 us
    pallas_call x1, Pallas kernels, run_gate(): pl.pallas_call(gate_kernel, grid=(groups, tiles), in_specs=[row_spec, row...  36.9 us
    all_to_all x3, waiting for transfers between devices, swap(): lax.all_to_all(blocks, 'seq', split_axis=0, concat_axis=0, tiled=True)  31.2 us
    dot_general x6, matrix products, across(): lax.dot_general(left_rows, right_rows, (((0,), (0,)), ((), ())), preferre...  25.6 us
    pallas_call x2, Pallas kernels, run_backward(): pl.pallas_call(functools.partial(attend_backward, blocks, len(others)), g...  22.3 us
    convert_element_type x29, other arithmetic, low(): return values.astype(jnp.bfloat16)  21.2 us
    unnamed x156, local copies, waits for them, and re-layouts  19.4 us
    ppermute x23, starting transfers between devices, flip(): return lax.ppermute(blocks, axis, [(i, i ^ mask) for i in range(count)])  18.9 us
  transfers between devices with their start and end apart: 36, of which 18 were waited for; matrix products, arithmetic and copies ran while one was open for 27% of the time, Pallas kernels for 7%

profile of v4, /device:TPU:0, one launch (start us, length us, event | category | flops | bytes accessed | tf_op | source)
XLA Modules:
  0.0 556.3 jit_solution(15786529682302026881)
XLA Ops:
  13.8 7.3 %all-to-all-start = ((bf16[8,3,24,768]{3,2,1,0:T(8,128)(2,1)}), bf16[8,3,24,768]{3,2,1,0:T(8,128)(2,1)}, u32[]{:S(2)}, u32[]{:S(2)}) async-start(bf16[8,3,24,768]{3,2,1,0:T(8,128)(2,1)} %broadcast_in_dim.16), calls=%async_computation | async-start | bytes 1769472 | tf_op jit(solution)/shard_map/all_to_all | solution.py:376
  32.1 18.6 %all-to-all-done = bf16[8,3,24,768]{3,2,1,0:T(8,128)(2,1)} async-done(((bf16[8,3,24,768]{3,2,1,0:T(8,128)(2,1)}), bf16[8,3,24,768]{3,2,1,0:T(8,128)(2,1)}, u32[]{:S(2)}, u32[]{:S(2)}) %all-to-all-start) | async-done | bytes 884768 | tf_op jit(solution)/shard_map/all_to_all | solution.py:376
  58.2 23.1 %collective-permute-done.2 = bf16[3,8,24,768]{3,2,1,0:T(8,128)(2,1)S(1)} collective-permute-done((bf16[3,8,24,768]{3,2,1,0:T(8,128)(2,1)S(1)}, bf16[3,8,24,768]{3,2,1,0:T(8,128)(2,1)S(1)}, u32[]{:S(2)}, u32[]{:S(2)}) %collective-permute-start.2) | collective-permute-done | bytes 884768 | tf_op jit(solution)/shard_map/ppermute | solution.py:367
  89.6 4.4 copy.183
  102.2 2.5 add_convert_fusion.4
  104.8 3.4 convolution_convert_fusion.2
  108.2 3.5 add_convert_fusion
  111.7 14.6 %attend_forward.1 = (bf16[2,512,768]{2,1,0:T(8,128)(2,1)}, f32[2,6,8,128]{3,2,1,0:T(8,128)}) custom-call(s32[2]{0:T(128)} %lengths.5, s32[1]{0:T(128)} %bitcast.1.base, bf16[2,512,768]{2,1,0:T(8,128)(2,1)} %bitcast.439, bf16[2,768,768]{2,1,0:T(8,128)(2,1)} %bitcast.420, bf16[2,768,768]{2,1,0:T(8,128)(2,1)} %bitcast.423), custom_call_target="tpu_custom_call" | custom-call | flops 2415919104 | bytes 7864320 | tf_op jit(solution)/shard_map/attend_forward/pallas_call | solution.py:191
  126.3 2.9 behind.3
  129.2 4.5 all-to-all-start.1
  137.1 18.8 %all-to-all-done.1 = bf16[4,288,768]{2,1,0:T(8,128)(2,1)} async-done(((bf16[4,288,768]{2,1,0:T(8,128)(2,1)}), bf16[4,288,768]{2,1,0:T(8,128)(2,1)}, u32[]{:S(2)}, u32[]{:S(2)}) %all-to-all-start.1) | async-done | bytes 1769504 | tf_op jit(solution)/shard_map/all_to_all | solution.py:371
  159.4 3.3 fusion.72
  164.9 36.9 %gate.1 = (bf16[1024,3072]{1,0:T(8,128)(2,1)}, bf16[1024,3072]{1,0:T(8,128)(2,1)}, f32[2,8,3072]{2,1,0:T(8,128)}, f32[1024,768]{1,0:T(8,128)}, f32[1024,768]{1,0:T(8,128)}) custom-call(bf16[1024,768]{1,0:T(8,128)(2,1)} %add_convert_fusion.3.rows_ref, bf16[1024,768]{1,0:T(8,128)(2,1)} %bitcast.388, ...), custom_call_target="tpu_custom_call" | custom-call | flops 2415919104 | bytes 25165824 | tf_op jit(solution)/shard_map/gate/pallas_call | solution.py:330
  201.7 9.9 %convolution_convert_fusion = bf16[3072,768]{1,0:T(8,128)(2,1)} fusion(bf16[1024,3072]{1,0:T(8,128)(2,1)} %get-tuple-element.40, bf16[1024,768]{1,0:T(8,128)(2,1)S(1)} %copy-done.22), kind=kOutput, calls=%fused_computation.8 | convolution fusion | flops 4834197504 | bytes 12582912 | tf_op jit(solution)/shard_map/dot_general | solution.py:46
  211.7 6.9 %convolution_convert_fusion.1 = bf16[3072,768]{1,0:T(8,128)(2,1)} fusion(bf16[1024,3072]{1,0:T(8,128)(2,1)S(1)} %copy-done.72, bf16[1024,768]{1,0:T(8,128)(2,1)S(1)} %bitcast.389), kind=kOutput, calls=%fused_computation.9 | convolution fusion | flops 4834197504 | bytes 12582912 | tf_op jit(solution)/shard_map/dot_general | solution.py:46
  218.6 6.7 %constant_dynamic-slice_fusion.3 = (bf16[4,2,1,2,2,2,24,768]{7,6,5,4,3,2,1,0:T(8,128)(2,1)S(1)}, bf16[4,2,1,2,2,2,24,768]{7,6,5,4,3,2,1,0:T(8,128)(2,1)}, bf16[4...) fusion(bf16[4,2,2,2,2,2,24,768]{7,6,5,4,3,2,1,0:T(8,128)(2,1)} %bitcast.412, ...), kind=kLoop, calls=%fused_computation.199 | loop fusion | bytes 18874376 | tf_op jit(solution)/shard_map/jit(dynamic_index_in_dim)/dynamic_slice | solution.py:419
  227.3 2.5 fusion.68
  233.6 2.6 fusion.63
  237.9 4.4 convolution_convert_fusion.3
  251.6 4.5 fusion.24
  259.2 14.1 %attend_backward.2 = (bf16[2,512,768]{2,1,0:T(8,128)(2,1)}, bf16[2,768,768]{2,1,0:T(8,128)(2,1)}, bf16[2,768,768]{2,1,0:T(8,128)(2,1)}) custom-call(s32[2]{0:T(128)} %lengths.5, s32[1]{0:T(128)} %bitcast.1.base, bf16[2,512,768]{2,1,0:T(8,128)(2,1)} %bitcast.440, bf16[2,768,768]{2,1,0:T(8,128)(2,1)} %bitcast.421, bf16[2,768,768]{2,1,0:T(8,128)(2,1)} %bitcast.424, ...), custom_call_target="tpu_custom_call" | custom-call | flops 4026531840 | bytes 7864320 | tf_op jit(solution)/shard_map/attend_backward/pallas_call | solution.py:222
  284.0 8.2 %attend_backward.3 = (bf16[2,512,768]{2,1,0:T(8,128)(2,1)}, bf16[2,768,768]{2,1,0:T(8,128)(2,1)}, bf16[2,768,768]{2,1,0:T(8,128)(2,1)}) custom-call(s32[2]{0:T(128)} %lengths.5, s32[1]{0:T(128)} %bitcast.1.base, bf16[2,512,768]{2,1,0:T(8,128)(2,1)} %bitcast.441, ...), custom_call_target="tpu_custom_call", output_to_operand_aliasing={{0}: (7, {}), {1}: (8, {}), {2}: (9, {})} | custom-call | flops 2013265920 | bytes 7864320 | tf_op jit(solution)/shard_map/attend_backward/pallas_call | solution.py:222
  296.8 3.1 fusion.73
  304.8 12.0 %collective-permute-done.18 = bf16[4,2,2,24,768]{4,3,0,1,2:T(8,128)(2,1)S(1)} collective-permute-done((bf16[4,2,2,24,768]{4,3,0,1,2:T(8,128)(2,1)S(1)}, bf16[4,2,2,24,768]{4,3,0,1,2:T(8,128)(2,1)S(1)}, u32[]{:S(2)}, u32[]{:S(2)}) %collective-permute-start.18) | collective-permute-done | bytes 589856 | tf_op jit(solution)/shard_map/ppermute | solution.py:367
  328.7 3.0 fusion.74
  331.8 16.4 %collective-permute-done.19 = bf16[4,2,24,768]{3,2,0,1:T(8,128)(2,1)S(1)} collective-permute-done((bf16[4,2,24,768]{3,2,0,1:T(8,128)(2,1)S(1)}, bf16[4,2,24,768]{3,2,0,1:T(8,128)(2,1)S(1)}, u32[]{:S(2)}, u32[]{:S(2)}) %collective-permute-start.19) | collective-permute-done | bytes 294944 | tf_op jit(solution)/shard_map/ppermute | solution.py:367
  349.7 3.7 collective-permute-done.20
  353.5 8.3 %collective-permute-done.17 = bf16[4,24,768]{2,1,0:T(8,128)(2,1)S(1)} collective-permute-done((bf16[4,24,768]{2,1,0:T(8,128)(2,1)S(1)}, bf16[4,24,768]{2,1,0:T(8,128)(2,1)S(1)}, u32[]{:S(2)}, u32[]{:S(2)}) %collective-permute-start.17) | collective-permute-done | bytes 147488 | tf_op jit(solution)/shard_map/ppermute | solution.py:367
  364.4 7.1 %fusion.61 = (f32[768]{0:T(1024)S(1)}, f32[1024]{0:T(1024)S(1)}, f32[1024,768]{1,0:T(8,128)}) fusion(f32[768]{0:T(1024)S(1)} %get-tuple-element.168, f32[1024]{0:T(1024)S(1)} %bitcast.476, bf16[2,512,768]{2,1,0:T(8,128)(2,1)S(1)} %copy-done, bf16[1024,768]{1,0:T(8,128)(2,1)} %bitcast.399, bf16[768,768]{1,0:T(8,128)(2,1)} %bitcast.403, ...), kind=kOutput, calls=%fused_computation.231 | convolution fusion | flops 1214249216 | bytes 13776896 | tf_op jit(solution)/shard_map/dot_general | solution.py:42
  373.0 3.0 fusion.6
  384.2 11.5 %collective-permute-done.23 = bf16[2,2,2,2,24,768]{5,4,1,2,3,0:T(8,128)(2,1)S(1)} collective-permute-done((bf16[2,2,2,2,24,768]{5,4,1,2,3,0:T(8,128)(2,1)S(1)}, bf16[2,2,2,2,24,768]{5,4,1,2,3,0:T(8,128)(2,1)S(1)}, u32[]{:S(2)}, u32[]{:S(2)}) %collective-permute-start.23) | collective-permute-done | bytes 589856 | tf_op jit(solution)/shard_map/ppermute | solution.py:367
  398.5 10.0 %collective-permute-done.24 = bf16[2,2,2,24,768]{4,3,1,2,0:T(8,128)(2,1)S(1)} collective-permute-done((bf16[2,2,2,24,768]{4,3,1,2,0:T(8,128)(2,1)S(1)}, bf16[2,2,2,24,768]{4,3,1,2,0:T(8,128)(2,1)S(1)}, u32[]{:S(2)}, u32[]{:S(2)}) %collective-permute-start.24) | collective-permute-done | bytes 294944 | tf_op jit(solution)/shard_map/ppermute | solution.py:367
  408.8 2.8 collective-permute-start.13
  411.6 11.2 %collective-permute-done.25 = bf16[2,2,24,768]{3,2,1,0:T(8,128)(2,1)S(1)} collective-permute-done((bf16[2,2,24,768]{3,2,1,0:T(8,128)(2,1)S(1)}, bf16[2,2,24,768]{3,2,1,0:T(8,128)(2,1)S(1)}, u32[]{:S(2)}, u32[]{:S(2)}) %collective-permute-start.25) | collective-permute-done | bytes 147488 | tf_op jit(solution)/shard_map/ppermute | solution.py:367
  422.9 2.3 collective-permute-done.13
  427.3 3.7 fusion.64
  437.0 10.4 %hidden_update.1 = (bf16[4,400,768]{2,1,0:T(8,128)(2,1)}, bf16[768,384]{1,0:T(8,128)(2,1)}) custom-call(s32[1]{0:T(128)} %bitcast.50.index_ref, bf16[2,768,768]{2,1,0:T(8,128)(2,1)} %all-gather.10.cloned.1.call-done.panels_ref, bf16[4,2,96,768]{3,2,1,0:T(8,128)(2,1)} %bitcast.408, bf16[384,768]{1,0:T(8,128)(2,1)} %bitcast.429, bf16[768,768]{1,0:T(8,128)(2,1)} %bitcast.405, ...), custom_call_target="tpu_custom_call" | custom-call | flops 2264924160 | bytes 7077888 | tf_op jit(solution)/shard_map/hidden_update/pallas_call | solution.py:555
  447.4 4.3 all-to-all-start.2
  455.5 10.1 %all-to-all-done.2 = bf16[8,96,384]{2,1,0:T(8,128)(2,1)} async-done(((bf16[8,96,384]{2,1,0:T(8,128)(2,1)}), bf16[8,96,384]{2,1,0:T(8,128)(2,1)}, u32[]{:S(2)}, u32[]{:S(2)}) %all-to-all-start.2) | async-done | bytes 589856 | tf_op jit(solution)/shard_map/all_to_all | solution.py:968
  465.6 2.3 copy.252
  468.0 2.8 reshape.762
  470.7 3.7 pad_maximum_fusion.2
  474.5 4.8 all-to-all-start.3
  479.3 4.5 add_convert_fusion.1
  483.8 17.1 %all-gather.12.cloned.1.call-done = bf16[1024,768]{1,0:T(8,128)(2,1)} async-done(((bf16[128,768]{1,0:T(8,128)(2,1)}), bf16[1024,768]{1,0:T(8,128)(2,1)}) %all-gather.12.cloned.1.call-update) | async-done | bytes 1572880 | tf_op jit(solution)/shard_map/all_gather | solution.py:937
  505.1 10.1 %all-to-all-done.3 = bf16[4,496,768]{2,1,0:T(8,128)(2,1)} async-done(((bf16[4,496,768]{2,1,0:T(8,128)(2,1)}), bf16[4,496,768]{2,1,0:T(8,128)(2,1)}, u32[]{:S(2)}, u32[]{:S(2)}) %all-to-all-start.3) | async-done | bytes 3047456 | tf_op jit(solution)/shard_map/all_to_all | solution.py:371
  521.0 4.6 attend_update.1
  525.7 4.4 all-to-all-start.4
  (387 shorter events, 157.0 us)
Async XLA Ops:
  7.2 152.2 %all-gather.6.cloned.1.call-start = ((), (), s32[]{:S(2)}) async-start(), calls=%async_computation.5 | async-start | bytes 10948608 | tf_op jit(solution)/shard_map/all_gather | solution.py:736
  11.9 9.2 %copy-start = (bf16[2,512,768]{2,1,0:T(8,128)(2,1)S(1)}, bf16[2,512,768]{2,1,0:T(8,128)(2,1)}, u32[]{:S(2)}) copy-start(bf16[2,512,768]{2,1,0:T(8,128)(2,1)} %param.23) | copy-start | bytes 4718596
  13.8 36.8 %all-to-all-start = ((bf16[8,3,24,768]{3,2,1,0:T(8,128)(2,1)}), bf16[8,3,24,768]{3,2,1,0:T(8,128)(2,1)}, u32[]{:S(2)}, u32[]{:S(2)}) async-start(bf16[8,3,24,768]{3,2,1,0:T(8,128)(2,1)} %broadcast_in_dim.16), calls=%async_computation | async-start | bytes 1769472 | tf_op jit(solution)/shard_map/all_to_all | solution.py:376
  22.8 60.0 %collective-permute-start = (bf16[2,128,768]{1,2,0:T(8,128)(2,1)}, bf16[2,128,768]{1,2,0:T(8,128)(2,1)S(1)}, u32[]{:S(2)}, u32[]{:S(2)}) collective-permute-start(bf16[2,128,768]{1,2,0:T(8,128)(2,1)} %get-tuple-element.206), channel_id=1, source_target_pairs={{0,8},{8,16},{16,24},{1,9},{9,17},{17,25},{2,10},{10,18},{18,26},{... | collective-permute-start | bytes 1179656 | tf_op jit(solution)/shard_map/ppermute | solution.py:714
  24.3 58.5 %collective-permute-start.1 = (bf16[2,128,768]{1,2,0:T(8,128)(2,1)}, bf16[2,128,768]{1,2,0:T(8,128)(2,1)}, u32[]{:S(2)}, u32[]{:S(2)}) collective-permute-start(bf16[2,128,768]{1,2,0:T(8,128)(2,1)} %get-tuple-element.207), channel_id=1, source_target_pairs={{8,0},{16,8},{24,16},{9,1},{17,9},{25,17},{10,2},{18,10},{26,18},{... | collective-permute-start | bytes 1179656 | tf_op jit(solution)/shard_map/ppermute | solution.py:717
  51.9 32.3 %copy-start.20 = (bf16[8,3,24,768]{3,2,0,1:T(8,128)(2,1)}, bf16[8,3,24,768]{3,2,0,1:T(8,128)(2,1)S(1)}, u32[]{:S(2)}) copy-start(bf16[8,3,24,768]{3,2,0,1:T(8,128)(2,1)S(1)} %copy.251) | copy-start | bytes 2654212
  51.9 29.4 %collective-permute-start.2 = (bf16[3,8,24,768]{3,2,1,0:T(8,128)(2,1)S(1)}, bf16[3,8,24,768]{3,2,1,0:T(8,128)(2,1)S(1)}, u32[]{:S(2)}, u32[]{:S(2)}) collective-permute-start(bf16[3,8,24,768]{3,2,1,0:T(8,128)(2,1)S(1)} %bitcast.393), channel_id=1, source_target_pairs={{0,16},{8,24},{16,0},{24,8},{1,17},{9,25},{17,1},{25,9},{2,18},{10... | collective-permute-start | bytes 2654216 | tf_op jit(solution)/shard_map/ppermute | solution.py:367
  82.8 15.2 %collective-permute-start.3 = (bf16[3,2,8,24,768]{4,3,2,1,0:T(8,128)(2,1)}, bf16[3,2,8,24,768]{4,3,2,1,0:T(8,128)(2,1)}, u32[]{:S(2)}, u32[]{:S(2)}) collective-permute-start(bf16[3,2,8,24,768]{4,3,2,1,0:T(8,128)(2,1)} %maximum_select_fusion.1), channel_id=1, source_target_pairs={{0,8},{8,0},{16,24},{24,16},{1,9},{9,1},{17,25},{25,17},{2,10},{10... | collective-permute-start | bytes 5308424 | tf_op jit(solution)/shard_map/ppermute | solution.py:367
  100.6 7.6 %copy-start.24 = (bf16[1,2,2,8,24,768]{5,4,3,2,1,0:T(8,128)(2,1)}, bf16[1,2,2,8,24,768]{5,4,3,2,1,0:T(8,128)(2,1)S(1)}, u32[]{:S(2)}) copy-start(bf16[1,2,2,8,24,768]{5,4,3,2,1,0:T(8,128)(2,1)S(1)} %get-tuple-element.191) | copy-start | bytes 3538948
  129.2 26.8 %all-to-all-start.1 = ((bf16[4,288,768]{2,1,0:T(8,128)(2,1)}), bf16[4,288,768]{2,1,0:T(8,128)(2,1)}, u32[]{:S(2)}, u32[]{:S(2)}) async-start(bf16[4,288,768]{2,1,0:T(8,128)(2,1)} %bitcast.396), calls=%async_computation.1 | async-start | bytes 3538944 | tf_op jit(solution)/shard_map/all_to_all | solution.py:371
  133.7 293.6 %all-gather.8.cloned.1.call-start = ((), (), s32[]{:S(2)}) async-start(), calls=%async_computation.6 | async-start | bytes 3981312 | tf_op jit(solution)/shard_map/all_gather | solution.py:838
  135.6 23.8 %copy-start.69 = (f32[768]{0:T(1024)S(1)}, f32[768]{0:T(1024)}, u32[]{:S(2)}) copy-start(f32[768]{0:T(1024)} %get-tuple-element.164) | copy-start | bytes 9220
  164.9 36.9 %copy-start.22 = (bf16[1024,768]{1,0:T(8,128)(2,1)S(1)}, bf16[1024,768]{1,0:T(8,128)(2,1)}, u32[]{:S(2)}) copy-start(bf16[1024,768]{1,0:T(8,128)(2,1)} %add_convert_fusion.3.rows_ref) | copy-start | bytes 4718596
  201.7 9.9 %copy-start.6 = (bf16[2,512,768]{2,1,0:T(8,128)(2,1)S(1)}, bf16[2,512,768]{2,1,0:T(8,128)(2,1)}, u32[]{:S(2)}) copy-start(bf16[2,512,768]{2,1,0:T(8,128)(2,1)} %param.24) | copy-start | bytes 4718596
  201.7 9.9 %copy-start.72 = (bf16[1024,3072]{1,0:T(8,128)(2,1)S(1)}, bf16[1024,3072]{1,0:T(8,128)(2,1)}, u32[]{:S(2)}) copy-start(bf16[1024,3072]{1,0:T(8,128)(2,1)} %get-tuple-element.39) | copy-start | bytes 18874372
  227.2 15.1 %collective-permute-start.4 = (bf16[4,2,2,2,2,24,768]{6,5,0,2,3,4,1:T(8,128)(2,1)S(1)}, bf16[4,2,2,2,2,24,768]{6,5,0,2,3,4,1:T(8,128)(2,1)S(1)}, u32[]{:S(2)}, u32[]{:S(2)}) collective-permute-start(bf16[4,2,2,2,2,24,768]{6,5,0,2,3,4,1:T(8,128)(2,1)S(1)} %bitcast.433), channel_id=1, source_target_pairs={{0,8},{8,0},{16,24},{24,16},{1,9},{9,1},{17,25},{25,17},{2,10},{10... | collective-permute-start | bytes 7077896 | tf_op jit(solution)/shard_map/ppermute | solution.py:367
  230.1 14.6 %collective-permute-start.5 = (bf16[4,2,2,2,2,24,768]{6,5,0,1,2,3,4:T(8,128)(2,1)S(1)}, bf16[4,2,2,2,2,24,768]{6,5,0,1,2,3,4:T(8,128)(2,1)S(1)}, u32[]{:S(2)}, u32[]{:S(2)}) collective-permute-start(bf16[4,2,2,2,2,24,768]{6,5,0,1,2,3,4:T(8,128)(2,1)S(1)} %bitcast.432), channel_id=1, source_target_pairs={{0,8},{8,0},{16,24},{24,16},{1,9},{9,1},{17,25},{25,17},{2,10},{10... | collective-permute-start | bytes 7077896 | tf_op jit(solution)/shard_map/ppermute | solution.py:367
  244.2 29.2 %collective-permute-start.6 = (bf16[4,2,2,2,24,768]{5,4,0,1,2,3:T(8,128)(2,1)}, bf16[4,2,2,2,24,768]{5,4,0,1,2,3:T(8,128)(2,1)}, u32[]{:S(2)}, u32[]{:S(2)}) collective-permute-start(bf16[4,2,2,2,24,768]{5,4,0,1,2,3:T(8,128)(2,1)} %dynamic-slice_bitcast_fusion.1), channel_id=1, source_target_pairs={{0,16},{8,24},{16,0},{24,8},{1,17},{9,25},{17,1},{25,9},{2,18},{10... | collective-permute-start | bytes 3538952 | tf_op jit(solution)/shard_map/ppermute | solution.py:367
  247.2 28.8 %collective-permute-start.7 = (bf16[4,2,2,2,24,768]{5,4,0,1,2,3:T(8,128)(2,1)}, bf16[4,2,2,2,24,768]{5,4,0,1,2,3:T(8,128)(2,1)}, u32[]{:S(2)}, u32[]{:S(2)}) collective-permute-start(bf16[4,2,2,2,24,768]{5,4,0,1,2,3:T(8,128)(2,1)} %dynamic-slice_bitcast_fusion), channel_id=1, source_target_pairs={{0,1},{1,0},{2,3},{3,2},{4,5},{5,4},{6,7},{7,6},{8,9},{9,8},{10,11... | collective-permute-start | bytes 3538952 | tf_op jit(solution)/shard_map/ppermute | solution.py:367
  281.7 155.4 %all-gather.10.cloned.1.call-start = ((), (), s32[]{:S(2)}) async-start(), calls=%async_computation.7 | async-start | bytes 2654208 | tf_op jit(solution)/shard_map/all_gather | solution.py:900
  281.7 20.9 %collective-permute-start.15 = (bf16[4,2,2,24,768]{4,3,0,1,2:T(8,128)(2,1)}, bf16[4,2,2,24,768]{4,3,0,1,2:T(8,128)(2,1)S(1)}, u32[]{:S(2)}, u32[]{:S(2)}) collective-permute-start(bf16[4,2,2,24,768]{4,3,0,1,2:T(8,128)(2,1)} %dynamic-slice_bitcast_fusion.4), channel_id=1, source_target_pairs={{0,1},{1,0},{2,3},{3,2},{4,5},{5,4},{6,7},{7,6},{8,9},{9,8},{10,11... | collective-permute-start | bytes 1769480 | tf_op jit(solution)/shard_map/ppermute | solution.py:367
  283.9 32.9 %collective-permute-start.18 = (bf16[4,2,2,24,768]{4,3,0,1,2:T(8,128)(2,1)S(1)}, bf16[4,2,2,24,768]{4,3,0,1,2:T(8,128)(2,1)S(1)}, u32[]{:S(2)}, u32[]{:S(2)}) collective-permute-start(bf16[4,2,2,24,768]{4,3,0,1,2:T(8,128)(2,1)S(1)} %dynamic-slice_bitcast_fusion.3), channel_id=1, source_target_pairs={{0,2},{1,3},{2,0},{3,1},{4,6},{5,7},{6,4},{7,5},{8,10},{9,11},{10,... | collective-permute-start | bytes 1769480 | tf_op jit(solution)/shard_map/ppermute | solution.py:367
  293.8 24.4 %collective-permute-start.8 = (bf16[2,2,128,768]{3,2,1,0:T(8,128)(2,1)S(1)}, bf16[2,2,128,768]{3,2,1,0:T(8,128)(2,1)S(1)}, u32[]{:S(2)}, u32[]{:S(2)}) collective-permute-start(bf16[2,2,128,768]{3,2,1,0:T(8,128)(2,1)S(1)} %get-tuple-element.182), channel_id=1, source_target_pairs={{0,8},{8,16},{16,24},{1,9},{9,17},{17,25},{2,10},{10,18},{18,26},{... | collective-permute-start | bytes 2359304 | tf_op jit(solution)/shard_map/ppermute | solution.py:858
  300.2 18.1 %collective-permute-start.9 = (bf16[2,2,128,768]{3,2,1,0:T(8,128)(2,1)S(1)}, bf16[2,2,128,768]{3,2,1,0:T(8,128)(2,1)S(1)}, u32[]{:S(2)}, u32[]{:S(2)}) collective-permute-start(bf16[2,2,128,768]{3,2,1,0:T(8,128)(2,1)S(1)} %get-tuple-element.183), channel_id=1, source_target_pairs={{8,0},{16,8},{24,16},{9,1},{17,9},{25,17},{10,2},{18,10},{26,18},{... | collective-permute-start | bytes 2359304 | tf_op jit(solution)/shard_map/ppermute | solution.py:855
  302.0 14.9 %copy-start.16 = (bf16[4,2,2,2,24,768]{5,4,0,1,2,3:T(8,128)(2,1)S(1)}, bf16[4,2,2,2,24,768]{5,4,0,1,2,3:T(8,128)(2,1)}, u32[]{:S(2)}) copy-start(bf16[4,2,2,2,24,768]{5,4,0,1,2,3:T(8,128)(2,1)} %copy-done.15) | copy-start | bytes 3538948
  302.8 46.8 %collective-permute-start.16 = (bf16[4,2,24,768]{3,2,0,1:T(8,128)(2,1)S(1)}, bf16[4,2,24,768]{3,2,0,1:T(8,128)(2,1)S(1)}, u32[]{:S(2)}, u32[]{:S(2)}) collective-permute-start(bf16[4,2,24,768]{3,2,0,1:T(8,128)(2,1)S(1)} %dynamic-slice_bitcast_fusion.8), channel_id=1, source_target_pairs={{0,2},{1,3},{2,0},{3,1},{4,6},{5,7},{6,4},{7,5},{8,10},{9,11},{10,... | collective-permute-start | bytes 884744 | tf_op jit(solution)/shard_map/ppermute | solution.py:367
  317.1 31.1 %collective-permute-start.19 = (bf16[4,2,24,768]{3,2,0,1:T(8,128)(2,1)S(1)}, bf16[4,2,24,768]{3,2,0,1:T(8,128)(2,1)S(1)}, u32[]{:S(2)}, u32[]{:S(2)}) collective-permute-start(bf16[4,2,24,768]{3,2,0,1:T(8,128)(2,1)S(1)} %dynamic-slice_bitcast_fusion.7), channel_id=1, source_target_pairs={{0,4},{1,5},{2,6},{3,7},{4,0},{5,1},{6,2},{7,3},{8,12},{9,13},{10,... | collective-permute-start | bytes 884744 | tf_op jit(solution)/shard_map/ppermute | solution.py:367
  328.7 44.3 %collective-permute-start.10 = (bf16[2,2,2,2,2,2,24,768]{7,6,2,3,4,5,1,0:T(8,128)(2,1)}, bf16[2,2,2,2,2,2,24,768]{7,6,2,3,4,5,1,0:T(8,128)(2,1)}, u32[]{:S(2)}, u32[]{:S(2)}) collective-permute-start(bf16[2,2,2,2,2,2,24,768]{7,6,2,3,4,5,1,0:T(8,128)(2,1)} %bitcast.377), channel_id=1, source_target_pairs={{0,8},{8,0},{16,24},{24,16},{1,9},{9,1},{17,25},{25,17},{2,10},{10... | collective-permute-start | bytes 7077896 | tf_op jit(solution)/shard_map/ppermute | solution.py:367
  348.2 5.2 collective-permute-start.20
  349.7 12.2 %collective-permute-start.17 = (bf16[4,24,768]{2,1,0:T(8,128)(2,1)S(1)}, bf16[4,24,768]{2,1,0:T(8,128)(2,1)S(1)}, u32[]{:S(2)}, u32[]{:S(2)}) collective-permute-start(bf16[4,24,768]{2,1,0:T(8,128)(2,1)S(1)} %dynamic-slice_bitcast_fusion.12), channel_id=1, source_target_pairs={{0,4},{1,5},{2,6},{3,7},{4,0},{5,1},{6,2},{7,3},{8,12},{9,13},{10,... | collective-permute-start | bytes 442376 | tf_op jit(solution)/shard_map/ppermute | solution.py:367
  363.5 8.0 %copy-start.44 = (bf16[2,96,768]{2,1,0:T(8,128)(2,1)}, bf16[2,96,768]{2,1,0:T(8,128)(2,1)S(1)}, u32[]{:S(2)}) copy-start(bf16[2,96,768]{2,1,0:T(8,128)(2,1)S(1)} %get-tuple-element.220) | copy-start | bytes 884740
  363.5 8.0 %collective-permute-start.21 = (bf16[2,96,768]{2,1,0:T(8,128)(2,1)S(1)}, bf16[2,96,768]{2,1,0:T(8,128)(2,1)}, u32[]{:S(2)}, u32[]{:S(2)}) collective-permute-start(bf16[2,96,768]{2,1,0:T(8,128)(2,1)S(1)} %get-tuple-element.220), channel_id=1, source_target_pairs={{0,16},{8,24},{16,0},{24,8},{1,17},{9,25},{17,1},{25,9},{2,18},{10... | collective-permute-start | bytes 884744 | tf_op jit(solution)/shard_map/ppermute | solution.py:367
  372.9 10.0 %collective-permute-start.22 = (bf16[2,2,96,768]{3,2,1,0:T(8,128)(2,1)S(1)}, bf16[2,2,96,768]{3,2,1,0:T(8,128)(2,1)S(1)}, u32[]{:S(2)}, u32[]{:S(2)}) collective-permute-start(bf16[2,2,96,768]{3,2,1,0:T(8,128)(2,1)S(1)} %maximum_select_fusion.4), channel_id=1, source_target_pairs={{0,8},{8,0},{16,24},{24,16},{1,9},{9,1},{17,25},{25,17},{2,10},{10... | collective-permute-start | bytes 1769480 | tf_op jit(solution)/shard_map/ppermute | solution.py:367
  376.3 19.4 %collective-permute-start.23 = (bf16[2,2,2,2,24,768]{5,4,1,2,3,0:T(8,128)(2,1)S(1)}, bf16[2,2,2,2,24,768]{5,4,1,2,3,0:T(8,128)(2,1)S(1)}, u32[]{:S(2)}, u32[]{:S(2)}) collective-permute-start(bf16[2,2,2,2,24,768]{5,4,1,2,3,0:T(8,128)(2,1)S(1)} %dynamic-slice_bitcast_fusion.2), channel_id=1, source_target_pairs={{0,1},{1,0},{2,3},{3,2},{4,5},{5,4},{6,7},{7,6},{8,9},{9,8},{10,11... | collective-permute-start | bytes 1769480 | tf_op jit(solution)/shard_map/ppermute | solution.py:367
  380.9 15.5 %collective-permute-start.11 = (bf16[2,2,2,2,24,768]{5,4,0,1,2,3:T(8,128)(2,1)S(1)}, bf16[2,2,2,2,24,768]{5,4,0,1,2,3:T(8,128)(2,1)S(1)}, u32[]{:S(2)}, u32[]{:S(2)}) collective-permute-start(bf16[2,2,2,2,24,768]{5,4,0,1,2,3:T(8,128)(2,1)S(1)} %dynamic-slice_bitcast_fusion.5), channel_id=1, source_target_pairs={{0,16},{8,24},{16,0},{24,8},{1,17},{9,25},{17,1},{25,9},{2,18},{10... | collective-permute-start | bytes 1769480 | tf_op jit(solution)/shard_map/ppermute | solution.py:367
  395.9 12.6 %collective-permute-start.24 = (bf16[2,2,2,24,768]{4,3,1,2,0:T(8,128)(2,1)S(1)}, bf16[2,2,2,24,768]{4,3,1,2,0:T(8,128)(2,1)S(1)}, u32[]{:S(2)}, u32[]{:S(2)}) collective-permute-start(bf16[2,2,2,24,768]{4,3,1,2,0:T(8,128)(2,1)S(1)} %dynamic-slice_bitcast_fusion.6), channel_id=1, source_target_pairs={{0,2},{1,3},{2,0},{3,1},{4,6},{5,7},{6,4},{7,5},{8,10},{9,11},{10,... | collective-permute-start | bytes 884744 | tf_op jit(solution)/shard_map/ppermute | solution.py:367
  396.6 12.1 %collective-permute-start.12 = (bf16[2,2,2,24,768]{4,3,0,1,2:T(8,128)(2,1)S(1)}, bf16[2,2,2,24,768]{4,3,0,1,2:T(8,128)(2,1)S(1)}, u32[]{:S(2)}, u32[]{:S(2)}) collective-permute-start(bf16[2,2,2,24,768]{4,3,0,1,2:T(8,128)(2,1)S(1)} %dynamic-slice_bitcast_fusion.9), channel_id=1, source_target_pairs={{0,1},{1,0},{2,3},{3,2},{4,5},{5,4},{6,7},{7,6},{8,9},{9,8},{10,11... | collective-permute-start | bytes 884744 | tf_op jit(solution)/shard_map/ppermute | solution.py:367
  408.6 14.2 %collective-permute-start.25 = (bf16[2,2,24,768]{3,2,1,0:T(8,128)(2,1)S(1)}, bf16[2,2,24,768]{3,2,1,0:T(8,128)(2,1)S(1)}, u32[]{:S(2)}, u32[]{:S(2)}) collective-permute-start(bf16[2,2,24,768]{3,2,1,0:T(8,128)(2,1)S(1)} %dynamic-slice_bitcast_fusion.10), channel_id=1, source_target_pairs={{0,4},{1,5},{2,6},{3,7},{4,0},{5,1},{6,2},{7,3},{8,12},{9,13},{10,... | collective-permute-start | bytes 442376 | tf_op jit(solution)/shard_map/ppermute | solution.py:367
  408.8 16.4 %collective-permute-start.13 = (bf16[2,2,24,768]{3,2,0,1:T(8,128)(2,1)S(1)}, bf16[2,2,24,768]{3,2,0,1:T(8,128)(2,1)S(1)}, u32[]{:S(2)}, u32[]{:S(2)}) collective-permute-start(bf16[2,2,24,768]{3,2,0,1:T(8,128)(2,1)S(1)} %dynamic-slice_bitcast_fusion.13), channel_id=1, source_target_pairs={{0,2},{1,3},{2,0},{3,1},{4,6},{5,7},{6,4},{7,5},{8,10},{9,11},{10,... | collective-permute-start | bytes 442376 | tf_op jit(solution)/shard_map/ppermute | solution.py:367
  422.9 4.4 collective-permute-start.26
  425.3 8.1 %collective-permute-start.14 = (bf16[2,24,768]{2,1,0:T(8,128)(2,1)S(1)}, bf16[2,24,768]{2,1,0:T(8,128)(2,1)}, u32[]{:S(2)}, u32[]{:S(2)}) collective-permute-start(bf16[2,24,768]{2,1,0:T(8,128)(2,1)S(1)} %dynamic-slice_bitcast_fusion.15), channel_id=1, source_target_pairs={{0,4},{1,5},{2,6},{3,7},{4,0},{5,1},{6,2},{7,3},{8,12},{9,13},{10,... | collective-permute-start | bytes 221192 | tf_op jit(solution)/shard_map/ppermute | solution.py:367
  427.3 8.6 %copy-start.47 = (f32[2,24,768]{2,1,0:T(8,128)}, f32[2,24,768]{2,1,0:T(8,128)S(1)}, u32[]{:S(2)}) copy-start(f32[2,24,768]{2,1,0:T(8,128)S(1)} %convert_add_fusion.17) | copy-start | bytes 442372
  447.4 6.2 %copy-start.67 = (f32[1,768]{1,0:T(1,128)S(1)}, f32[1,768]{1,0:T(1,128)}, u32[]{:S(2)}) copy-start(f32[1,768]{1,0:T(1,128)} %reshape.755) | copy-start | bytes 9220
  447.4 18.2 %all-to-all-start.2 = ((bf16[8,96,384]{2,1,0:T(8,128)(2,1)}), bf16[8,96,384]{2,1,0:T(8,128)(2,1)}, u32[]{:S(2)}, u32[]{:S(2)}) async-start(bf16[8,96,384]{2,1,0:T(8,128)(2,1)} %bitcast.468), calls=%async_computation.2 | async-start | bytes 1179648 | tf_op jit(solution)/shard_map/all_to_all | solution.py:968
  451.8 49.1 %all-gather.12.cloned.1.call-start = ((), (), s32[]{:S(2)}) async-start(), calls=%async_computation.8 | async-start | bytes 1769472 | tf_op jit(solution)/shard_map/all_gather | solution.py:937
  454.7 19.8 %copy-start.27 = (f32[4,24,768]{2,1,0:T(8,128)}, f32[4,24,768]{2,1,0:T(8,128)S(1)}, u32[]{:S(2)}) copy-start(f32[4,24,768]{2,1,0:T(8,128)S(1)} %pad_maximum_fusion.10) | copy-start | bytes 884740
  474.5 40.7 %all-to-all-start.3 = ((bf16[4,496,768]{2,1,0:T(8,128)(2,1)}), bf16[4,496,768]{2,1,0:T(8,128)(2,1)}, u32[]{:S(2)}, u32[]{:S(2)}) async-start(bf16[4,496,768]{2,1,0:T(8,128)(2,1)} %pad_maximum_fusion.2), calls=%async_computation.3 | async-start | bytes 6094848 | tf_op jit(solution)/shard_map/all_to_all | solution.py:371
  525.7 18.2 %all-to-all-start.4 = ((bf16[4,5,32,768]{3,2,1,0:T(8,128)(2,1)}), bf16[4,5,32,768]{3,2,1,0:T(8,128)(2,1)}, u32[]{:S(2)}, u32[]{:S(2)}) async-start(bf16[4,5,32,768]{3,2,1,0:T(8,128)(2,1)} %attend_update.1), calls=%async_computation.4 | async-start | bytes 1966080 | tf_op jit(solution)/shard_map/all_to_all | solution.py:371
  (63 other events, 189.3 us)
Sparse Core Ops, SparseCore 0:
  12.9 107.5 all-gather.5
  281.8 83.0 all-gather.7
  371.6 62.1 all-gather.9
  455.6 45.2 all-gather.11
